TPU v7x, 256 devices: a whole 4x4x8 slice. The times are simulated.
256 devices in a mesh: dir: 2 (over core), seq: 128 (over y, z, x).
Axes of the slice: x: 4, y: 4, z: 8, core: 2. Of those that a mesh axis runs over, the one named last changes fastest.
Arguments:
- queries: bfloat16 [2, 4, 8192, 4096], P('dir', None, 'seq'), may hold values from -35 to 35
- key_states: bfloat16 [2, 4, 8192, 4096], P('dir', None, 'seq'), may hold values from -6 to 6
- value_vectors: bfloat16 [2, 4, 8192, 4096], P('dir', None, 'seq'), may hold values from -6 to 6
- hypothesis_lengths: int32 [4, 512], replicated, may hold values from 1 to 256, 8192 in all within a row
- join_weight: bfloat16 [8192, 2, 1024], P('seq', None, 'dir'), may hold values from -0.0625 to 0.0625
Outputs:
- joined: bfloat16 [4, 8192, 1024], P(None, 'seq', 'dir')
All inputs are finite; a program needn't handle non-finite values.
Results may differ from a plain program's by a relative error of at most 0.0072.
Values may be sent and summed in bfloat16 or wider, within the bound.
No kernel may reach another device: no remote copies, remote signals or barrier semaphores. Data moves between devices by JAX's collectives and lax.ppermute only.
A program may use at most 128 MiB of HBM per device.

v0:
```python
import math

import jax
import jax.numpy as jnp
from jax import lax
from jax.sharding import PartitionSpec as P

ATTENTION_HEADS = 32
LONGEST_TOKENS = 256


def swapped(array, axis, stride):
    return lax.ppermute(array, axis, [(i, i ^ 1 << stride) for i in range(lax.axis_size(axis))])


def hypothesis_tables(length_list, row_len):
    ends = jnp.cumsum(length_list)
    starts = ends - length_list
    places = jnp.arange(row_len, dtype=jnp.int32)
    inside = (places[:, None] >= starts[None, :]) & (places[:, None] < ends[None, :])
    first = jnp.sum(jnp.where(inside, starts[None, :], 0), axis=1)
    after = jnp.sum(jnp.where(inside, ends[None, :], 0), axis=1)
    mirror = first + after - 1 - places
    return (first, mirror)


def attend_group(query_row, k_row, v_row, first):
    row_len = query_row.shape[0]
    block_item = min(512, row_len)
    token_span = min(block_item + LONGEST_TOKENS, row_len)
    scale = 1.0 / math.sqrt(query_row.shape[2])

    def single_block(index):
        q_start = index * block_item
        k_start = jnp.maximum(q_start + block_item - token_span, 0)
        q_part = lax.dynamic_slice_in_dim(query_row, q_start, block_item, 0)
        k_part = lax.dynamic_slice_in_dim(k_row, k_start, token_span, 0)
        v_part = lax.dynamic_slice_in_dim(v_row, k_start, token_span, 0)
        scores = (
            jnp.einsum("qhc,khc->hqk", q_part, k_part, preferred_element_type=jnp.float32) * scale
        )
        q_places = q_start + jnp.arange(block_item, dtype=jnp.int32)
        k_places = k_start + jnp.arange(token_span, dtype=jnp.int32)
        starts = lax.dynamic_slice_in_dim(first, q_start, block_item, 0)
        allowed = (k_places[None, :] >= starts[:, None]) & (k_places[None, :] <= q_places[:, None])
        scores = jnp.where(allowed[None], scores, jnp.float32(-1e30))
        top = jnp.max(scores, axis=2, keepdims=True)
        raised = jnp.exp(scores - top)
        weights = (raised / jnp.sum(raised, axis=2, keepdims=True)).astype(jnp.bfloat16)
        return jnp.einsum(
            "hqk,khc->qhc", weights, v_part, preferred_element_type=jnp.float32
        ).astype(jnp.bfloat16)

    block_list = lax.map(single_block, jnp.arange(row_len // block_item, dtype=jnp.int32))
    return block_list.reshape(row_len, query_row.shape[1], query_row.shape[2])


def body(queries, key_states, value_vectors, hypothesis_lengths, join_weight):
    rows, piece, width = (queries.shape[1], queries.shape[2], queries.shape[3])
    devices = lax.axis_size("seq")
    groups = devices // rows
    head_width = width // ATTENTION_HEADS
    pair = width // groups
    heads_here = pair // head_width
    row_bits = rows.bit_length() - 1
    place = lax.axis_index("seq")
    row = place % rows
    row_len = devices * piece

    def regroup(states):
        states = states.reshape(rows, piece, groups, pair)
        return jnp.transpose(states, (2, 0, 1, 3)).reshape(groups * rows, piece, pair)

    q_all, k_all, v_all = (
        lax.all_to_all(regroup(queries[0]), "seq", split_axis=0, concat_axis=1, tiled=True),
        lax.all_to_all(regroup(key_states[0]), "seq", split_axis=0, concat_axis=1, tiled=True),
        lax.all_to_all(regroup(value_vectors[0]), "seq", split_axis=0, concat_axis=1, tiled=True),
    )
    block_rows = join_weight
    for bit in range(row_bits):
        partner = swapped(block_rows, "seq", bit)
        lower = place // 2**bit % 2 == 0
        block_rows = jnp.where(
            lower,
            jnp.concatenate([block_rows, partner], 0),
            jnp.concatenate([partner, block_rows], 0),
        )
    length_list = lax.dynamic_index_in_dim(hypothesis_lengths, row, 0, keepdims=False)
    first, mirror = hypothesis_tables(length_list, row_len)
    array_shape = (row_len, heads_here, head_width)
    context_vectors = attend_group(
        q_all.reshape(array_shape), k_all.reshape(array_shape), v_all.reshape(array_shape), first
    )
    other = swapped(context_vectors, "dir", 0)
    side = lax.axis_index("dir")
    left_side = jnp.where(side == 0, context_vectors, other)
    right_side = jnp.where(side == 0, other, context_vectors)
    right_side = jnp.take(right_side, mirror, axis=0)
    feature_rows = jnp.stack([left_side, right_side], axis=2).reshape(row_len, 2 * pair)
    columns = block_rows.shape[2]
    partial_value = jnp.dot(
        feature_rows, block_rows.reshape(2 * pair, 2 * columns), preferred_element_type=jnp.float32
    ).astype(jnp.bfloat16)
    arrived = lax.all_to_all(
        partial_value.reshape(devices, piece, 2 * columns),
        "seq",
        split_axis=0,
        concat_axis=0,
        tiled=True,
    )
    totals = jnp.sum(arrived.reshape(groups, rows, piece, 2 * columns).astype(jnp.float32), axis=0)
    joined = jax.nn.silu(totals[..., :columns]) * totals[..., columns:]
    return joined.astype(jnp.bfloat16)


def solution(mesh):
    return jax.shard_map(
        body,
        mesh=mesh,
        in_specs=(
            P("dir", None, "seq", None),
            P("dir", None, "seq", None),
            P("dir", None, "seq", None),
            P(),
            P("seq", None, "dir"),
        ),
        out_specs=P(None, "seq", "dir"),
        check_vma=False,
    )
```

profile of v0, /device:TPU:8, one launch (start us, length us, event | category | flops | bytes accessed | tf_op | source)
XLA Modules:
  0.0 711.8 jit_solution(9223435160331193547)
XLA Ops:
  0.0 2.1 copy.23
  2.1 2.1 copy.16
  4.2 16.0 %all-to-all-start.1 = ((bf16[128,64,128]{2,1,0:T(8,128)(2,1)}), bf16[128,64,128]{2,1,0:T(8,128)(2,1)}, u32[]{:S(2)}, u32[]{:S(2)}) async-start(bf16[128,64,128]{2,1,0:T(8,128)(2,1)} %bitcast.15), calls=%async_computation.1 | async-start | bytes 4194304 | tf_op jit(solution)/shard_map/all_to_all | solution.py:75
  20.7 2.1 copy.17
  22.9 48.9 %all-to-all-done.1 = bf16[128,64,128]{2,1,0:T(8,128)(2,1)} async-done(((bf16[128,64,128]{2,1,0:T(8,128)(2,1)}), bf16[128,64,128]{2,1,0:T(8,128)(2,1)}, u32[]{:S(2)}, u32[]{:S(2)}) %all-to-all-start.1) | async-done | bytes 2097184 | tf_op jit(solution)/shard_map/all_to_all | solution.py:75
  71.8 8.3 %all-to-all-start.2 = ((bf16[128,64,128]{2,1,0:T(8,128)(2,1)}), bf16[128,64,128]{2,1,0:T(8,128)(2,1)}, u32[]{:S(2)}, u32[]{:S(2)}) async-start(bf16[128,64,128]{2,1,0:T(8,128)(2,1)} %bitcast.18), calls=%async_computation.2 | async-start | bytes 4194304 | tf_op jit(solution)/shard_map/all_to_all | solution.py:76
  80.6 2.2 copy.15
  82.7 48.2 %all-to-all-done.2 = bf16[128,64,128]{2,1,0:T(8,128)(2,1)} async-done(((bf16[128,64,128]{2,1,0:T(8,128)(2,1)}), bf16[128,64,128]{2,1,0:T(8,128)(2,1)}, u32[]{:S(2)}, u32[]{:S(2)}) %all-to-all-start.2) | async-done | bytes 2097184 | tf_op jit(solution)/shard_map/all_to_all | solution.py:76
  131.0 8.0 %all-to-all-start = ((bf16[128,64,128]{2,1,0:T(8,128)(2,1)}), bf16[128,64,128]{2,1,0:T(8,128)(2,1)S(1)}, u32[]{:S(2)}, u32[]{:S(2)}) async-start(bf16[128,64,128]{2,1,0:T(8,128)(2,1)} %bitcast.8), calls=%async_computation | async-start | bytes 4194304 | tf_op jit(solution)/shard_map/all_to_all | solution.py:77
  138.9 1.7 collective-permute-start.1
  141.4 9.6 %select_reduce_fusion = (s32[8192]{0:T(1024)S(1)}, s32[8192]{0:T(1024)S(1)}) fusion(s32[512]{0:T(512)S(1)} %fusion.22, s32[512]{0:T(512)S(1)} %bitcast.105), kind=kLoop, calls=%fused_computation.19 | loop fusion | flops 29343744 | bytes 69632 | tf_op jit(solution)/shard_map/reduce_sum | solution.py:22
  151.0 38.9 %all-to-all-done = bf16[128,64,128]{2,1,0:T(8,128)(2,1)S(1)} async-done(((bf16[128,64,128]{2,1,0:T(8,128)(2,1)}), bf16[128,64,128]{2,1,0:T(8,128)(2,1)S(1)}, u32[]{:S(2)}, u32[]{:S(2)}) %all-to-all-start) | async-done | bytes 2097184 | tf_op jit(solution)/shard_map/all_to_all | solution.py:77
  190.0 75.6 %while.14 = (s32[]{:T(128)}, bf16[16,512,1,128]{3,1,0,2:T(8,128)(2,1)}, s32[16]{0:T(128)S(1)}, bf16[8192,1,128]{2,0,1:T(8,128)(2,1)S(1)}, s32[8192]{0:T(1024)S(1...) while((s32[]{:T(128)}, ...), condition=%wide.region_6.7_spmd, body=%wide.region_3.6_spmd.sunk | while | flops 205717760 | bytes 5925099 | solution.py:54
  191.2 1.6 fusion.28
  193.2 0.7 fusion.30
  196.0 1.6 fusion.28
  197.9 0.7 fusion.30
  200.7 1.6 fusion.28
  202.7 0.7 fusion.30
  203.5 0.7 constant_dynamic-update-slice_fusion.2
  205.4 1.6 fusion.28
  207.4 0.7 fusion.30
  208.2 0.7 constant_dynamic-update-slice_fusion.2
  210.1 1.6 fusion.28
  212.9 0.7 constant_dynamic-update-slice_fusion.2
  214.8 1.6 fusion.28
  217.6 0.7 constant_dynamic-update-slice_fusion.2
  219.6 1.6 fusion.28
  221.6 0.7 fusion.30
  222.4 0.7 constant_dynamic-update-slice_fusion.2
  224.3 1.6 fusion.28
  226.3 0.7 fusion.30
  227.1 0.7 constant_dynamic-update-slice_fusion.2
  229.0 1.6 fusion.28
  233.7 1.6 fusion.28
  235.7 0.7 fusion.30
  236.5 0.7 constant_dynamic-update-slice_fusion.2
  238.5 1.6 fusion.28
  240.4 0.7 fusion.30
  241.2 0.7 constant_dynamic-update-slice_fusion.2
  243.2 1.6 fusion.28
  245.2 0.7 fusion.30
  246.0 0.7 constant_dynamic-update-slice_fusion.2
  247.9 1.6 fusion.28
  249.9 0.7 fusion.30
  250.7 0.7 constant_dynamic-update-slice_fusion.2
  252.6 1.6 fusion.28
  254.6 0.7 fusion.30
  255.4 0.7 constant_dynamic-update-slice_fusion.2
  257.4 1.6 fusion.28
  260.2 0.7 constant_dynamic-update-slice_fusion.2
  262.1 1.6 fusion.28
  264.9 0.7 constant_dynamic-update-slice_fusion.2
  266.3 1.4 collective-permute-start.2
  267.8 8.8 %collective-permute-done.2 = bf16[128,2,512]{2,1,0:T(2,128)(2,1)S(1)} collective-permute-done((bf16[128,2,512]{2,1,0:T(2,128)(2,1)S(1)}, bf16[128,2,512]{2,1,0:T(2,128)(2,1)S(1)}, u32[]{:S(2)}, u32[]{:S(2)}) %collective-permute-start.2) | collective-permute-done | bytes 262176 | tf_op jit(solution)/shard_map/ppermute | solution.py:13
  276.6 3.2 select_bitcast_fusion.1
  279.9 29.2 %gather_fusion = bf16[8192,128]{1,0:T(8,128)(2,1)} fusion(bf16[8192,128]{1,0:T(8,128)(2,1)S(1)} %get-tuple-element.168, s32[8192]{0:T(1024)S(1)} %broadcast_clamp_fusion), kind=kCustom, calls=%fused_computation | custom fusion | bytes 4227072 | tf_op jit(solution)/shard_map/jit(_take)/gather | solution.py:98
  309.0 6.0 bitcast_select_fusion
  315.0 2.3 pad_maximum_fusion
  317.3 6.4 copy.19
  323.7 10.5 %convolution_convert_fusion.1 = bf16[8192,1024]{1,0:T(8,128)(2,1)} fusion(bf16[8192,256]{0,1:T(8,128)(2,1)} %bitcast.86, bf16[128,1024]{1,0:T(8,128)(2,1)S(1)} %bitcast.95, bf16[128,1024]{1,0:T(8,128)(2,1)S(1)} %maximum_select_fusion.2, pred[]{:T(512)S(6)} %eq.15), kind=kOutput, calls=%fused_computation.24 | convolution fusion | flops 4305715200 | bytes 21495808 | tf_op jit(solution)/shard_map/dot_general | solution.py:101
  334.2 373.7 %all_to_all.32 = bf16[128,64,1024]{2,1,0:T(8,128)(2,1)S(1)} all-to-all(bf16[128,64,1024]{2,1,0:T(8,128)(2,1)} %bitcast.84), channel_id=1, replica_groups=mesh['dir'=2,'seq'=128] {'seq'}, dimensions={0} | all-to-all | bytes 33554432 | tf_op jit(solution)/shard_map/all_to_all | solution.py:104
  707.9 3.1 convert_reduce_fusion
  711.0 0.9 fusion.11
  (139 shorter events, 26.8 us)
Async XLA Ops:
  4.2 16.0 %copy-start.1 = (bf16[1,4,64,4096]{3,2,1,0:T(8,128)(2,1)S(1)}, bf16[1,4,64,4096]{3,2,1,0:T(8,128)(2,1)}, u32[]{:S(2)}) copy-start(bf16[1,4,64,4096]{3,2,1,0:T(8,128)(2,1)} %param.8) | copy-start | bytes 6291460
  4.2 67.6 %all-to-all-start.1 = ((bf16[128,64,128]{2,1,0:T(8,128)(2,1)}), bf16[128,64,128]{2,1,0:T(8,128)(2,1)}, u32[]{:S(2)}, u32[]{:S(2)}) async-start(bf16[128,64,128]{2,1,0:T(8,128)(2,1)} %bitcast.15), calls=%async_computation.1 | async-start | bytes 4194304 | tf_op jit(solution)/shard_map/all_to_all | solution.py:75
  71.8 8.3 %copy-start.2 = (bf16[1,4,64,4096]{3,2,1,0:T(8,128)(2,1)S(1)}, bf16[1,4,64,4096]{3,2,1,0:T(8,128)(2,1)}, u32[]{:S(2)}) copy-start(bf16[1,4,64,4096]{3,2,1,0:T(8,128)(2,1)} %param.9) | copy-start | bytes 6291460
  71.8 59.2 %all-to-all-start.2 = ((bf16[128,64,128]{2,1,0:T(8,128)(2,1)}), bf16[128,64,128]{2,1,0:T(8,128)(2,1)}, u32[]{:S(2)}, u32[]{:S(2)}) async-start(bf16[128,64,128]{2,1,0:T(8,128)(2,1)} %bitcast.18), calls=%async_computation.2 | async-start | bytes 4194304 | tf_op jit(solution)/shard_map/all_to_all | solution.py:76
  131.0 8.0 %copy-start.4 = (bf16[64,2,512]{2,1,0:T(2,128)(2,1)S(1)}, bf16[64,2,512]{2,1,0:T(2,128)(2,1)}, u32[]{:S(2)}) copy-start(bf16[64,2,512]{2,1,0:T(2,128)(2,1)} %param.11) | copy-start | bytes 393220
  131.0 9.7 %copy-start.5 = (s32[4,512]{1,0:T(4,128)S(1)}, s32[4,512]{1,0:T(4,128)}, u32[]{:S(2)}) copy-start(s32[4,512]{1,0:T(4,128)} %param.10) | copy-start | bytes 24580
  131.0 59.0 %all-to-all-start = ((bf16[128,64,128]{2,1,0:T(8,128)(2,1)}), bf16[128,64,128]{2,1,0:T(8,128)(2,1)S(1)}, u32[]{:S(2)}, u32[]{:S(2)}) async-start(bf16[128,64,128]{2,1,0:T(8,128)(2,1)} %bitcast.8), calls=%async_computation | async-start | bytes 4194304 | tf_op jit(solution)/shard_map/all_to_all | solution.py:77
  138.9 126.7 %collective-permute-start.1 = (bf16[64,2,512]{2,1,0:T(2,128)(2,1)S(1)}, bf16[64,2,512]{2,1,0:T(2,128)(2,1)S(1)}, u32[]{:S(2)}, u32[]{:S(2)}) collective-permute-start(bf16[64,2,512]{2,1,0:T(2,128)(2,1)S(1)} %copy-done.4), channel_id=1, source_target_pairs={{0,1},{1,0},{2,3},{3,2},{4,5},{5,4},{6,7},{7,6},{8,9},{9,8},{10,11... | collective-permute-start | bytes 393224 | tf_op jit(solution)/shard_map/ppermute | solution.py:13
  265.5 11.1 %collective-permute-start = (bf16[8192,1,128]{2,0,1:T(8,128)(2,1)}, bf16[8192,1,128]{2,0,1:T(8,128)(2,1)}, u32[]{:S(2)}, u32[]{:S(2)}) collective-permute-start(bf16[8192,1,128]{2,0,1:T(8,128)(2,1)} %bitcast.94), channel_id=1, source_target_pairs={{0,128},{128,0},{1,129},{129,1},{2,130},{130,2},{3,131},{131,3},{4... | collective-permute-start | bytes 6291464 | tf_op jit(solution)/shard_map/ppermute | solution.py:13
  265.6 11.0 %copy-start.3 = (bf16[16,512,1,128]{3,1,0,2:T(8,128)(2,1)S(1)}, bf16[16,512,1,128]{3,1,0,2:T(8,128)(2,1)}, u32[]{:S(2)}) copy-start(bf16[16,512,1,128]{3,1,0,2:T(8,128)(2,1)} %get-tuple-element.146) | copy-start | bytes 6291460
  266.3 10.3 %collective-permute-start.2 = (bf16[128,2,512]{2,1,0:T(2,128)(2,1)S(1)}, bf16[128,2,512]{2,1,0:T(2,128)(2,1)S(1)}, u32[]{:S(2)}, u32[]{:S(2)}) collective-permute-start(bf16[128,2,512]{2,1,0:T(2,128)(2,1)S(1)} %broadcast_select_fusion), channel_id=1, source_target_pairs={{0,2},{1,3},{2,0},{3,1},{4,6},{5,7},{6,4},{7,5},{8,10},{9,11},{10,... | collective-permute-start | bytes 786440 | tf_op jit(solution)/shard_map/ppermute | solution.py:13
  309.0 6.0 copy-start
where the time goes:
time: 713 us; the launch traced here: 712 us
  blocking collectives  374 us (52%)
  waiting for transfers between devices  145 us (20%)
  local copies, waits for them, and re-layouts  68.5 us (10%)
  matrix products  46.6 us (7%)
  starting transfers between devices  35.4 us (5%)
  other arithmetic  32.7 us (5%)
  loops' own time  9.77 us (1%)
    all_to_all x1, blocking collectives, body(): lax.all_to_all(partial_value.reshape(devices, piece, 2 * columns), 'seq',...  374 us
    all_to_all x1, waiting for transfers between devices, body(): lax.all_to_all(regroup(queries[0]), 'seq', split_axis=0, concat_axis=1, t...  48.9 us
    all_to_all x1, waiting for transfers between devices, body(): lax.all_to_all(regroup(key_states[0]), 'seq', split_axis=0, concat_axis=1...  48.2 us
    all_to_all x1, waiting for transfers between devices, body(): lax.all_to_all(regroup(value_vectors[0]), 'seq', split_axis=0, concat_axi...  38.9 us
    gather x1, local copies, waits for them, and re-layouts, body(): right_side = jnp.take(right_side, mirror, axis=0)  29.2 us
    dot_general x16, matrix products, single_block(): jnp.einsum('qhc,khc->hqk', q_part, k_part, preferred_element_type=jnp.flo...  25.4 us
    all_to_all x1, starting transfers between devices, body(): lax.all_to_all(regroup(queries[0]), 'seq', split_axis=0, concat_axis=1, t...  16 us
  transfers between devices with their start and end apart: 6, of which 4 were waited for; matrix products, arithmetic and copies ran while one was open for 12% of the time, Pallas kernels for 0%

commit v1 on v0

v1 whole, which is shorter than its diff:
```python
import math

import jax
import jax.numpy as jnp
from jax import lax
from jax.experimental import pallas as pl
from jax.experimental.pallas import tpu as pltpu
from jax.sharding import Mesh
from jax.sharding import PartitionSpec as P

HEAD = 128
SPAN = 256
HALF = SPAN // 2
RINGS = 32
PER_STEP = 2
NT = (((1,), (1,)), ((), ()))
NN = (((1,), (0,)), ((), ()))


def dot(a, b, dims=NN):
    return lax.dot_general(a, b, dims, preferred_element_type=jnp.float32)


def one_hot(index, rows, columns):
    at = lax.broadcasted_iota(jnp.int32, (rows, columns), 1)
    return jnp.where(at == index, 1.0, 0.0).astype(jnp.bfloat16)


def tables(lengths, base):
    count = lengths.shape[1]
    order = jnp.arange(count, dtype=jnp.int32)
    upto = order[None, :] <= order[:, None]
    ends = jnp.sum(jnp.where(upto[None], lengths[:, None, :], 0), axis=2)
    starts = ends - lengths
    places = base + jnp.arange(SPAN, dtype=jnp.int32)
    at = places[None, :, None]
    inside = (at >= starts[:, None, :]) & (at < ends[:, None, :])
    first = jnp.sum(jnp.where(inside, starts[:, None, :], 0), axis=2) - base
    end = jnp.sum(jnp.where(inside, ends[:, None, :], 0), axis=2) - base
    return first, end


def attend_kernel(edge_ref, low_ref, q_ref, own_ref, before_ref, out_ref, ahead_ref, back_ref, bias):
    factor = math.log2(math.e) / math.sqrt(HEAD)
    wide = SPAN + HALF

    @pl.when(pl.program_id(0) == 0)
    def _():
        for part in range(2):
            key = lax.broadcasted_iota(jnp.int32, (HALF, wide), 1) + part * HALF
            here = lax.broadcasted_iota(jnp.int32, (HALF, wide), 0) + (part * HALF + SPAN)
            low = low_ref[part * HALF : (part + 1) * HALF, :] + SPAN
            keep = (key >= low) & (key <= here)
            bias[part] = jnp.where(keep, 0.0, -1e30)

    for h in range(PER_STEP):
        lanes = slice(h * HEAD, (h + 1) * HEAD)
        q = q_ref[:, :, lanes].reshape(SPAN, HEAD)
        k = jnp.concatenate([before_ref[:, 0, :, lanes].reshape(SPAN, HEAD), own_ref[:, 0, :, lanes].reshape(SPAN, HEAD)], 0)
        v = jnp.concatenate([before_ref[:, 1, :, lanes].reshape(SPAN, HEAD), own_ref[:, 1, :, lanes].reshape(SPAN, HEAD)], 0)
        for part in range(2):
            rows = slice(part * HALF, (part + 1) * HALF)
            keys = slice(part * HALF, part * HALF + wide)
            scores = dot(q[rows], k[keys], NT) + bias[part]
            top = jnp.max(scores, axis=1, keepdims=True)
            raised = jnp.exp2((scores - top) * factor)
            total = jnp.sum(raised, axis=1, keepdims=True)
            context = dot(raised.astype(jnp.bfloat16), v[keys]) / total
            out_ref[rows, lanes] = context.astype(jnp.bfloat16)
    turn = HALF - 1 - lax.broadcasted_iota(jnp.int32, (HALF, 1), 0)
    context = out_ref[...]
    ahead_ref[...] = dot(one_hot(edge_ref[0] + turn, HALF, SPAN), context).astype(jnp.bfloat16)
    back_ref[...] = dot(one_hot(edge_ref[1] - HALF + turn, HALF, SPAN), context).astype(jnp.bfloat16)


def attend(edge, low, q, own, before):
    features = q.shape[2]
    lanes = PER_STEP * HEAD
    pieces, piece = q.shape[0], q.shape[1]
    pair = pl.BlockSpec((pieces, 2, piece, lanes), lambda g: (0, 0, 0, g))
    return pl.pallas_call(
        attend_kernel,
        grid=(features // lanes,),
        in_specs=[
            pl.BlockSpec(memory_space=pltpu.SMEM),
            pl.BlockSpec((SPAN, 1), lambda g: (0, 0)),
            pl.BlockSpec((pieces, piece, lanes), lambda g: (0, 0, g)),
            pair,
            pair,
        ],
        out_specs=[
            pl.BlockSpec((SPAN, lanes), lambda g: (0, g)),
            pl.BlockSpec((HALF, lanes), lambda g: (0, g)),
            pl.BlockSpec((HALF, lanes), lambda g: (0, g)),
        ],
        out_shape=[
            jax.ShapeDtypeStruct((SPAN, features), jnp.bfloat16),
            jax.ShapeDtypeStruct((HALF, features), jnp.bfloat16),
            jax.ShapeDtypeStruct((HALF, features), jnp.bfloat16),
        ],
        scratch_shapes=[pltpu.VMEM((2, HALF, SPAN + HALF), jnp.float32)],
        compiler_params=pltpu.CompilerParams(vmem_limit_bytes=32 * 2**20),
        cost_estimate=pl.CostEstimate(flops=10**9, bytes_accessed=4 * 2**20, transcendentals=10**6),
        name="attend",
    )(edge, low, q, own, before)


def mirror_kernel(source_ref, own_ref, before_ref, after_ref, out_ref):
    source = source_ref[...]
    out = dot(one_hot(source, SPAN, SPAN), own_ref[...])
    out = out + dot(one_hot(source - SPAN, SPAN, HALF), before_ref[...])
    out = out + dot(one_hot(source - SPAN - HALF, SPAN, HALF), after_ref[...])
    out_ref[...] = out.astype(jnp.bfloat16)


def mirrored(source, own, before, after):
    return pl.pallas_call(
        mirror_kernel,
        out_shape=jax.ShapeDtypeStruct(own.shape, jnp.bfloat16),
        compiler_params=pltpu.CompilerParams(vmem_limit_bytes=32 * 2**20),
        cost_estimate=pl.CostEstimate(flops=3 * 10**8, bytes_accessed=2 * 2**20, transcendentals=0),
        name="mirror",
    )(source, own, before, after)


def join_kernel(side_ref, mine_ref, other_ref, weight_ref, second_ref, out_ref):
    depth = mine_ref.shape[1]
    wide = out_ref.shape[2]
    total = dot(mine_ref[...], weight_ref[...].reshape(depth, wide))
    total = total + dot(other_ref[...], second_ref[...].reshape(depth, wide))
    out_ref[...] = total.astype(jnp.bfloat16).reshape(out_ref.shape)


def join(side, mine, other, weight, pieces):
    tokens, depth = mine.shape
    heads, _, head, units = weight.shape
    wide = 256
    whole = pl.BlockSpec((tokens, depth), lambda n, side: (0, 0))
    return pl.pallas_call(
        join_kernel,
        grid_spec=pltpu.PrefetchScalarGridSpec(
            num_scalar_prefetch=1,
            grid=(units // wide,),
            in_specs=[
                whole,
                whole,
                pl.BlockSpec((heads, 1, head, wide), lambda n, side: (0, side[0], 0, n)),
                pl.BlockSpec((heads, 1, head, wide), lambda n, side: (0, 1 - side[0], 0, n)),
            ],
            out_specs=pl.BlockSpec((pieces, tokens // pieces, wide), lambda n, side: (0, 0, n)),
        ),
        out_shape=jax.ShapeDtypeStruct((pieces, tokens // pieces, units), jnp.bfloat16),
        compiler_params=pltpu.CompilerParams(vmem_limit_bytes=32 * 2**20),
        cost_estimate=pl.CostEstimate(flops=10**9, bytes_accessed=6 * 2**20, transcendentals=0),
        name="join",
    )(side, mine, other, weight, weight)


def body(queries, key_states, value_vectors, hypothesis_lengths, join_weight):
    _, rows, piece, width = queries.shape
    pieces = SPAN // piece
    share = width // pieces
    side = lax.axis_index("dir")
    ring = lax.axis_index("y") * 8 + lax.axis_index("z")
    base = ring * SPAN

    def exchange(parts):
        return lax.all_to_all(parts, "x", split_axis=0, concat_axis=0, tiled=True)

    def split(states):
        return states.reshape(piece, pieces, share).transpose(1, 0, 2)

    turned = lax.ppermute(
        join_weight.reshape(piece, -1), ("y", "x"), [(y * 4 + x, x * 4 + y) for y in range(4) for x in range(4)]
    )
    weight = lax.all_gather(turned, ("z", "y"), tiled=True)
    units = weight.shape[1]
    weight = weight.reshape(share // HEAD, 2, HEAD, units)

    first, end = tables(hypothesis_lengths, base)
    here = jnp.arange(SPAN, dtype=jnp.int32)[None, :]
    mirror = first + end - 1 - here
    source = jnp.where(
        mirror < 0, SPAN + here - end + HALF, jnp.where(mirror >= SPAN, SPAN + HALF + here - first, mirror)
    )
    source = jnp.where(side == 0, here, source)
    edges = jnp.stack([first[:, -1], end[:, 0]], axis=1)

    next_ring = [(c, c + 1) for c in range(RINGS - 1)]
    swap_ahead = [(RINGS + c, RINGS + c + 1) for c in range(RINGS - 1)]
    swap_back = [(RINGS + c + 1, RINGS + c) for c in range(RINGS - 1)]
    joined = []
    for r in range(rows):
        own = exchange(jnp.stack([split(key_states[0, r]), split(value_vectors[0, r])], axis=1))
        q = exchange(split(queries[0, r]))
        before = lax.ppermute(own, ("y", "z"), next_ring)
        context, ahead, back = attend(edges[r], first[r][:, None], q, own, before)
        from_before = lax.ppermute(ahead, ("dir", "y", "z"), swap_ahead)
        from_after = lax.ppermute(back, ("dir", "y", "z"), swap_back)
        mine = mirrored(source[r][:, None], context, from_before, from_after)
        other = lax.ppermute(mine, "dir", [(0, 1), (1, 0)])
        partial_value = join(side[None], mine, other, weight, pieces)
        total = jnp.sum(exchange(partial_value).astype(jnp.float32), axis=0)
        joined.append((jax.nn.silu(total[:, : units // 2]) * total[:, units // 2 :]).astype(jnp.bfloat16))
    return jnp.stack(joined)


def solution(mesh):
    fine = Mesh(mesh.devices.reshape(2, 4, 8, 4), ("dir", "y", "z", "x"))
    states = P("dir", None, ("y", "z", "x"), None)
    return jax.shard_map(
        body,
        mesh=fine,
        in_specs=(states, states, states, P(), P(("y", "z", "x"), None, "dir")),
        out_specs=P(None, ("y", "z", "x"), "dir"),
        check_vma=False,
    )
```

time: 713 us -> 322 us (0.45)
  blocking collectives: 374 us -> 0 us
  starting transfers between devices: 35.4 us -> 147 us
  waiting for transfers between devices: 145 us -> 52.5 us
  Pallas kernels: 0 us -> 47.3 us
  matrix products: 46.6 us -> 0 us
  other arithmetic: 32.7 us -> 8.41 us
  local copies, waits for them, and re-layouts: 68.5 us -> 51 us
  between operations: 0.24 us -> 14 us
  loops' own time: 9.77 us -> 0 us
    all_to_all x1 -> x0, blocking collectives: 374 us -> none  [body(): lax.all_to_all(partial_value.reshape(devices, piece, 2 * columns), 'seq',...]
    ppermute x3 -> x17, starting transfers between devices: 3.14 us -> 94.2 us  [the longest x4 68.1 us: body(): other = lax.ppermute(mine, 'dir', [(0, 1), (1, 0)])]
    all_to_all x3 -> x12, waiting for transfers between devices: 136 us -> 47.4 us  [exchange(): return lax.all_to_all(parts, 'x', split_axis=0, concat_axis=0, tiled=True)]
    pallas_call x0 -> x12, Pallas kernels: none -> 47.3 us  [the longest x4 29.5 us: attend(): pl.pallas_call(attend_kernel, grid=(features // lanes,), in_specs=[pl.Blo...]
    dot_general x33 -> x0, matrix products: 46.6 us -> none  [the longest x16 25.4 us: single_block(): jnp.einsum('qhc,khc->hqk', q_part, k_part, preferred_element_type=jnp.flo...]
    gather x1 -> x0, local copies, waits for them, and re-layouts: 29.2 us -> none  [body(): right_side = jnp.take(right_side, mirror, axis=0)]
    all_to_all x3 -> x12, starting transfers between devices: 32.3 us -> 52.7 us  [exchange(): return lax.all_to_all(parts, 'x', split_axis=0, concat_axis=0, tiled=True)]
    reduce_sum x18 -> x6, other arithmetic: 19.1 us -> 2.93 us  [the longest x4 1.38 us: body(): total = jnp.sum(exchange(partial_value).astype(jnp.float32), axis=0)]
  transfers between devices with their start and end apart: 6 -> 30, of which waited for: 4 -> 9; matrix products, arithmetic and copies ran while one was open for 12% -> 12% of each run, Pallas kernels for 0% -> 15%
where the time goes in v1:
time: 322 us; the launch traced here: 320 us
  starting transfers between devices  147 us (46%)
  waiting for transfers between devices  52.5 us (16%)
  local copies, waits for them, and re-layouts  51 us (16%)
  Pallas kernels  47.3 us (15%)
  between operations  14 us (4%)
  other arithmetic  8.41 us (3%)
    ppermute x4, starting transfers between devices, body(): other = lax.ppermute(mine, 'dir', [(0, 1), (1, 0)])  68.1 us
    all_to_all x12, starting transfers between devices, exchange(): return lax.all_to_all(parts, 'x', split_axis=0, concat_axis=0, tiled=True)  52.7 us
    all_to_all x12, waiting for transfers between devices, exchange(): return lax.all_to_all(parts, 'x', split_axis=0, concat_axis=0, tiled=True)  47.4 us
    pallas_call x4, Pallas kernels, attend(): pl.pallas_call(attend_kernel, grid=(features // lanes,), in_specs=[pl.Blo...  29.5 us
    unnamed x57, local copies, waits for them, and re-layouts  18.6 us
    another operation x16, local copies, waits for them, and re-layouts, split(): return states.reshape(piece, pieces, share).transpose(1, 0, 2)  18.2 us
    ppermute x4, starting transfers between devices, body(): before = lax.ppermute(own, ('y', 'z'), next_ring)  16.4 us
    pallas_call x4, Pallas kernels, join(): pl.pallas_call(join_kernel, grid_spec=pltpu.PrefetchScalarGridSpec(num_sc...  14.4 us
  transfers between devices with their start and end apart: 30, of which 9 were waited for; matrix products, arithmetic and copies ran while one was open for 12% of the time, Pallas kernels for 15%

profile of v1, /device:TPU:8, one launch (start us, length us, event | category | flops | bytes accessed | tf_op | source)
XLA Modules:
  0.0 320.2 jit_solution(15514211569267572801)
XLA Ops:
  6.5 0.9 copy.46
  7.5 3.3 %collective-permute-start.4 = (bf16[64,1024]{1,0:T(8,128)(2,1)S(1)}, bf16[64,1024]{1,0:T(8,128)(2,1)S(1)}, u32[]{:S(2)}, u32[]{:S(2)}) collective-permute-start(bf16[64,1024]{1,0:T(8,128)(2,1)S(1)} %bitcast.116), channel_id=1, source_target_pairs={{0,0},{1,32},{2,64},{3,96},{32,1},{33,33},{34,65},{35,97},{64,2},{... | collective-permute-start | bytes 393224 | tf_op jit(solution)/shard_map/ppermute | solution.py:173
  10.8 4.7 %collective-permute-done.4 = bf16[64,1024]{1,0:T(8,128)(2,1)S(1)} collective-permute-done((bf16[64,1024]{1,0:T(8,128)(2,1)S(1)}, bf16[64,1024]{1,0:T(8,128)(2,1)S(1)}, u32[]{:S(2)}, u32[]{:S(2)}) %collective-permute-start.4) | collective-permute-done | bytes 131104 | tf_op jit(solution)/shard_map/ppermute | solution.py:173
  16.2 2.7 fusion.13
  19.3 1.0 copy.62
  20.2 7.8 %all-to-all-start = ((bf16[4,64,1024]{2,1,0:T(8,128)(2,1)}), bf16[4,64,1024]{2,1,0:T(8,128)(2,1)S(1)}, u32[]{:S(2)}, u32[]{:S(2)}) async-start(bf16[4,64,1024]{2,1,0:T(8,128)(2,1)} %bitcast.103), calls=%async_computation | async-start | bytes 1048576 | tf_op jit(solution)/shard_map/all_to_all | solution.py:168
  28.1 1.2 fusion.11
  29.7 2.7 fusion.12
  33.0 1.1 pad_maximum_fusion
  34.1 2.3 all-to-all-done.q_ref
  37.2 3.5 %all-to-all-start.1 = ((bf16[4,2,64,1024]{3,2,1,0:T(8,128)(2,1)}), bf16[4,2,64,1024]{3,2,1,0:T(8,128)(2,1)S(1)}, u32[]{:S(2)}, u32[]{:S(2)}) async-start(bf16[4,2,64,1024]{3,2,1,0:T(8,128)(2,1)} %pad_maximum_fusion), calls=%async_computation.1 | async-start | bytes 2097152 | tf_op jit(solution)/shard_map/all_to_all | solution.py:168
  41.9 1.1 pad_maximum_fusion.1
  42.9 10.5 %all-to-all-done.1.own_ref = bf16[4,2,64,1024]{3,2,1,0:T(8,128)(2,1)S(1)} async-done(((bf16[4,2,64,1024]{3,2,1,0:T(8,128)(2,1)}), bf16[4,2,64,1024]{3,2,1,0:T(8,128)(2,1)S(1)}, u32[]{:S(2)}, u32[]{:S(2)}) %all-to-all-start.1) | async-done | bytes 1048608 | tf_op jit(solution)/shard_map/all_to_all | solution.py:168
  53.5 4.2 %all-to-all-start.4 = ((bf16[4,2,64,1024]{3,2,1,0:T(8,128)(2,1)}), bf16[4,2,64,1024]{3,2,1,0:T(8,128)(2,1)}, u32[]{:S(2)}, u32[]{:S(2)}) async-start(bf16[4,2,64,1024]{3,2,1,0:T(8,128)(2,1)} %pad_maximum_fusion.1), calls=%async_computation.4 | async-start | bytes 2097152 | tf_op jit(solution)/shard_map/all_to_all | solution.py:168
  58.8 1.1 pad_maximum_fusion.2
  59.9 9.5 %all-to-all-done.4.own_ref = bf16[4,2,64,1024]{3,2,1,0:T(8,128)(2,1)} async-done(((bf16[4,2,64,1024]{3,2,1,0:T(8,128)(2,1)}), bf16[4,2,64,1024]{3,2,1,0:T(8,128)(2,1)}, u32[]{:S(2)}, u32[]{:S(2)}) %all-to-all-start.4) | async-done | bytes 1048608 | tf_op jit(solution)/shard_map/all_to_all | solution.py:168
  69.4 3.5 %all-to-all-start.7 = ((bf16[4,2,64,1024]{3,2,1,0:T(8,128)(2,1)}), bf16[4,2,64,1024]{3,2,1,0:T(8,128)(2,1)S(1)}, u32[]{:S(2)}, u32[]{:S(2)}) async-start(bf16[4,2,64,1024]{3,2,1,0:T(8,128)(2,1)} %pad_maximum_fusion.2), calls=%async_computation.7 | async-start | bytes 2097152 | tf_op jit(solution)/shard_map/all_to_all | solution.py:168
  73.3 1.4 reshape_squeeze.47
  75.1 1.1 pad_maximum_fusion.3
  76.2 7.6 %all-to-all-done.7.own_ref = bf16[4,2,64,1024]{3,2,1,0:T(8,128)(2,1)S(1)} async-done(((bf16[4,2,64,1024]{3,2,1,0:T(8,128)(2,1)}), bf16[4,2,64,1024]{3,2,1,0:T(8,128)(2,1)S(1)}, u32[]{:S(2)}, u32[]{:S(2)}) %all-to-all-start.7) | async-done | bytes 1048608 | tf_op jit(solution)/shard_map/all_to_all | solution.py:168
  83.8 3.5 %all-to-all-start.10 = ((bf16[4,2,64,1024]{3,2,1,0:T(8,128)(2,1)}), bf16[4,2,64,1024]{3,2,1,0:T(8,128)(2,1)S(1)}, u32[]{:S(2)}, u32[]{:S(2)}) async-start(bf16[4,2,64,1024]{3,2,1,0:T(8,128)(2,1)} %pad_maximum_fusion.3), calls=%async_computation.10 | async-start | bytes 2097152 | tf_op jit(solution)/shard_map/all_to_all | solution.py:168
  88.1 3.8 %collective-permute-start = (bf16[4,2,64,1024]{3,2,1,0:T(8,128)(2,1)S(1)}, bf16[4,2,64,1024]{3,2,1,0:T(8,128)(2,1)}, u32[]{:S(2)}, u32[]{:S(2)}) collective-permute-start(bf16[4,2,64,1024]{3,2,1,0:T(8,128)(2,1)S(1)} %all-to-all-done.1.own_ref), channel_id=1, source_target_pairs={{0,4},{4,8},{8,12},{12,16},{16,20},{20,24},{24,28},{28,32},{32,36}... | collective-permute-start | bytes 3145736 | tf_op jit(solution)/shard_map/ppermute | solution.py:196
  91.9 2.3 reshape_squeeze.39
  94.2 2.0 copy.61
  97.1 3.8 %collective-permute-start.5 = (bf16[4,2,64,1024]{3,2,1,0:T(8,128)(2,1)}, bf16[4,2,64,1024]{3,2,1,0:T(8,128)(2,1)}, u32[]{:S(2)}, u32[]{:S(2)}) collective-permute-start(bf16[4,2,64,1024]{3,2,1,0:T(8,128)(2,1)} %all-to-all-done.4.own_ref), channel_id=1, source_target_pairs={{0,4},{4,8},{8,12},{12,16},{16,20},{20,24},{24,28},{28,32},{32,36}... | collective-permute-start | bytes 3145736 | tf_op jit(solution)/shard_map/ppermute | solution.py:196
  100.9 4.8 %all-to-all-start.3 = ((bf16[4,64,1024]{2,1,0:T(8,128)(2,1)}), bf16[4,64,1024]{2,1,0:T(8,128)(2,1)}, u32[]{:S(2)}, u32[]{:S(2)}) async-start(bf16[4,64,1024]{2,1,0:T(8,128)(2,1)} %bitcast.114), calls=%async_computation.3 | async-start | bytes 1048576 | tf_op jit(solution)/shard_map/all_to_all | solution.py:168
  106.4 3.8 %collective-permute-start.9 = (bf16[4,2,64,1024]{3,2,1,0:T(8,128)(2,1)S(1)}, bf16[4,2,64,1024]{3,2,1,0:T(8,128)(2,1)}, u32[]{:S(2)}, u32[]{:S(2)}) collective-permute-start(bf16[4,2,64,1024]{3,2,1,0:T(8,128)(2,1)S(1)} %all-to-all-done.7.own_ref), channel_id=1, source_target_pairs={{0,4},{4,8},{8,12},{12,16},{16,20},{20,24},{24,28},{28,32},{32,36}... | collective-permute-start | bytes 3145736 | tf_op jit(solution)/shard_map/ppermute | solution.py:196
  110.3 2.2 reshape_squeeze.42
  112.5 2.0 copy.60
  114.5 5.0 %collective-permute-start.13 = (bf16[4,2,64,1024]{3,2,1,0:T(8,128)(2,1)S(1)}, bf16[4,2,64,1024]{3,2,1,0:T(8,128)(2,1)}, u32[]{:S(2)}, u32[]{:S(2)}) collective-permute-start(bf16[4,2,64,1024]{3,2,1,0:T(8,128)(2,1)S(1)} %all-to-all-done.10.own_ref), channel_id=1, source_target_pairs={{0,4},{4,8},{8,12},{12,16},{16,20},{20,24},{24,28},{28,32},{32,36}... | collective-permute-start | bytes 3145736 | tf_op jit(solution)/shard_map/ppermute | solution.py:196
  119.6 4.8 %all-to-all-start.6 = ((bf16[4,64,1024]{2,1,0:T(8,128)(2,1)}), bf16[4,64,1024]{2,1,0:T(8,128)(2,1)}, u32[]{:S(2)}, u32[]{:S(2)}) async-start(bf16[4,64,1024]{2,1,0:T(8,128)(2,1)} %bitcast.113), calls=%async_computation.6 | async-start | bytes 1048576 | tf_op jit(solution)/shard_map/all_to_all | solution.py:168
  124.9 1.0 copy-done.5
  125.9 7.4 %attend.4 = (bf16[256,1024]{1,0:T(8,128)(2,1)S(1)}, bf16[128,1024]{1,0:T(8,128)(2,1)}, bf16[128,1024]{1,0:T(8,128)(2,1)}) custom-call(s32[2]{0:T(128)S(1)} %get-tuple-element.54.edge_ref, s32[256,1]{1,0:T(8,128)S(1)} %copy.29.low_ref, bf16[4,64,1024]{2,1,0:T(8,128)(2,1)S(1)} %copy-done.5, bf16[4,2,64,1024]{3,2,1,0:T(8,128)(2,1)S(1)} %all-to-all-done.1.own_ref, ...), custom_call_target="tpu_custom_call" | custom-call | flops 1000000000 | bytes 4194304 | tf_op jit(solution)/shard_map/attend/pallas_call | solution.py:81
  136.5 1.5 copy.34.low_ref
  138.0 2.2 reshape_squeeze.45
  140.2 2.0 copy.59
  142.9 0.9 copy-done.13
  144.5 50.3 %collective-permute-start.3 = (bf16[256,1024]{1,0:T(8,128)(2,1)S(1)}, bf16[256,1024]{1,0:T(8,128)(2,1)}, u32[]{:S(2)}, u32[]{:S(2)}) collective-permute-start(bf16[256,1024]{1,0:T(8,128)(2,1)S(1)} %mirror.4.mine_ref), channel_id=1, source_target_pairs={{0,128},{128,0},{1,129},{129,1},{2,130},{130,2},{3,131},{131,3},{4... | collective-permute-start | bytes 1572872 | tf_op jit(solution)/shard_map/ppermute | solution.py:201
  194.7 4.5 %all-to-all-start.9 = ((bf16[4,64,1024]{2,1,0:T(8,128)(2,1)}), bf16[4,64,1024]{2,1,0:T(8,128)(2,1)}, u32[]{:S(2)}, u32[]{:S(2)}) async-start(bf16[4,64,1024]{2,1,0:T(8,128)(2,1)} %bitcast.112), calls=%async_computation.9 | async-start | bytes 1048576 | tf_op jit(solution)/shard_map/all_to_all | solution.py:168
  200.2 7.4 %attend.5 = (bf16[256,1024]{1,0:T(8,128)(2,1)S(1)}, bf16[128,1024]{1,0:T(8,128)(2,1)}, bf16[128,1024]{1,0:T(8,128)(2,1)S(1)}) custom-call(s32[2]{0:T(128)S(1)} %get-tuple-element.57.edge_ref, s32[256,1]{1,0:T(8,128)S(1)} %copy-done.17, bf16[4,64,1024]{2,1,0:T(8,128)(2,1)} %all-to-all-done.3.q_ref, bf16[4,2,64,1024]{3,2,1,0:T(8,128)(2,1)} %all-to-all-done.4.own_ref, ...), custom_call_target="tpu_custom_call" | custom-call | flops 1000000000 | bytes 4194304 | tf_op jit(solution)/shard_map/attend/pallas_call | solution.py:81
  210.6 1.5 copy.39.low_ref
  213.6 1.0 copy-done.11
  214.6 0.9 copy-done.15
  216.2 6.0 %collective-permute-start.8 = (bf16[256,1024]{1,0:T(8,128)(2,1)S(1)}, bf16[256,1024]{1,0:T(8,128)(2,1)}, u32[]{:S(2)}, u32[]{:S(2)}) collective-permute-start(bf16[256,1024]{1,0:T(8,128)(2,1)S(1)} %mirror.5.mine_ref), channel_id=1, source_target_pairs={{0,128},{128,0},{1,129},{129,1},{2,130},{130,2},{3,131},{131,3},{4... | collective-permute-start | bytes 1572872 | tf_op jit(solution)/shard_map/ppermute | solution.py:201
  223.2 7.4 %attend.6 = (bf16[256,1024]{1,0:T(8,128)(2,1)S(1)}, bf16[128,1024]{1,0:T(8,128)(2,1)}, bf16[128,1024]{1,0:T(8,128)(2,1)}) custom-call(s32[2]{0:T(128)S(1)} %get-tuple-element.56.edge_ref, s32[256,1]{1,0:T(8,128)S(1)} %copy-done.18, bf16[4,64,1024]{2,1,0:T(8,128)(2,1)} %all-to-all-done.6.q_ref, bf16[4,2,64,1024]{3,2,1,0:T(8,128)(2,1)S(1)} %all-to-all-done.7.own_ref, ...), custom_call_target="tpu_custom_call" | custom-call | flops 1000000000 | bytes 4194304 | tf_op jit(solution)/shard_map/attend/pallas_call | solution.py:81
  232.7 7.4 %attend.7 = (bf16[256,1024]{1,0:T(8,128)(2,1)S(1)}, bf16[128,1024]{1,0:T(8,128)(2,1)}, bf16[128,1024]{1,0:T(8,128)(2,1)}) custom-call(s32[2]{0:T(128)S(1)} %get-tuple-element.55.edge_ref, s32[256,1]{1,0:T(8,128)S(1)} %copy-done.16, bf16[4,64,1024]{2,1,0:T(8,128)(2,1)} %all-to-all-done.9.q_ref, bf16[4,2,64,1024]{3,2,1,0:T(8,128)(2,1)S(1)} %all-to-all-done.10.own_ref, ...), custom_call_target="tpu_custom_call" | custom-call | flops 1000000000 | bytes 4194304 | tf_op jit(solution)/shard_map/attend/pallas_call | solution.py:81
  240.8 1.4 collective-permute-start.15
  242.2 2.2 copy-done
  244.4 4.0 %join.4 = bf16[4,64,1024]{2,1,0:T(8,128)(2,1)} custom-call(s32[1]{0:T(128)} %bitcast.side_ref, bf16[256,1024]{1,0:T(8,128)(2,1)S(1)} %mirror.4.mine_ref, bf16[256,1024]{1,0:T(8,128)(2,1)} %collective-permute-done.3.other_ref, bf16[8,2,128,1024]{3,2,1,0:T(8,128)(2,1)S(1)} %bitcast.104, bf16[8,2,128,1024]{3,2,1,0:T(8,128)(2,1)S(1)} %bitcast.105), custom_call_target="tpu_custom_call" | custom-call | flops 1000000000 | bytes 6291456 | tf_op jit(solution)/shard_map/join/pallas_call | solution.py:139
  248.4 4.5 %all-to-all-start.2 = ((bf16[4,64,1024]{2,1,0:T(8,128)(2,1)}), bf16[4,64,1024]{2,1,0:T(8,128)(2,1)}, u32[]{:S(2)}, u32[]{:S(2)}) async-start(bf16[4,64,1024]{2,1,0:T(8,128)(2,1)} %join.4), calls=%async_computation.2 | async-start | bytes 1048576 | tf_op jit(solution)/shard_map/all_to_all | solution.py:168
  253.7 11.7 %collective-permute-start.12 = (bf16[256,1024]{1,0:T(8,128)(2,1)S(1)}, bf16[256,1024]{1,0:T(8,128)(2,1)S(1)}, u32[]{:S(2)}, u32[]{:S(2)}) collective-permute-start(bf16[256,1024]{1,0:T(8,128)(2,1)S(1)} %mirror.6.mine_ref), channel_id=1, source_target_pairs={{0,128},{128,0},{1,129},{129,1},{2,130},{130,2},{3,131},{131,3},{4... | collective-permute-start | bytes 1572872 | tf_op jit(solution)/shard_map/ppermute | solution.py:201
  265.6 1.6 mirror.7.mine_ref
  267.2 2.2 copy-done.1
  269.4 4.0 %join.5 = bf16[4,64,1024]{2,1,0:T(8,128)(2,1)} custom-call(s32[1]{0:T(128)} %bitcast.side_ref, bf16[256,1024]{1,0:T(8,128)(2,1)S(1)} %mirror.5.mine_ref, bf16[256,1024]{1,0:T(8,128)(2,1)} %collective-permute-done.8.other_ref, bf16[8,2,128,1024]{3,2,1,0:T(8,128)(2,1)S(1)} %bitcast.106, bf16[8,2,128,1024]{3,2,1,0:T(8,128)(2,1)S(1)} %bitcast.107), custom_call_target="tpu_custom_call" | custom-call | flops 1000000000 | bytes 6291456 | tf_op jit(solution)/shard_map/join/pallas_call | solution.py:139
  273.5 4.5 %all-to-all-start.5 = ((bf16[4,64,1024]{2,1,0:T(8,128)(2,1)}), bf16[4,64,1024]{2,1,0:T(8,128)(2,1)S(1)}, u32[]{:S(2)}, u32[]{:S(2)}) async-start(bf16[4,64,1024]{2,1,0:T(8,128)(2,1)} %join.5), calls=%async_computation.5 | async-start | bytes 1048576 | tf_op jit(solution)/shard_map/all_to_all | solution.py:168
  278.0 2.2 copy-done.2
  280.2 3.2 join.6
  283.4 3.1 join.7
  286.5 1.6 all-to-all-done.5
  288.1 3.5 %all-to-all-start.8 = ((bf16[4,64,1024]{2,1,0:T(8,128)(2,1)}), bf16[4,64,1024]{2,1,0:T(8,128)(2,1)S(1)}, u32[]{:S(2)}, u32[]{:S(2)}) async-start(bf16[4,64,1024]{2,1,0:T(8,128)(2,1)} %join.6), calls=%async_computation.8 | async-start | bytes 1048576 | tf_op jit(solution)/shard_map/all_to_all | solution.py:168
  291.6 1.1 convert_reduce_fusion.3
  292.9 8.0 %all-to-all-done.8 = bf16[4,64,1024]{2,1,0:T(8,128)(2,1)S(1)} async-done(((bf16[4,64,1024]{2,1,0:T(8,128)(2,1)}), bf16[4,64,1024]{2,1,0:T(8,128)(2,1)S(1)}, u32[]{:S(2)}, u32[]{:S(2)}) %all-to-all-start.8) | async-done | bytes 524320 | tf_op jit(solution)/shard_map/all_to_all | solution.py:168
  300.9 3.5 %all-to-all-start.11 = ((bf16[4,64,1024]{2,1,0:T(8,128)(2,1)}), bf16[4,64,1024]{2,1,0:T(8,128)(2,1)S(1)}, u32[]{:S(2)}, u32[]{:S(2)}) async-start(bf16[4,64,1024]{2,1,0:T(8,128)(2,1)} %join.7), calls=%async_computation.11 | async-start | bytes 1048576 | tf_op jit(solution)/shard_map/all_to_all | solution.py:168
  304.6 7.9 %all-to-all-done.11 = bf16[4,64,1024]{2,1,0:T(8,128)(2,1)S(1)} async-done(((bf16[4,64,1024]{2,1,0:T(8,128)(2,1)}), bf16[4,64,1024]{2,1,0:T(8,128)(2,1)S(1)}, u32[]{:S(2)}, u32[]{:S(2)}) %all-to-all-start.11) | async-done | bytes 524320 | tf_op jit(solution)/shard_map/all_to_all | solution.py:168
  (123 shorter events, 25.0 us)
Async XLA Ops:
  6.5 235.6 %all-gather.2.cloned.1.call-start = ((), (), s32[]{:S(2)}) async-start(), calls=%async_computation.12 | async-start | bytes 4325376 | tf_op jit(solution)/shard_map/all_gather | solution.py:176
  7.5 8.0 %collective-permute-start.4 = (bf16[64,1024]{1,0:T(8,128)(2,1)S(1)}, bf16[64,1024]{1,0:T(8,128)(2,1)S(1)}, u32[]{:S(2)}, u32[]{:S(2)}) collective-permute-start(bf16[64,1024]{1,0:T(8,128)(2,1)S(1)} %bitcast.116), channel_id=1, source_target_pairs={{0,0},{1,32},{2,64},{3,96},{32,1},{33,33},{34,65},{35,97},{64,2},{... | collective-permute-start | bytes 393224 | tf_op jit(solution)/shard_map/ppermute | solution.py:173
  15.5 0.7 copy-start.24
  18.9 9.2 %copy-start.19 = (bf16[1,4,64,4096]{3,2,1,0:T(8,128)(2,1)S(1)}, bf16[1,4,64,4096]{3,2,1,0:T(8,128)(2,1)}, u32[]{:S(2)}) copy-start(bf16[1,4,64,4096]{3,2,1,0:T(8,128)(2,1)} %param.6) | copy-start | bytes 6291460
  20.2 16.2 %all-to-all-start = ((bf16[4,64,1024]{2,1,0:T(8,128)(2,1)}), bf16[4,64,1024]{2,1,0:T(8,128)(2,1)S(1)}, u32[]{:S(2)}, u32[]{:S(2)}) async-start(bf16[4,64,1024]{2,1,0:T(8,128)(2,1)} %bitcast.103), calls=%async_computation | async-start | bytes 1048576 | tf_op jit(solution)/shard_map/all_to_all | solution.py:168
  33.0 7.7 %copy-start.23 = (bf16[1,1,64,4096]{3,2,1,0:T(8,128)(2,1)S(1)}, bf16[1,1,64,4096]{3,2,1,0:T(8,128)(2,1)}, u32[]{:S(2)}) copy-start(bf16[1,1,64,4096]{3,2,1,0:T(8,128)(2,1)} %get-tuple-element.35) | copy-start | bytes 1572868
  36.4 0.8 copy-start.4
  37.2 16.2 %all-to-all-start.1 = ((bf16[4,2,64,1024]{3,2,1,0:T(8,128)(2,1)}), bf16[4,2,64,1024]{3,2,1,0:T(8,128)(2,1)S(1)}, u32[]{:S(2)}, u32[]{:S(2)}) async-start(bf16[4,2,64,1024]{3,2,1,0:T(8,128)(2,1)} %pad_maximum_fusion), calls=%async_computation.1 | async-start | bytes 2097152 | tf_op jit(solution)/shard_map/all_to_all | solution.py:168
  41.8 15.9 %copy-start.21 = (bf16[1,1,64,4096]{3,2,1,0:T(8,128)(2,1)S(1)}, bf16[1,1,64,4096]{3,2,1,0:T(8,128)(2,1)}, u32[]{:S(2)}) copy-start(bf16[1,1,64,4096]{3,2,1,0:T(8,128)(2,1)} %get-tuple-element.37) | copy-start | bytes 1572868
  42.9 15.2 %copy-start.22 = (bf16[1,1,64,4096]{3,2,1,0:T(8,128)(2,1)S(1)}, bf16[1,1,64,4096]{3,2,1,0:T(8,128)(2,1)}, u32[]{:S(2)}) copy-start(bf16[1,1,64,4096]{3,2,1,0:T(8,128)(2,1)} %get-tuple-element.41) | copy-start | bytes 1572868
  53.5 15.9 %all-to-all-start.4 = ((bf16[4,2,64,1024]{3,2,1,0:T(8,128)(2,1)}), bf16[4,2,64,1024]{3,2,1,0:T(8,128)(2,1)}, u32[]{:S(2)}, u32[]{:S(2)}) async-start(bf16[4,2,64,1024]{3,2,1,0:T(8,128)(2,1)} %pad_maximum_fusion.1), calls=%async_computation.4 | async-start | bytes 2097152 | tf_op jit(solution)/shard_map/all_to_all | solution.py:168
  59.9 13.0 %copy-start.20 = (bf16[1,1,64,4096]{3,2,1,0:T(8,128)(2,1)S(1)}, bf16[1,1,64,4096]{3,2,1,0:T(8,128)(2,1)}, u32[]{:S(2)}) copy-start(bf16[1,1,64,4096]{3,2,1,0:T(8,128)(2,1)} %get-tuple-element.36) | copy-start | bytes 1572868
  69.4 14.4 %all-to-all-start.7 = ((bf16[4,2,64,1024]{3,2,1,0:T(8,128)(2,1)}), bf16[4,2,64,1024]{3,2,1,0:T(8,128)(2,1)S(1)}, u32[]{:S(2)}, u32[]{:S(2)}) async-start(bf16[4,2,64,1024]{3,2,1,0:T(8,128)(2,1)} %pad_maximum_fusion.2), calls=%async_computation.7 | async-start | bytes 2097152 | tf_op jit(solution)/shard_map/all_to_all | solution.py:168
  75.1 12.4 %copy-start.25 = (s32[4,512]{1,0:T(4,128)S(1)}, s32[4,512]{1,0:T(4,128)}, u32[]{:S(2)}) copy-start(s32[4,512]{1,0:T(4,128)} %param.8) | copy-start | bytes 24580
  83.8 17.1 %all-to-all-start.10 = ((bf16[4,2,64,1024]{3,2,1,0:T(8,128)(2,1)}), bf16[4,2,64,1024]{3,2,1,0:T(8,128)(2,1)S(1)}, u32[]{:S(2)}, u32[]{:S(2)}) async-start(bf16[4,2,64,1024]{3,2,1,0:T(8,128)(2,1)} %pad_maximum_fusion.3), calls=%async_computation.10 | async-start | bytes 2097152 | tf_op jit(solution)/shard_map/all_to_all | solution.py:168
  88.1 36.8 %collective-permute-start = (bf16[4,2,64,1024]{3,2,1,0:T(8,128)(2,1)S(1)}, bf16[4,2,64,1024]{3,2,1,0:T(8,128)(2,1)}, u32[]{:S(2)}, u32[]{:S(2)}) collective-permute-start(bf16[4,2,64,1024]{3,2,1,0:T(8,128)(2,1)S(1)} %all-to-all-done.1.own_ref), channel_id=1, source_target_pairs={{0,4},{4,8},{8,12},{12,16},{16,20},{20,24},{24,28},{28,32},{32,36}... | collective-permute-start | bytes 3145736 | tf_op jit(solution)/shard_map/ppermute | solution.py:196
  97.1 102.2 %collective-permute-start.5 = (bf16[4,2,64,1024]{3,2,1,0:T(8,128)(2,1)}, bf16[4,2,64,1024]{3,2,1,0:T(8,128)(2,1)}, u32[]{:S(2)}, u32[]{:S(2)}) collective-permute-start(bf16[4,2,64,1024]{3,2,1,0:T(8,128)(2,1)} %all-to-all-done.4.own_ref), channel_id=1, source_target_pairs={{0,4},{4,8},{8,12},{12,16},{16,20},{20,24},{24,28},{28,32},{32,36}... | collective-permute-start | bytes 3145736 | tf_op jit(solution)/shard_map/ppermute | solution.py:196
  100.9 18.7 %all-to-all-start.3 = ((bf16[4,64,1024]{2,1,0:T(8,128)(2,1)}), bf16[4,64,1024]{2,1,0:T(8,128)(2,1)}, u32[]{:S(2)}, u32[]{:S(2)}) async-start(bf16[4,64,1024]{2,1,0:T(8,128)(2,1)} %bitcast.114), calls=%async_computation.3 | async-start | bytes 1048576 | tf_op jit(solution)/shard_map/all_to_all | solution.py:168
  106.4 115.9 %collective-permute-start.9 = (bf16[4,2,64,1024]{3,2,1,0:T(8,128)(2,1)S(1)}, bf16[4,2,64,1024]{3,2,1,0:T(8,128)(2,1)}, u32[]{:S(2)}, u32[]{:S(2)}) collective-permute-start(bf16[4,2,64,1024]{3,2,1,0:T(8,128)(2,1)S(1)} %all-to-all-done.7.own_ref), channel_id=1, source_target_pairs={{0,4},{4,8},{8,12},{12,16},{16,20},{20,24},{24,28},{28,32},{32,36}... | collective-permute-start | bytes 3145736 | tf_op jit(solution)/shard_map/ppermute | solution.py:196
  114.5 118.2 %collective-permute-start.13 = (bf16[4,2,64,1024]{3,2,1,0:T(8,128)(2,1)S(1)}, bf16[4,2,64,1024]{3,2,1,0:T(8,128)(2,1)}, u32[]{:S(2)}, u32[]{:S(2)}) collective-permute-start(bf16[4,2,64,1024]{3,2,1,0:T(8,128)(2,1)S(1)} %all-to-all-done.10.own_ref), channel_id=1, source_target_pairs={{0,4},{4,8},{8,12},{12,16},{16,20},{20,24},{24,28},{28,32},{32,36}... | collective-permute-start | bytes 3145736 | tf_op jit(solution)/shard_map/ppermute | solution.py:196
  119.6 75.1 %all-to-all-start.6 = ((bf16[4,64,1024]{2,1,0:T(8,128)(2,1)}), bf16[4,64,1024]{2,1,0:T(8,128)(2,1)}, u32[]{:S(2)}, u32[]{:S(2)}) async-start(bf16[4,64,1024]{2,1,0:T(8,128)(2,1)} %bitcast.113), calls=%async_computation.6 | async-start | bytes 1048576 | tf_op jit(solution)/shard_map/all_to_all | solution.py:168
  124.9 1.0 copy-start.5
  133.3 0.8 copy-start.8
  134.1 8.8 %copy-start.9 = (bf16[256,1024]{1,0:T(8,128)(2,1)S(1)}, bf16[256,1024]{1,0:T(8,128)(2,1)}, u32[]{:S(2)}) copy-start(bf16[256,1024]{1,0:T(8,128)(2,1)} %copy-done.8) | copy-start | bytes 1572868
  134.1 8.1 %collective-permute-start.1 = (bf16[128,1024]{1,0:T(8,128)(2,1)}, bf16[128,1024]{1,0:T(8,128)(2,1)S(1)}, u32[]{:S(2)}, u32[]{:S(2)}) collective-permute-start(bf16[128,1024]{1,0:T(8,128)(2,1)} %get-tuple-element.18), channel_id=1, source_target_pairs={{128,132},{132,136},{136,140},{140,144},{144,148},{148,152},{152,1... | collective-permute-start | bytes 786440 | tf_op jit(solution)/shard_map/ppermute | solution.py:198
  134.9 7.3 %collective-permute-start.2 = (bf16[128,1024]{1,0:T(8,128)(2,1)}, bf16[128,1024]{1,0:T(8,128)(2,1)S(1)}, u32[]{:S(2)}, u32[]{:S(2)}) collective-permute-start(bf16[128,1024]{1,0:T(8,128)(2,1)} %get-tuple-element.19), channel_id=1, source_target_pairs={{132,128},{136,132},{140,136},{144,140},{148,144},{152,148},{156,1... | collective-permute-start | bytes 786440 | tf_op jit(solution)/shard_map/ppermute | solution.py:199
  142.2 0.7 copy-start.12
  142.9 1.0 copy-start.13
  144.5 96.3 %collective-permute-start.3 = (bf16[256,1024]{1,0:T(8,128)(2,1)S(1)}, bf16[256,1024]{1,0:T(8,128)(2,1)}, u32[]{:S(2)}, u32[]{:S(2)}) collective-permute-start(bf16[256,1024]{1,0:T(8,128)(2,1)S(1)} %mirror.4.mine_ref), channel_id=1, source_target_pairs={{0,128},{128,0},{1,129},{129,1},{2,130},{130,2},{3,131},{131,3},{4... | collective-permute-start | bytes 1572872 | tf_op jit(solution)/shard_map/ppermute | solution.py:201
  194.7 38.0 %all-to-all-start.9 = ((bf16[4,64,1024]{2,1,0:T(8,128)(2,1)}), bf16[4,64,1024]{2,1,0:T(8,128)(2,1)}, u32[]{:S(2)}, u32[]{:S(2)}) async-start(bf16[4,64,1024]{2,1,0:T(8,128)(2,1)} %bitcast.112), calls=%async_computation.9 | async-start | bytes 1048576 | tf_op jit(solution)/shard_map/all_to_all | solution.py:168
  199.3 12.8 %copy-start.27 = (s32[256,1]{0,1:T(1,128)S(1)}, s32[256,1]{0,1:T(1,128)}, u32[]{:S(2)}) copy-start(s32[256,1]{0,1:T(1,128)} %get-tuple-element.49) | copy-start | bytes 3076
  199.3 0.9 copy-start.17
  207.6 0.8 copy-start.10
  208.4 4.5 %collective-permute-start.6 = (bf16[128,1024]{1,0:T(8,128)(2,1)}, bf16[128,1024]{1,0:T(8,128)(2,1)S(1)}, u32[]{:S(2)}, u32[]{:S(2)}) collective-permute-start(bf16[128,1024]{1,0:T(8,128)(2,1)} %get-tuple-element.21), channel_id=1, source_target_pairs={{128,132},{132,136},{136,140},{140,144},{144,148},{148,152},{152,1... | collective-permute-start | bytes 786440 | tf_op jit(solution)/shard_map/ppermute | solution.py:198
  209.1 3.8 %collective-permute-start.7 = (bf16[128,1024]{1,0:T(8,128)(2,1)S(1)}, bf16[128,1024]{1,0:T(8,128)(2,1)S(1)}, u32[]{:S(2)}, u32[]{:S(2)}) collective-permute-start(bf16[128,1024]{1,0:T(8,128)(2,1)S(1)} %get-tuple-element.22), channel_id=1, source_target_pairs={{132,128},{136,132},{140,136},{144,140},{148,144},{152,148},{156,1... | collective-permute-start | bytes 786440 | tf_op jit(solution)/shard_map/ppermute | solution.py:199
  212.9 0.7 copy-start.14
  213.6 1.0 copy-start.11
  214.6 0.9 copy-start.15
  216.2 16.5 %copy-start.16 = (s32[256,1]{1,0:T(8,128)S(1)}, s32[256,1]{1,0:T(8,128)}, u32[]{:S(2)}) copy-start(s32[256,1]{1,0:T(8,128)} %copy.44.low_ref) | copy-start | bytes 3076
  216.2 51.0 %collective-permute-start.8 = (bf16[256,1024]{1,0:T(8,128)(2,1)S(1)}, bf16[256,1024]{1,0:T(8,128)(2,1)}, u32[]{:S(2)}, u32[]{:S(2)}) collective-permute-start(bf16[256,1024]{1,0:T(8,128)(2,1)S(1)} %mirror.5.mine_ref), channel_id=1, source_target_pairs={{0,128},{128,0},{1,129},{129,1},{2,130},{130,2},{3,131},{131,3},{4... | collective-permute-start | bytes 1572872 | tf_op jit(solution)/shard_map/ppermute | solution.py:201
  222.2 0.9 copy-start.18
  230.5 0.8 copy-start.6
  231.4 21.7 %collective-permute-start.10 = (bf16[128,1024]{1,0:T(8,128)(2,1)}, bf16[128,1024]{1,0:T(8,128)(2,1)S(1)}, u32[]{:S(2)}, u32[]{:S(2)}) collective-permute-start(bf16[128,1024]{1,0:T(8,128)(2,1)} %get-tuple-element.24), channel_id=1, source_target_pairs={{128,132},{132,136},{136,140},{140,144},{144,148},{148,152},{152,1... | collective-permute-start | bytes 786440 | tf_op jit(solution)/shard_map/ppermute | solution.py:198
  232.0 21.0 %collective-permute-start.11 = (bf16[128,1024]{1,0:T(8,128)(2,1)}, bf16[128,1024]{1,0:T(8,128)(2,1)S(1)}, u32[]{:S(2)}, u32[]{:S(2)}) collective-permute-start(bf16[128,1024]{1,0:T(8,128)(2,1)} %get-tuple-element.25), channel_id=1, source_target_pairs={{132,128},{136,132},{140,136},{144,140},{148,144},{152,148},{156,1... | collective-permute-start | bytes 786440 | tf_op jit(solution)/shard_map/ppermute | solution.py:199
  240.1 25.4 %collective-permute-start.14 = (bf16[128,1024]{1,0:T(8,128)(2,1)}, bf16[128,1024]{1,0:T(8,128)(2,1)S(1)}, u32[]{:S(2)}, u32[]{:S(2)}) collective-permute-start(bf16[128,1024]{1,0:T(8,128)(2,1)} %get-tuple-element.27), channel_id=1, source_target_pairs={{128,132},{132,136},{136,140},{140,144},{144,148},{148,152},{152,1... | collective-permute-start | bytes 786440 | tf_op jit(solution)/shard_map/ppermute | solution.py:198
  240.8 24.8 %collective-permute-start.15 = (bf16[128,1024]{1,0:T(8,128)(2,1)}, bf16[128,1024]{1,0:T(8,128)(2,1)}, u32[]{:S(2)}, u32[]{:S(2)}) collective-permute-start(bf16[128,1024]{1,0:T(8,128)(2,1)} %get-tuple-element.28), channel_id=1, source_target_pairs={{132,128},{136,132},{140,136},{144,140},{148,144},{152,148},{156,1... | collective-permute-start | bytes 786440 | tf_op jit(solution)/shard_map/ppermute | solution.py:199
  242.2 2.2 copy-start
  244.4 8.6 %copy-start.26 = (s32[256,1]{0,1:T(1,128)S(1)}, s32[256,1]{0,1:T(1,128)}, u32[]{:S(2)}) copy-start(s32[256,1]{0,1:T(1,128)} %get-tuple-element.59) | copy-start | bytes 3076
  244.4 8.7 %copy-start.7 = (bf16[256,1024]{1,0:T(8,128)(2,1)S(1)}, bf16[256,1024]{1,0:T(8,128)(2,1)}, u32[]{:S(2)}) copy-start(bf16[256,1024]{1,0:T(8,128)(2,1)} %copy-done.6) | copy-start | bytes 1572868
  248.4 25.1 %all-to-all-start.2 = ((bf16[4,64,1024]{2,1,0:T(8,128)(2,1)}), bf16[4,64,1024]{2,1,0:T(8,128)(2,1)}, u32[]{:S(2)}, u32[]{:S(2)}) async-start(bf16[4,64,1024]{2,1,0:T(8,128)(2,1)} %join.4), calls=%async_computation.2 | async-start | bytes 1048576 | tf_op jit(solution)/shard_map/all_to_all | solution.py:168
  253.7 24.3 %collective-permute-start.12 = (bf16[256,1024]{1,0:T(8,128)(2,1)S(1)}, bf16[256,1024]{1,0:T(8,128)(2,1)S(1)}, u32[]{:S(2)}, u32[]{:S(2)}) collective-permute-start(bf16[256,1024]{1,0:T(8,128)(2,1)S(1)} %mirror.6.mine_ref), channel_id=1, source_target_pairs={{0,128},{128,0},{1,129},{129,1},{2,130},{130,2},{3,131},{131,3},{4... | collective-permute-start | bytes 1572872 | tf_op jit(solution)/shard_map/ppermute | solution.py:201
  267.1 16.2 %collective-permute-start.16 = (bf16[256,1024]{1,0:T(8,128)(2,1)S(1)}, bf16[256,1024]{1,0:T(8,128)(2,1)S(1)}, u32[]{:S(2)}, u32[]{:S(2)}) collective-permute-start(bf16[256,1024]{1,0:T(8,128)(2,1)S(1)} %mirror.7.mine_ref), channel_id=1, source_target_pairs={{0,128},{128,0},{1,129},{129,1},{2,130},{130,2},{3,131},{131,3},{4... | collective-permute-start | bytes 1572872 | tf_op jit(solution)/shard_map/ppermute | solution.py:201
  267.2 2.2 copy-start.1
  273.5 14.6 %all-to-all-start.5 = ((bf16[4,64,1024]{2,1,0:T(8,128)(2,1)}), bf16[4,64,1024]{2,1,0:T(8,128)(2,1)S(1)}, u32[]{:S(2)}, u32[]{:S(2)}) async-start(bf16[4,64,1024]{2,1,0:T(8,128)(2,1)} %join.5), calls=%async_computation.5 | async-start | bytes 1048576 | tf_op jit(solution)/shard_map/all_to_all | solution.py:168
  278.0 2.2 copy-start.2
  280.2 3.2 copy-start.3
  288.1 12.8 %all-to-all-start.8 = ((bf16[4,64,1024]{2,1,0:T(8,128)(2,1)}), bf16[4,64,1024]{2,1,0:T(8,128)(2,1)S(1)}, u32[]{:S(2)}, u32[]{:S(2)}) async-start(bf16[4,64,1024]{2,1,0:T(8,128)(2,1)} %join.6), calls=%async_computation.8 | async-start | bytes 1048576 | tf_op jit(solution)/shard_map/all_to_all | solution.py:168
  300.9 11.6 %all-to-all-start.11 = ((bf16[4,64,1024]{2,1,0:T(8,128)(2,1)}), bf16[4,64,1024]{2,1,0:T(8,128)(2,1)S(1)}, u32[]{:S(2)}, u32[]{:S(2)}) async-start(bf16[4,64,1024]{2,1,0:T(8,128)(2,1)} %join.7), calls=%async_computation.11 | async-start | bytes 1048576 | tf_op jit(solution)/shard_map/all_to_all | solution.py:168
Sparse Core Ops, SparseCore 0:
  16.3 90.5 all-gather.1

commit v2 on v1

v2 whole, which is shorter than its diff:
```python
import math

import jax
import jax.numpy as jnp
from jax import lax
from jax.experimental import pallas as pl
from jax.experimental.pallas import tpu as pltpu
from jax.sharding import Mesh
from jax.sharding import PartitionSpec as P

HEAD = 128
SPAN = 256
HALF = SPAN // 2
RINGS = 32
PER_STEP = 2
CHUNKS = ((0, 1), (1, 3), (3, 4))
NT = (((1,), (1,)), ((), ()))
NN = (((1,), (0,)), ((), ()))
ANYWHERE = pl.BlockSpec(memory_space=pl.ANY)
PARAMS = pltpu.CompilerParams(vmem_limit_bytes=32 * 2**20)


def dot(a, b, dims=NN):
    return lax.dot_general(a, b, dims, preferred_element_type=jnp.float32)


def one_hot(index, rows, columns):
    at = lax.broadcasted_iota(jnp.int32, (rows, columns), 1)
    return jnp.where(at == index, 1.0, 0.0).astype(jnp.bfloat16)


def cost(flops, nbytes):
    return pl.CostEstimate(flops=flops, bytes_accessed=nbytes, transcendentals=0)


def table_kernel(place_ref, lengths_ref, first_ref, end_ref, source_ref):
    rows, count = lengths_ref.shape
    base, side = place_ref[0], place_ref[1]
    lengths = lengths_ref[...].astype(jnp.float32)
    upto = lax.broadcasted_iota(jnp.int32, (count, count), 0) <= lax.broadcasted_iota(jnp.int32, (count, count), 1)
    ends = dot(lengths.astype(jnp.bfloat16), jnp.where(upto, 1.0, 0.0).astype(jnp.bfloat16))
    starts = ends - lengths
    here = lax.broadcasted_iota(jnp.int32, (SPAN, 1), 0)
    at = (here + base).astype(jnp.float32)
    for r in range(rows):
        start, stop = starts[r : r + 1], ends[r : r + 1]
        first = jnp.max(jnp.where(start <= at, start, 0.0), axis=1, keepdims=True).astype(jnp.int32) - base
        end = jnp.min(jnp.where(stop > at, stop, 1e9), axis=1, keepdims=True).astype(jnp.int32) - base
        mirror = first + end - 1 - here
        source = jnp.where(
            mirror < 0, SPAN + here - end + HALF, jnp.where(mirror >= SPAN, SPAN + HALF + here - first, mirror)
        )
        first_ref[r] = first
        end_ref[r] = end
        source_ref[r] = jnp.where(side == 0, here, source)


def tables(place, lengths):
    column = jax.ShapeDtypeStruct((lengths.shape[0], SPAN, 1), jnp.int32)
    return pl.pallas_call(
        table_kernel,
        in_specs=[pl.BlockSpec(memory_space=pltpu.SMEM), pl.BlockSpec(memory_space=pltpu.VMEM)],
        out_shape=[column] * 3,
        compiler_params=PARAMS,
        cost_estimate=cost(1, 1),
        name="tables",
    )(place, lengths)


def pack_kernel(count, *refs):
    out_ref = refs[-1]
    pieces, share = out_ref.shape[0], out_ref.shape[-1]
    for t in range(count):
        for f in range(pieces):
            out_ref[f, 0, t] = refs[t][0, 0, :, f * share : (f + 1) * share]


def pack(states, chunk, pieces, after=()):
    low, high = chunk
    _, _, piece, width = states[0].shape
    share = width // pieces
    count = len(states)
    shape = (pieces, high - low, count, piece, share)
    return pl.pallas_call(
        lambda *refs: pack_kernel(count, *refs),
        grid=(high - low,),
        in_specs=[pl.BlockSpec((1, 1, piece, width), lambda r: (0, r + low, 0, 0))] * count + [ANYWHERE] * len(after),
        out_specs=pl.BlockSpec((pieces, 1, count, piece, share), lambda r: (0, r, 0, 0, 0)),
        out_shape=jax.ShapeDtypeStruct(shape, jnp.bfloat16),
        compiler_params=PARAMS,
        cost_estimate=cost(1, 1),
        name="pack",
    )(*states, *after)


def attend_kernel(first_ref, end_ref, q_ref, own_ref, before_ref, *refs):
    out_ref, ahead_ref, back_ref, bias = refs[-4:]
    factor = math.log2(math.e) / math.sqrt(HEAD)
    wide = SPAN + HALF

    @pl.when(pl.program_id(1) == 0)
    def _():
        for part in range(2):
            key = lax.broadcasted_iota(jnp.int32, (HALF, wide), 1) + part * HALF
            here = lax.broadcasted_iota(jnp.int32, (HALF, wide), 0) + (part * HALF + SPAN)
            low = first_ref[0, part * HALF : (part + 1) * HALF, :] + SPAN
            keep = (key >= low) & (key <= here)
            bias[part] = jnp.where(keep, 0.0, -1e30)

    def keyed(index, lanes):
        return jnp.concatenate(
            [before_ref[:, 0, index, :, lanes].reshape(SPAN, HEAD), own_ref[:, 0, index, :, lanes].reshape(SPAN, HEAD)], 0
        )

    for h in range(PER_STEP):
        lanes = slice(h * HEAD, (h + 1) * HEAD)
        q = q_ref[:, 0, 0, :, lanes].reshape(SPAN, HEAD)
        k, v = keyed(0, lanes), keyed(1, lanes)
        for part in range(2):
            rows = slice(part * HALF, (part + 1) * HALF)
            keys = slice(part * HALF, part * HALF + wide)
            scores = dot(q[rows], k[keys], NT) + bias[part]
            top = jnp.max(scores, axis=1, keepdims=True)
            raised = jnp.exp2((scores - top) * factor)
            total = jnp.sum(raised, axis=1, keepdims=True)
            context = dot(raised.astype(jnp.bfloat16), v[keys]) / total
            out_ref[0, rows, lanes] = context.astype(jnp.bfloat16)
    turn = HALF - 1 - lax.broadcasted_iota(jnp.int32, (HALF, 1), 0)
    context = out_ref[0]
    ahead = first_ref[0, SPAN - 1 :, :] + turn
    ahead_ref[0] = dot(one_hot(ahead, HALF, SPAN), context).astype(jnp.bfloat16)
    back = end_ref[0, :1, :] - HALF + turn
    back_ref[0] = dot(one_hot(back, HALF, SPAN), context).astype(jnp.bfloat16)


def attend(first, end, q, own, before, low, after=()):
    pieces, rows, _, piece, features = own.shape
    lanes = PER_STEP * HEAD
    column = pl.BlockSpec((1, SPAN, 1), lambda r, g: (r + low, 0, 0))
    pair = pl.BlockSpec((pieces, 1, 2, piece, lanes), lambda r, g: (0, r, 0, 0, g))

    def out(tokens):
        return pl.BlockSpec((1, tokens, lanes), lambda r, g: (r, 0, g))

    return pl.pallas_call(
        attend_kernel,
        grid=(rows, features // lanes),
        in_specs=[
            column,
            column,
            pl.BlockSpec((pieces, 1, 1, piece, lanes), lambda r, g: (0, r + low, 0, 0, g)),
            pair,
            pair,
            *[ANYWHERE] * len(after),
        ],
        out_specs=[out(SPAN), out(HALF), out(HALF)],
        out_shape=[jax.ShapeDtypeStruct((rows, tokens, features), jnp.bfloat16) for tokens in (SPAN, HALF, HALF)],
        scratch_shapes=[pltpu.VMEM((2, HALF, SPAN + HALF), jnp.float32)],
        compiler_params=PARAMS,
        cost_estimate=cost(rows * 10**10, rows * 4 * 2**20),
        name="attend",
    )(first, end, q, own, before, *after)


def mirror_kernel(source_ref, own_ref, before_ref, after_ref, out_ref):
    source = source_ref[0]
    out = dot(one_hot(source, SPAN, SPAN), own_ref[0])
    out = out + dot(one_hot(source - SPAN, SPAN, HALF), before_ref[0])
    out = out + dot(one_hot(source - SPAN - HALF, SPAN, HALF), after_ref[0])
    out_ref[0] = out.astype(jnp.bfloat16)


def mirrored(source, own, before, after, low):
    rows, _, features = own.shape

    def block(tokens):
        return pl.BlockSpec((1, tokens, features), lambda r: (r, 0, 0))

    return pl.pallas_call(
        mirror_kernel,
        grid=(rows,),
        in_specs=[pl.BlockSpec((1, SPAN, 1), lambda r: (r + low, 0, 0)), block(SPAN), block(HALF), block(HALF)],
        out_specs=block(SPAN),
        out_shape=jax.ShapeDtypeStruct(own.shape, jnp.bfloat16),
        compiler_params=PARAMS,
        cost_estimate=cost(1, 1),
        name="mirror",
    )(source, own, before, after)


def join_kernel(side_ref, mine_ref, other_ref, weight_ref, second_ref, *refs):
    out_ref = refs[-1]
    rows, tokens, depth = mine_ref.shape
    pieces, _, piece, wide = out_ref.shape
    weight = weight_ref[...].reshape(depth, wide)
    second = second_ref[...].reshape(depth, wide)
    for r in range(rows):
        total = dot(mine_ref[r], weight) + dot(other_ref[r], second)
        out_ref[:, r] = total.astype(jnp.bfloat16).reshape(pieces, piece, wide)


def join(side, mine, other, weight, pieces, after=()):
    rows, tokens, depth = mine.shape
    heads, _, head, units = weight.shape
    wide = units // 2
    whole = pl.BlockSpec((rows, tokens, depth), lambda n, side: (0, 0, 0))
    return pl.pallas_call(
        join_kernel,
        grid_spec=pltpu.PrefetchScalarGridSpec(
            num_scalar_prefetch=1,
            grid=(units // wide,),
            in_specs=[
                whole,
                whole,
                pl.BlockSpec((heads, 1, head, wide), lambda n, side: (0, side[0], 0, n)),
                pl.BlockSpec((heads, 1, head, wide), lambda n, side: (0, 1 - side[0], 0, n)),
                *[ANYWHERE] * len(after),
            ],
            out_specs=pl.BlockSpec((pieces, rows, tokens // pieces, wide), lambda n, side: (0, 0, 0, n)),
        ),
        out_shape=jax.ShapeDtypeStruct((pieces, rows, tokens // pieces, units), jnp.bfloat16),
        compiler_params=PARAMS,
        cost_estimate=cost(1, 1),
        name="join",
    )(side, mine, other, weight, weight, *after)


def body(queries, key_states, value_vectors, hypothesis_lengths, join_weight):
    _, rows, piece, width = queries.shape
    pieces = SPAN // piece
    share = width // pieces
    side = lax.axis_index("dir")
    ring = lax.axis_index("y") * 8 + lax.axis_index("z")

    def exchange(parts):
        return lax.all_to_all(parts, "x", split_axis=0, concat_axis=0, tiled=True)

    next_ring = [(c, c + 1) for c in range(RINGS - 1)]
    swap_ahead = [(RINGS + c, RINGS + c + 1) for c in range(RINGS - 1)]
    swap_back = [(RINGS + c + 1, RINGS + c) for c in range(RINGS - 1)]

    def forward(own):
        return lax.ppermute(own, ("y", "z"), next_ring)

    turned = lax.ppermute(
        join_weight.reshape(piece, -1), ("y", "x"), [(y * 4 + x, x * 4 + y) for y in range(4) for x in range(4)]
    )
    weight = lax.all_gather(turned, ("z", "y"), tiled=True)
    units = weight.shape[1]
    weight = weight.reshape(share // HEAD, 2, HEAD, units)
    first, end, source = tables(jnp.stack([ring * SPAN, side]).astype(jnp.int32), hypothesis_lengths)

    both = (key_states, value_vectors)
    own, before = [None] * 3, [None] * 3
    own[0] = exchange(pack(both, CHUNKS[0], pieces))
    before[0] = forward(own[0])
    own[1] = exchange(pack(both, CHUNKS[1], pieces, (own[0],)))
    before[1] = forward(own[1])
    q = exchange(pack((queries,), (0, rows), pieces, (own[1], before[0])))

    def contexts(i, after):
        return attend(first, end, q, own[i], before[i], CHUNKS[i][0], after)

    def swapped(i, parts):
        context, ahead, back = parts
        from_before = lax.ppermute(ahead, ("dir", "y", "z"), swap_ahead)
        from_after = lax.ppermute(back, ("dir", "y", "z"), swap_back)
        mine = mirrored(source, context, from_before, from_after, CHUNKS[i][0])
        return mine, lax.ppermute(mine, "dir", [(0, 1), (1, 0)])

    def gated(partial_value):
        total = jnp.sum(exchange(partial_value).astype(jnp.float32), axis=0)
        return (jax.nn.silu(total[..., : units // 2]) * total[..., units // 2 :]).astype(jnp.bfloat16)

    parts = [contexts(0, ())]
    own[2] = exchange(pack(both, CHUNKS[2], pieces, (q, parts[0][1])))
    before[2] = forward(own[2])
    parts.append(contexts(1, (own[2],)))
    partials = [join(side[None], *swapped(0, parts[0]), weight, pieces)]
    parts.append(contexts(2, (parts[1][1], partials[0])))
    partials.append(join(side[None], *swapped(1, parts[1]), weight, pieces))
    partials.append(join(side[None], *swapped(2, parts[2]), weight, pieces, (partials[1],)))
    joined = [gated(partial_value) for partial_value in partials]
    return jnp.concatenate(joined)


def solution(mesh):
    fine = Mesh(mesh.devices.reshape(2, 4, 8, 4), ("dir", "y", "z", "x"))
    states = P("dir", None, ("y", "z", "x"), None)
    return jax.shard_map(
        body,
        mesh=fine,
        in_specs=(states, states, states, P(), P(("y", "z", "x"), None, "dir")),
        out_specs=P(None, ("y", "z", "x"), "dir"),
        check_vma=False,
    )
```

time: 322 us -> 248 us (0.77)
  starting transfers between devices: 147 us -> 68.1 us
  waiting for transfers between devices: 52.5 us -> 89.8 us
  local copies, waits for them, and re-layouts: 51 us -> 28.3 us
  other arithmetic: 8.41 us -> 2.39 us
  Pallas kernels: 47.3 us -> 41.9 us
    ppermute x16 -> x12, starting transfers between devices: 90.9 us -> 31.9 us  [the longest x3 20.1 us: swapped(): return (mine, lax.ppermute(mine, 'dir', [(0, 1), (1, 0)]))]
    ppermute x16 -> x12, waiting for transfers between devices: 0.34 us -> 35.1 us  [the longest x3 34.7 us: forward(): return lax.ppermute(own, ('y', 'z'), next_ring)]
    another operation x29 -> x0, local copies, waits for them, and re-layouts: 25.8 us -> none  [the longest x16 18.2 us: split(): return states.reshape(piece, pieces, share).transpose(1, 0, 2)]
    all_to_all x12 -> x7, starting transfers between devices: 52.7 us -> 32.9 us  [exchange(): return lax.all_to_all(parts, 'x', split_axis=0, concat_axis=0, tiled=True)]
    unnamed x57 -> x65, local copies, waits for them, and re-layouts: 18.6 us -> 28.3 us
    all_to_all x12 -> x7, waiting for transfers between devices: 47.4 us -> 54.7 us  [exchange(): return lax.all_to_all(parts, 'x', split_axis=0, concat_axis=0, tiled=True)]
    slice x5 -> x0, local copies, waits for them, and re-layouts: 6.64 us -> none  [the longest x1 2.72 us: body(): q = exchange(split(queries[0, r]))]
    another operation x10 -> x1, other arithmetic: 5.37 us -> 0.08 us  [body(): jnp.stack([ring * SPAN, side]).astype(jnp.int32)]
  transfers between devices with their start and end apart: 30 -> 21, of which waited for: 9 -> 7; matrix products, arithmetic and copies ran while one was open for 12% -> 1% of each run, Pallas kernels for 15% -> 17%
where the time goes in v2:
time: 248 us; the launch traced here: 244 us
  waiting for transfers between devices  89.8 us (36%)
  starting transfers between devices  68.1 us (27%)
  Pallas kernels  41.9 us (17%)
  local copies, waits for them, and re-layouts  28.3 us (11%)
  between operations  13.8 us (6%)
    all_to_all x7, waiting for transfers between devices, exchange(): return lax.all_to_all(parts, 'x', split_axis=0, concat_axis=0, tiled=True)  54.7 us
    ppermute x3, waiting for transfers between devices, forward(): return lax.ppermute(own, ('y', 'z'), next_ring)  34.7 us
    all_to_all x7, starting transfers between devices, exchange(): return lax.all_to_all(parts, 'x', split_axis=0, concat_axis=0, tiled=True)  32.9 us
    unnamed x65, local copies, waits for them, and re-layouts  28.3 us
    pallas_call x3, Pallas kernels, attend(): pl.pallas_call(attend_kernel, grid=(rows, features // lanes), in_specs=[c...  27.6 us
    ppermute x3, starting transfers between devices, swapped(): return (mine, lax.ppermute(mine, 'dir', [(0, 1), (1, 0)]))  20.1 us
    pallas_call x3, Pallas kernels, join(): pl.pallas_call(join_kernel, grid_spec=pltpu.PrefetchScalarGridSpec(num_sc...  9.69 us
    ppermute x3, starting transfers between devices, forward(): return lax.ppermute(own, ('y', 'z'), next_ring)  7.66 us
  transfers between devices with their start and end apart: 21, of which 7 were waited for; matrix products, arithmetic and copies ran while one was open for 1% of the time, Pallas kernels for 17%

profile of v2, /device:TPU:8, one launch (start us, length us, event | category | flops | bytes accessed | tf_op | source)
XLA Modules:
  0.0 244.2 jit_solution(12739045285897804661)
XLA Ops:
  6.5 0.9 copy.6
  7.5 3.3 %collective-permute-start.4 = (bf16[64,1024]{1,0:T(8,128)(2,1)S(1)}, bf16[64,1024]{1,0:T(8,128)(2,1)S(1)}, u32[]{:S(2)}, u32[]{:S(2)}) collective-permute-start(bf16[64,1024]{1,0:T(8,128)(2,1)S(1)} %bitcast.16), channel_id=1, source_target_pairs={{0,0},{1,32},{2,64},{3,96},{32,1},{33,33},{34,65},{35,97},{64,2},{... | collective-permute-start | bytes 393224 | tf_op jit(solution)/shard_map/ppermute | solution.py:245
  10.8 1.6 copy-done.3
  12.3 1.6 copy-done.5
  14.0 1.0 copy-done.12
  15.0 5.9 %all-to-all-start = ((bf16[4,1,2,64,1024]{4,3,2,1,0:T(8,128)(2,1)}), bf16[4,1,2,64,1024]{4,3,2,1,0:T(8,128)(2,1)S(1)}, u32[]{:S(2)}, u32[]{:S(2)}) async-start(bf16[4,1,2,64,1024]{4,3,2,1,0:T(8,128)(2,1)} %copy-done.12), calls=%async_computation | async-start | bytes 2097152 | tf_op jit(solution)/shard_map/all_to_all | solution.py:236
  20.9 0.6 copy-done.31
  21.6 14.1 %all-to-all-done.refs_2_.own_ref = bf16[4,1,2,64,1024]{4,3,2,1,0:T(8,128)(2,1)S(1)} async-done(((bf16[4,1,2,64,1024]{4,3,2,1,0:T(8,128)(2,1)}), bf16[4,1,2,64,1024]{4,3,2,1,0:T(8,128)(2,1)S(1)}, u32[]{:S(2)}, u32[]{:S(2)}) %all-to-all-start) | async-done | bytes 1048608 | tf_op jit(solution)/shard_map/all_to_all | solution.py:236
  35.7 1.6 copy-done.6
  37.3 0.3 pack.5
  37.7 1.4 copy-done.9
  39.0 4.4 %all-to-all-start.1 = ((bf16[4,2,2,64,1024]{4,3,2,1,0:T(8,128)(2,1)}), bf16[4,2,2,64,1024]{4,3,2,1,0:T(8,128)(2,1)}, u32[]{:S(2)}, u32[]{:S(2)}) async-start(bf16[4,2,2,64,1024]{4,3,2,1,0:T(8,128)(2,1)} %copy-done.9), calls=%async_computation.1 | async-start | bytes 4194304 | tf_op jit(solution)/shard_map/all_to_all | solution.py:236
  43.5 3.8 %collective-permute-start = (bf16[4,1,2,64,1024]{4,3,2,1,0:T(8,128)(2,1)S(1)}, bf16[4,1,2,64,1024]{4,3,2,1,0:T(8,128)(2,1)S(1)}, u32[]{:S(2)}, u32[]{:S(2)}) collective-permute-start(bf16[4,1,2,64,1024]{4,3,2,1,0:T(8,128)(2,1)S(1)} %all-to-all-done.refs_2_.own_ref), channel_id=1, source_target_pairs={{0,4},{4,8},{8,12},{12,16},{16,20},{20,24},{24,28},{28,32},{32,36}... | collective-permute-start | bytes 3145736 | tf_op jit(solution)/shard_map/ppermute | solution.py:243
  47.3 29.1 %collective-permute-done.refs_2_.before_ref = bf16[4,1,2,64,1024]{4,3,2,1,0:T(8,128)(2,1)S(1)} collective-permute-done((bf16[4,1,2,64,1024]{4,3,2,1,0:T(8,128)(2,1)S(1)}, bf16[4,1,2,64,1024]{4,3,2,1,0:T(8,128)(2,1)S(1)}, u32[]{:S(2)}, u32[]{:S(2)}) %collective-permute-start) | collective-permute-done | bytes 1048608 | tf_op jit(solution)/shard_map/ppermute | solution.py:243
  76.4 1.0 copy-done.15
  77.4 1.6 copy-done.14
  79.0 1.2 copy-done.16
  80.2 0.3 pack.6
  80.6 1.4 copy-done.8
  82.0 4.6 %all-to-all-start.2 = ((bf16[4,4,1,64,1024]{4,3,2,1,0:T(8,128)(2,1)}), bf16[4,4,1,64,1024]{4,3,2,1,0:T(8,128)(2,1)}, u32[]{:S(2)}, u32[]{:S(2)}) async-start(bf16[4,4,1,64,1024]{4,3,2,1,0:T(8,128)(2,1)} %copy-done.8), calls=%async_computation.2 | async-start | bytes 4194304 | tf_op jit(solution)/shard_map/all_to_all | solution.py:236
  86.6 1.9 collective-permute-start.5
  88.6 1.4 tables.1
  90.0 0.8 copy-done.19
  90.9 0.8 copy-done.23
  91.7 20.3 %all-to-all-done.2.q_ref.refs_2_ = bf16[4,4,1,64,1024]{4,3,2,1,0:T(8,128)(2,1)} async-done(((bf16[4,4,1,64,1024]{4,3,2,1,0:T(8,128)(2,1)}), bf16[4,4,1,64,1024]{4,3,2,1,0:T(8,128)(2,1)}, u32[]{:S(2)}, u32[]{:S(2)}) %all-to-all-start.2) | async-done | bytes 2097184 | tf_op jit(solution)/shard_map/all_to_all | solution.py:236
  111.9 1.2 copy-done.11
  113.2 1.2 copy-done.17
  114.4 1.0 copy-done.20
  115.4 1.0 copy-done.24
  116.5 7.0 %attend.3 = (bf16[1,256,1024]{2,1,0:T(8,128)(2,1)S(1)}, bf16[1,128,1024]{2,1,0:T(8,128)(2,1)S(1)}, bf16[1,128,1024]{2,1,0:T(8,128)(2,1)S(1)}) custom-call(s32[4,256,1]{2,1,0:T(8,128)S(1)} %copy-done.20, s32[4,256,1]{2,1,0:T(8,128)S(1)} %copy-done.24, bf16[4,4,1,64,1024]{4,3,2,1,0:T(8,128)(2,1)} %all-to-all-done.2.q_ref.refs_2_, ...), custom_call_target="tpu_custom_call" | custom-call | flops 10000000000 | bytes 4194304 | tf_op jit(solution)/shard_map/attend/pallas_call | solution.py:145
  123.5 0.7 copy-done.29
  124.2 1.0 copy-done.13
  125.3 4.4 %all-to-all-start.4 = ((bf16[4,1,2,64,1024]{4,3,2,1,0:T(8,128)(2,1)}), bf16[4,1,2,64,1024]{4,3,2,1,0:T(8,128)(2,1)}, u32[]{:S(2)}, u32[]{:S(2)}) async-start(bf16[4,1,2,64,1024]{4,3,2,1,0:T(8,128)(2,1)} %copy-done.13), calls=%async_computation.4 | async-start | bytes 2097152 | tf_op jit(solution)/shard_map/all_to_all | solution.py:236
  129.6 0.7 collective-permute-start.1
  130.3 0.7 collective-permute-start.2
  131.0 11.8 %all-to-all-done.4.refs_0_.own_ref = bf16[4,1,2,64,1024]{4,3,2,1,0:T(8,128)(2,1)} async-done(((bf16[4,1,2,64,1024]{4,3,2,1,0:T(8,128)(2,1)}), bf16[4,1,2,64,1024]{4,3,2,1,0:T(8,128)(2,1)}, u32[]{:S(2)}, u32[]{:S(2)}) %all-to-all-start.4) | async-done | bytes 1048608 | tf_op jit(solution)/shard_map/all_to_all | solution.py:236
  142.8 1.9 collective-permute-start.9
  144.7 5.6 %collective-permute-done.5.before_ref = bf16[4,2,2,64,1024]{4,3,2,1,0:T(8,128)(2,1)} collective-permute-done((bf16[4,2,2,64,1024]{4,3,2,1,0:T(8,128)(2,1)}, bf16[4,2,2,64,1024]{4,3,2,1,0:T(8,128)(2,1)}, u32[]{:S(2)}, u32[]{:S(2)}) %collective-permute-start.5) | collective-permute-done | bytes 2097184 | tf_op jit(solution)/shard_map/ppermute | solution.py:243
  150.4 13.0 %attend.4 = (bf16[2,256,1024]{2,1,0:T(8,128)(2,1)S(1)}, bf16[2,128,1024]{2,1,0:T(8,128)(2,1)S(1)}, bf16[2,128,1024]{2,1,0:T(8,128)(2,1)S(1)}) custom-call(s32[4,256,1]{2,1,0:T(8,128)S(1)} %copy-done.21, s32[4,256,1]{2,1,0:T(8,128)S(1)} %copy-done.25, bf16[4,4,1,64,1024]{4,3,2,1,0:T(8,128)(2,1)} %all-to-all-done.2.q_ref.refs_2_, ...), custom_call_target="tpu_custom_call" | custom-call | flops 20000000000 | bytes 8388608 | tf_op jit(solution)/shard_map/attend/pallas_call | solution.py:145
  163.3 0.7 collective-permute-start.6
  164.0 0.7 collective-permute-start.7
  164.8 0.6 mirror.3.mine_ref
  165.4 4.2 %collective-permute-start.3 = (bf16[1,256,1024]{2,1,0:T(8,128)(2,1)S(1)}, bf16[1,256,1024]{2,1,0:T(8,128)(2,1)S(1)}, u32[]{:S(2)}, u32[]{:S(2)}) collective-permute-start(bf16[1,256,1024]{2,1,0:T(8,128)(2,1)S(1)} %mirror.3.mine_ref), channel_id=1, source_target_pairs={{0,128},{128,0},{1,129},{129,1},{2,130},{130,2},{3,131},{131,3},{4... | collective-permute-start | bytes 1572872 | tf_op jit(solution)/shard_map/ppermute | solution.py:269
  169.5 1.2 mirror.4.mine_ref
  170.8 10.5 %collective-permute-start.8 = (bf16[2,256,1024]{2,1,0:T(8,128)(2,1)S(1)}, bf16[2,256,1024]{2,1,0:T(8,128)(2,1)}, u32[]{:S(2)}, u32[]{:S(2)}) collective-permute-start(bf16[2,256,1024]{2,1,0:T(8,128)(2,1)S(1)} %mirror.4.mine_ref), channel_id=1, source_target_pairs={{0,128},{128,0},{1,129},{129,1},{2,130},{130,2},{3,131},{131,3},{4... | collective-permute-start | bytes 3145736 | tf_op jit(solution)/shard_map/ppermute | solution.py:269
  181.3 2.2 copy-done
  183.5 2.4 join.3.refs_1_
  185.9 4.2 %all-to-all-start.3 = ((bf16[4,1,64,1024]{3,2,1,0:T(8,128)(2,1)}), bf16[4,1,64,1024]{3,2,1,0:T(8,128)(2,1)}, u32[]{:S(2)}, u32[]{:S(2)}) async-start(bf16[4,1,64,1024]{3,2,1,0:T(8,128)(2,1)} %join.3.refs_1_), calls=%async_computation.3 | async-start | bytes 1048576 | tf_op jit(solution)/shard_map/all_to_all | solution.py:236
  190.2 1.0 copy-done.26
  191.2 1.0 copy-done.28
  192.3 7.6 %attend.5 = (bf16[1,256,1024]{2,1,0:T(8,128)(2,1)S(1)}, bf16[1,128,1024]{2,1,0:T(8,128)(2,1)}, bf16[1,128,1024]{2,1,0:T(8,128)(2,1)S(1)}) custom-call(s32[4,256,1]{2,1,0:T(8,128)S(1)} %copy-done.22, s32[4,256,1]{2,1,0:T(8,128)S(1)} %copy-done.26, bf16[4,4,1,64,1024]{4,3,2,1,0:T(8,128)(2,1)} %all-to-all-done.2.q_ref.refs_2_, ...), custom_call_target="tpu_custom_call" | custom-call | flops 10000000000 | bytes 4194304 | tf_op jit(solution)/shard_map/attend/pallas_call | solution.py:145
  199.9 0.7 collective-permute-start.10
  200.6 0.7 collective-permute-start.11
  201.3 4.8 %join.4.refs_0_ = bf16[4,2,64,1024]{3,2,1,0:T(8,128)(2,1)} custom-call(s32[1]{0:T(128)} %bitcast.side_ref, bf16[2,256,1024]{2,1,0:T(8,128)(2,1)S(1)} %mirror.4.mine_ref, bf16[2,256,1024]{2,1,0:T(8,128)(2,1)} %collective-permute-done.8.other_ref, bf16[8,2,128,1024]{3,2,1,0:T(8,128)(2,1)S(1)} %bitcast.9, bf16[8,2,128,1024]{3,2,1,0:T(8,128)(2,1)S(1)} %bitcast.10), custom_call_target="tpu_custom_call" | custom-call | flops 1 | bytes 1 | tf_op jit(solution)/shard_map/join/pallas_call | solution.py:207
  206.1 4.8 %all-to-all-start.5 = ((bf16[4,2,64,1024]{3,2,1,0:T(8,128)(2,1)}), bf16[4,2,64,1024]{3,2,1,0:T(8,128)(2,1)S(1)}, u32[]{:S(2)}, u32[]{:S(2)}) async-start(bf16[4,2,64,1024]{3,2,1,0:T(8,128)(2,1)} %join.4.refs_0_), calls=%async_computation.5 | async-start | bytes 2097152 | tf_op jit(solution)/shard_map/all_to_all | solution.py:236
  210.9 0.6 mirror.5.mine_ref
  211.5 5.5 %collective-permute-start.12 = (bf16[1,256,1024]{2,1,0:T(8,128)(2,1)S(1)}, bf16[1,256,1024]{2,1,0:T(8,128)(2,1)S(1)}, u32[]{:S(2)}, u32[]{:S(2)}) collective-permute-start(bf16[1,256,1024]{2,1,0:T(8,128)(2,1)S(1)} %mirror.5.mine_ref), channel_id=1, source_target_pairs={{0,128},{128,0},{1,129},{129,1},{2,130},{130,2},{3,131},{131,3},{4... | collective-permute-start | bytes 1572872 | tf_op jit(solution)/shard_map/ppermute | solution.py:269
  217.0 1.1 convert_reduce_fusion.2
  218.2 0.3 collective-permute-done.12.other_ref
  218.5 2.2 copy-done.2
  220.7 2.5 %join.5 = bf16[4,1,64,1024]{3,2,1,0:T(8,128)(2,1)} custom-call(s32[1]{0:T(128)} %bitcast.side_ref, bf16[1,256,1024]{2,1,0:T(8,128)(2,1)S(1)} %mirror.5.mine_ref, bf16[1,256,1024]{2,1,0:T(8,128)(2,1)S(1)} %collective-permute-done.12.other_ref, bf16[8,2,128,1024]{3,2,1,0:T(8,128)(2,1)S(1)} %bitcast.11, bf16[8,2,128,1024]{3,2,1,0:T(8,128)(2,1)S(1)} %bitcast.12, ...), custom_call_target="tpu_custom_call" | custom-call | flops 1 | bytes 1 | tf_op jit(solution)/shard_map/join/pallas_call | solution.py:207
  223.2 4.5 %all-to-all-start.6 = ((bf16[4,1,64,1024]{3,2,1,0:T(8,128)(2,1)}), bf16[4,1,64,1024]{3,2,1,0:T(8,128)(2,1)S(1)}, u32[]{:S(2)}, u32[]{:S(2)}) async-start(bf16[4,1,64,1024]{3,2,1,0:T(8,128)(2,1)} %join.5), calls=%async_computation.6 | async-start | bytes 1048576 | tf_op jit(solution)/shard_map/all_to_all | solution.py:236
  228.0 8.5 %all-to-all-done.6 = bf16[4,1,64,1024]{3,2,1,0:T(8,128)(2,1)S(1)} async-done(((bf16[4,1,64,1024]{3,2,1,0:T(8,128)(2,1)}), bf16[4,1,64,1024]{3,2,1,0:T(8,128)(2,1)S(1)}, u32[]{:S(2)}, u32[]{:S(2)}) %all-to-all-start.6) | async-done | bytes 524320 | tf_op jit(solution)/shard_map/all_to_all | solution.py:236
  236.7 0.7 pad_maximum_fusion
  (66 shorter events, 0.8 us)
Async XLA Ops:
  7.5 13.5 %collective-permute-start.4 = (bf16[64,1024]{1,0:T(8,128)(2,1)S(1)}, bf16[64,1024]{1,0:T(8,128)(2,1)S(1)}, u32[]{:S(2)}, u32[]{:S(2)}) collective-permute-start(bf16[64,1024]{1,0:T(8,128)(2,1)S(1)} %bitcast.16), channel_id=1, source_target_pairs={{0,0},{1,32},{2,64},{3,96},{32,1},{33,33},{34,65},{35,97},{64,2},{... | collective-permute-start | bytes 393224 | tf_op jit(solution)/shard_map/ppermute | solution.py:245
  10.8 1.6 copy-start.3
  12.3 1.6 copy-start.5
  14.0 1.0 copy-start.12
  15.0 20.7 %copy-start.4 = (bf16[1,4,64,4096]{3,2,1,0:T(8,128)(2,1)S(1)}, bf16[1,4,64,4096]{3,2,1,0:T(8,128)(2,1)}, u32[]{:S(2)}) copy-start(bf16[1,4,64,4096]{3,2,1,0:T(8,128)(2,1)} %refs_0_.7) | copy-start | bytes 6291460
  15.0 20.7 %all-to-all-start = ((bf16[4,1,2,64,1024]{4,3,2,1,0:T(8,128)(2,1)}), bf16[4,1,2,64,1024]{4,3,2,1,0:T(8,128)(2,1)S(1)}, u32[]{:S(2)}, u32[]{:S(2)}) async-start(bf16[4,1,2,64,1024]{4,3,2,1,0:T(8,128)(2,1)} %copy-done.12), calls=%async_computation | async-start | bytes 2097152 | tf_op jit(solution)/shard_map/all_to_all | solution.py:236
  20.9 160.4 %all-gather.2.cloned.1.call-start = ((), (), s32[]{:S(2)}) async-start(), calls=%async_computation.7 | async-start | bytes 4325376 | tf_op jit(solution)/shard_map/all_gather | solution.py:248
  20.9 0.7 copy-start.31
  35.7 1.6 copy-start.6
  37.3 6.2 %copy-start.10 = (bf16[4,1,2,64,1024]{4,3,2,1,0:T(8,128)(2,1)}, bf16[4,1,2,64,1024]{4,3,2,1,0:T(8,128)(2,1)S(1)}, u32[]{:S(2)}) copy-start(bf16[4,1,2,64,1024]{4,3,2,1,0:T(8,128)(2,1)S(1)} %all-to-all-done.refs_2_.own_ref) | copy-start | bytes 3145732
  37.6 1.4 copy-start.9
  39.0 38.4 %all-to-all-start.1 = ((bf16[4,2,2,64,1024]{4,3,2,1,0:T(8,128)(2,1)}), bf16[4,2,2,64,1024]{4,3,2,1,0:T(8,128)(2,1)}, u32[]{:S(2)}, u32[]{:S(2)}) async-start(bf16[4,2,2,64,1024]{4,3,2,1,0:T(8,128)(2,1)} %copy-done.9), calls=%async_computation.1 | async-start | bytes 4194304 | tf_op jit(solution)/shard_map/all_to_all | solution.py:236
  43.5 32.9 %collective-permute-start = (bf16[4,1,2,64,1024]{4,3,2,1,0:T(8,128)(2,1)S(1)}, bf16[4,1,2,64,1024]{4,3,2,1,0:T(8,128)(2,1)S(1)}, u32[]{:S(2)}, u32[]{:S(2)}) collective-permute-start(bf16[4,1,2,64,1024]{4,3,2,1,0:T(8,128)(2,1)S(1)} %all-to-all-done.refs_2_.own_ref), channel_id=1, source_target_pairs={{0,4},{4,8},{8,12},{12,16},{16,20},{20,24},{24,28},{28,32},{32,36}... | collective-permute-start | bytes 3145736 | tf_op jit(solution)/shard_map/ppermute | solution.py:243
  76.4 1.0 copy-start.15
  77.4 1.6 copy-start.14
  79.0 1.2 copy-start.16
  80.6 1.4 copy-start.8
  82.0 6.6 %copy-start.18 = (s32[4,512]{1,0:T(4,128)S(1)}, s32[4,512]{1,0:T(4,128)}, u32[]{:S(2)}) copy-start(s32[4,512]{1,0:T(4,128)} %lengths_ref.1) | copy-start | bytes 24580
  82.0 29.9 %all-to-all-start.2 = ((bf16[4,4,1,64,1024]{4,3,2,1,0:T(8,128)(2,1)}), bf16[4,4,1,64,1024]{4,3,2,1,0:T(8,128)(2,1)}, u32[]{:S(2)}, u32[]{:S(2)}) async-start(bf16[4,4,1,64,1024]{4,3,2,1,0:T(8,128)(2,1)} %copy-done.8), calls=%async_computation.2 | async-start | bytes 4194304 | tf_op jit(solution)/shard_map/all_to_all | solution.py:236
  86.6 63.8 %collective-permute-start.5 = (bf16[4,2,2,64,1024]{4,3,2,1,0:T(8,128)(2,1)}, bf16[4,2,2,64,1024]{4,3,2,1,0:T(8,128)(2,1)}, u32[]{:S(2)}, u32[]{:S(2)}) collective-permute-start(bf16[4,2,2,64,1024]{4,3,2,1,0:T(8,128)(2,1)} %all-to-all-done.1.refs_1_.own_ref), channel_id=1, source_target_pairs={{0,4},{4,8},{8,12},{12,16},{16,20},{20,24},{24,28},{28,32},{32,36}... | collective-permute-start | bytes 6291464 | tf_op jit(solution)/shard_map/ppermute | solution.py:243
  90.0 0.8 copy-start.19
  90.9 0.8 copy-start.23
  111.9 1.2 copy-start.11
  113.2 1.2 copy-start.17
  114.4 1.0 copy-start.20
  115.4 1.0 copy-start.24
  116.5 7.7 %copy-start.7 = (bf16[1,4,64,4096]{3,2,1,0:T(8,128)(2,1)S(1)}, bf16[1,4,64,4096]{3,2,1,0:T(8,128)(2,1)}, u32[]{:S(2)}) copy-start(bf16[1,4,64,4096]{3,2,1,0:T(8,128)(2,1)} %refs_1_.5) | copy-start | bytes 6291460
  123.4 0.7 copy-start.29
  124.2 1.0 copy-start.13
  125.3 5.1 %copy-start.30 = (bf16[1,128,1024]{2,1,0:T(8,128)(2,1)S(1)}, bf16[1,128,1024]{2,1,0:T(8,128)(2,1)}, u32[]{:S(2)}) copy-start(bf16[1,128,1024]{2,1,0:T(8,128)(2,1)} %copy-done.29) | copy-start | bytes 786436
  125.3 25.1 %copy-start.21 = (s32[4,256,1]{2,1,0:T(8,128)S(1)}, s32[4,256,1]{2,1,0:T(8,128)}, u32[]{:S(2)}) copy-start(s32[4,256,1]{2,1,0:T(8,128)} %copy-done.19) | copy-start | bytes 12292
  125.3 25.1 %copy-start.25 = (s32[4,256,1]{2,1,0:T(8,128)S(1)}, s32[4,256,1]{2,1,0:T(8,128)}, u32[]{:S(2)}) copy-start(s32[4,256,1]{2,1,0:T(8,128)} %copy-done.23) | copy-start | bytes 12292
  125.3 17.5 %all-to-all-start.4 = ((bf16[4,1,2,64,1024]{4,3,2,1,0:T(8,128)(2,1)}), bf16[4,1,2,64,1024]{4,3,2,1,0:T(8,128)(2,1)}, u32[]{:S(2)}, u32[]{:S(2)}) async-start(bf16[4,1,2,64,1024]{4,3,2,1,0:T(8,128)(2,1)} %copy-done.13), calls=%async_computation.4 | async-start | bytes 2097152 | tf_op jit(solution)/shard_map/all_to_all | solution.py:236
  129.6 35.1 %collective-permute-start.1 = (bf16[1,128,1024]{2,1,0:T(8,128)(2,1)S(1)}, bf16[1,128,1024]{2,1,0:T(8,128)(2,1)S(1)}, u32[]{:S(2)}, u32[]{:S(2)}) collective-permute-start(bf16[1,128,1024]{2,1,0:T(8,128)(2,1)S(1)} %get-tuple-element.21.refs_3_), channel_id=1, source_target_pairs={{128,132},{132,136},{136,140},{140,144},{144,148},{148,152},{152,1... | collective-permute-start | bytes 786440 | tf_op jit(solution)/shard_map/ppermute | solution.py:266
  130.3 34.4 %collective-permute-start.2 = (bf16[1,128,1024]{2,1,0:T(8,128)(2,1)S(1)}, bf16[1,128,1024]{2,1,0:T(8,128)(2,1)S(1)}, u32[]{:S(2)}, u32[]{:S(2)}) collective-permute-start(bf16[1,128,1024]{2,1,0:T(8,128)(2,1)S(1)} %copy-done.30), channel_id=1, source_target_pairs={{132,128},{136,132},{140,136},{144,140},{148,144},{152,148},{156,1... | collective-permute-start | bytes 786440 | tf_op jit(solution)/shard_map/ppermute | solution.py:267
  142.8 47.4 %collective-permute-start.9 = (bf16[4,1,2,64,1024]{4,3,2,1,0:T(8,128)(2,1)}, bf16[4,1,2,64,1024]{4,3,2,1,0:T(8,128)(2,1)}, u32[]{:S(2)}, u32[]{:S(2)}) collective-permute-start(bf16[4,1,2,64,1024]{4,3,2,1,0:T(8,128)(2,1)} %all-to-all-done.4.refs_0_.own_ref), channel_id=1, source_target_pairs={{0,4},{4,8},{8,12},{12,16},{16,20},{20,24},{24,28},{28,32},{32,36}... | collective-permute-start | bytes 3145736 | tf_op jit(solution)/shard_map/ppermute | solution.py:243
  163.3 7.5 %copy-start.27 = (bf16[2,128,1024]{2,1,0:T(8,128)(2,1)}, bf16[2,128,1024]{2,1,0:T(8,128)(2,1)S(1)}, u32[]{:S(2)}) copy-start(bf16[2,128,1024]{2,1,0:T(8,128)(2,1)S(1)} %get-tuple-element.24.refs_0_) | copy-start | bytes 1572868
  163.3 6.2 %collective-permute-start.6 = (bf16[2,128,1024]{2,1,0:T(8,128)(2,1)S(1)}, bf16[2,128,1024]{2,1,0:T(8,128)(2,1)S(1)}, u32[]{:S(2)}, u32[]{:S(2)}) collective-permute-start(bf16[2,128,1024]{2,1,0:T(8,128)(2,1)S(1)} %get-tuple-element.24.refs_0_), channel_id=1, source_target_pairs={{128,132},{132,136},{136,140},{140,144},{144,148},{148,152},{152,1... | collective-permute-start | bytes 1572872 | tf_op jit(solution)/shard_map/ppermute | solution.py:266
  164.0 5.5 %collective-permute-start.7 = (bf16[2,128,1024]{2,1,0:T(8,128)(2,1)S(1)}, bf16[2,128,1024]{2,1,0:T(8,128)(2,1)S(1)}, u32[]{:S(2)}, u32[]{:S(2)}) collective-permute-start(bf16[2,128,1024]{2,1,0:T(8,128)(2,1)S(1)} %get-tuple-element.25), channel_id=1, source_target_pairs={{132,128},{136,132},{140,136},{144,140},{148,144},{152,148},{156,1... | collective-permute-start | bytes 1572872 | tf_op jit(solution)/shard_map/ppermute | solution.py:267
  165.4 15.9 %collective-permute-start.3 = (bf16[1,256,1024]{2,1,0:T(8,128)(2,1)S(1)}, bf16[1,256,1024]{2,1,0:T(8,128)(2,1)S(1)}, u32[]{:S(2)}, u32[]{:S(2)}) collective-permute-start(bf16[1,256,1024]{2,1,0:T(8,128)(2,1)S(1)} %mirror.3.mine_ref), channel_id=1, source_target_pairs={{0,128},{128,0},{1,129},{129,1},{2,130},{130,2},{3,131},{131,3},{4... | collective-permute-start | bytes 1572872 | tf_op jit(solution)/shard_map/ppermute | solution.py:269
  170.8 30.5 %collective-permute-start.8 = (bf16[2,256,1024]{2,1,0:T(8,128)(2,1)S(1)}, bf16[2,256,1024]{2,1,0:T(8,128)(2,1)}, u32[]{:S(2)}, u32[]{:S(2)}) collective-permute-start(bf16[2,256,1024]{2,1,0:T(8,128)(2,1)S(1)} %mirror.4.mine_ref), channel_id=1, source_target_pairs={{0,128},{128,0},{1,129},{129,1},{2,130},{130,2},{3,131},{131,3},{4... | collective-permute-start | bytes 3145736 | tf_op jit(solution)/shard_map/ppermute | solution.py:269
  181.3 2.2 copy-start
  183.5 6.7 %copy-start.22 = (s32[4,256,1]{2,1,0:T(8,128)S(1)}, s32[4,256,1]{2,1,0:T(8,128)}, u32[]{:S(2)}) copy-start(s32[4,256,1]{2,1,0:T(8,128)} %copy-done.19) | copy-start | bytes 12292
  185.9 20.2 %all-to-all-start.3 = ((bf16[4,1,64,1024]{3,2,1,0:T(8,128)(2,1)}), bf16[4,1,64,1024]{3,2,1,0:T(8,128)(2,1)}, u32[]{:S(2)}, u32[]{:S(2)}) async-start(bf16[4,1,64,1024]{3,2,1,0:T(8,128)(2,1)} %join.3.refs_1_), calls=%async_computation.3 | async-start | bytes 1048576 | tf_op jit(solution)/shard_map/all_to_all | solution.py:236
  190.2 1.0 copy-start.26
  191.2 1.0 copy-start.28
  192.3 9.0 %copy-start.1 = (bf16[2048,1024]{1,0:T(8,128)(2,1)S(1)}, bf16[2048,1024]{1,0:T(8,128)(2,1)}, u32[]{:S(2)}) copy-start(bf16[2048,1024]{1,0:T(8,128)(2,1)} %all-gather.2.cloned.1.call-done) | copy-start | bytes 12582916
  199.9 11.0 %collective-permute-start.10 = (bf16[1,128,1024]{2,1,0:T(8,128)(2,1)}, bf16[1,128,1024]{2,1,0:T(8,128)(2,1)S(1)}, u32[]{:S(2)}, u32[]{:S(2)}) collective-permute-start(bf16[1,128,1024]{2,1,0:T(8,128)(2,1)} %get-tuple-element.27), channel_id=1, source_target_pairs={{128,132},{132,136},{136,140},{140,144},{144,148},{148,152},{152,1... | collective-permute-start | bytes 786440 | tf_op jit(solution)/shard_map/ppermute | solution.py:266
  200.6 10.3 %collective-permute-start.11 = (bf16[1,128,1024]{2,1,0:T(8,128)(2,1)S(1)}, bf16[1,128,1024]{2,1,0:T(8,128)(2,1)S(1)}, u32[]{:S(2)}, u32[]{:S(2)}) collective-permute-start(bf16[1,128,1024]{2,1,0:T(8,128)(2,1)S(1)} %get-tuple-element.28), channel_id=1, source_target_pairs={{132,128},{136,132},{140,136},{144,140},{148,144},{152,148},{156,1... | collective-permute-start | bytes 786440 | tf_op jit(solution)/shard_map/ppermute | solution.py:267
  206.1 17.1 %all-to-all-start.5 = ((bf16[4,2,64,1024]{3,2,1,0:T(8,128)(2,1)}), bf16[4,2,64,1024]{3,2,1,0:T(8,128)(2,1)S(1)}, u32[]{:S(2)}, u32[]{:S(2)}) async-start(bf16[4,2,64,1024]{3,2,1,0:T(8,128)(2,1)} %join.4.refs_0_), calls=%async_computation.5 | async-start | bytes 2097152 | tf_op jit(solution)/shard_map/all_to_all | solution.py:236
  211.5 7.0 %collective-permute-start.12 = (bf16[1,256,1024]{2,1,0:T(8,128)(2,1)S(1)}, bf16[1,256,1024]{2,1,0:T(8,128)(2,1)S(1)}, u32[]{:S(2)}, u32[]{:S(2)}) collective-permute-start(bf16[1,256,1024]{2,1,0:T(8,128)(2,1)S(1)} %mirror.5.mine_ref), channel_id=1, source_target_pairs={{0,128},{128,0},{1,129},{129,1},{2,130},{130,2},{3,131},{131,3},{4... | collective-permute-start | bytes 1572872 | tf_op jit(solution)/shard_map/ppermute | solution.py:269
  218.5 2.2 copy-start.2
  223.2 13.3 %all-to-all-start.6 = ((bf16[4,1,64,1024]{3,2,1,0:T(8,128)(2,1)}), bf16[4,1,64,1024]{3,2,1,0:T(8,128)(2,1)S(1)}, u32[]{:S(2)}, u32[]{:S(2)}) async-start(bf16[4,1,64,1024]{3,2,1,0:T(8,128)(2,1)} %join.5), calls=%async_computation.6 | async-start | bytes 1048576 | tf_op jit(solution)/shard_map/all_to_all | solution.py:236
Sparse Core Ops, SparseCore 0:
  24.3 92.3 all-gather.1

commit v3 on v2

v3 whole, which is shorter than its diff:
```python
import math

import jax
import jax.numpy as jnp
from jax import lax
from jax.experimental import pallas as pl
from jax.experimental.pallas import tpu as pltpu
from jax.sharding import Mesh
from jax.sharding import PartitionSpec as P

HEAD = 128
SPAN = 256
HALF = SPAN // 2
RINGS = 32
LONG = 10**10
CHUNKS = ((0, 1), (1, 3), (3, 4))
NT = (((1,), (1,)), ((), ()))
NN = (((1,), (0,)), ((), ()))
TN = (((0,), (0,)), ((), ()))
PARAMS = pltpu.CompilerParams(vmem_limit_bytes=16 * 2**20)


def dot(a, b, dims=NN):
    return lax.dot_general(a, b, dims, preferred_element_type=jnp.float32)


def cost(flops, nbytes):
    return pl.CostEstimate(flops=flops, bytes_accessed=nbytes, transcendentals=0)


def table_kernel(place_ref, lengths_ref, first_ref, here_ref, ahead_ref):
    rows, count = lengths_ref.shape
    base, side = place_ref[0], place_ref[1]
    lengths = lengths_ref[...].astype(jnp.float32)
    upto = lax.broadcasted_iota(jnp.int32, (count, count), 1) <= lax.broadcasted_iota(jnp.int32, (count, count), 0)
    before = lax.broadcasted_iota(jnp.int32, (count, count), 1) < lax.broadcasted_iota(jnp.int32, (count, count), 0)
    lengths = lengths.astype(jnp.bfloat16)
    ends = dot(jnp.where(upto, 1.0, 0.0).astype(jnp.bfloat16), lengths, NT)
    starts = dot(jnp.where(before, 1.0, 0.0).astype(jnp.bfloat16), lengths, NT)
    place = lax.broadcasted_iota(jnp.int32, (1, 2 * SPAN), 1)
    at = (place + base).astype(jnp.float32)
    for r in range(rows):
        start, stop = starts[:, r : r + 1], ends[:, r : r + 1]
        first = jnp.max(jnp.where(start <= at, start, 0.0), axis=0, keepdims=True).astype(jnp.int32) - base
        end = jnp.min(jnp.where(stop > at, stop, 1e6), axis=0, keepdims=True).astype(jnp.int32) - base
        mirror = jnp.where((first >= 0) & (first < SPAN), first + end - 1 - place, -1)
        first_ref[r] = first
        here_ref[r] = jnp.where(side == 0, place[:, SPAN:], mirror[:, :SPAN])
        ahead_ref[r] = mirror[:, SPAN:]


def tables(place, lengths):
    rows = lengths.shape[0]
    return pl.pallas_call(
        table_kernel,
        in_specs=[pl.BlockSpec(memory_space=pltpu.SMEM), pl.BlockSpec(memory_space=pltpu.VMEM)],
        out_shape=[jax.ShapeDtypeStruct((rows, 1, n), jnp.int32) for n in (2 * SPAN, SPAN, SPAN)],
        compiler_params=PARAMS,
        cost_estimate=cost(1, 1),
        name="tables",
    )(place, lengths)


def pack_kernel(count, low, *refs):
    out_ref, done = refs[-2:]
    pieces, rows, _, _, share = out_ref.shape
    copies = []
    for r in range(rows):
        for t in range(count):
            for f in range(pieces):
                part = refs[t].at[0, low + r, :, pl.ds(f * share, share)]
                copies.append(pltpu.make_async_copy(part, out_ref.at[f, r, t], done.at[len(copies)]))
    for copy in copies:
        copy.start()
    for copy in copies:
        copy.wait()


def first_tile(array):
    lead = len(array.shape) - 2
    return pl.BlockSpec((1,) * lead + (16, 128), lambda *_: (0,) * (lead + 2))


def pack(states, chunk, pieces, after=(), weight=1):
    low, high = chunk
    _, _, piece, width = states[0].shape
    share = width // pieces
    count = len(states)
    shape = (pieces, high - low, count, piece, share)
    return pl.pallas_call(
        lambda *refs: pack_kernel(count, low, *refs),
        grid=(1,),
        in_specs=[pl.BlockSpec(memory_space=pltpu.HBM)] * count + [first_tile(array) for array in after],
        out_specs=pl.BlockSpec(memory_space=pltpu.HBM),
        out_shape=pltpu.HBM(shape, jnp.bfloat16),
        scratch_shapes=[pltpu.SemaphoreType.DMA((pieces * (high - low) * count,))],
        compiler_params=PARAMS,
        cost_estimate=cost(weight, 1),
        name="pack",
    )(*[pltpu.with_memory_space_constraint(state, pltpu.HBM) for state in states], *after)


def attend_kernel(
    side_ref, first_ref, here_ref, ahead_ref, q_ref, next_q_ref, own_ref, other_ref, *refs
):
    out_ref, sent_ref, keys, values, later, contexts = refs[-6:]
    factor = math.log2(math.e) / math.sqrt(HEAD)
    features = keys.shape[1]
    low, high = slice(0, SPAN), slice(SPAN, 2 * SPAN)

    def flat(ref, index):
        return ref[:, 0, index].reshape(SPAN, features)

    @pl.when(side_ref[0] == 0)
    def _():
        keys[low], keys[high] = flat(other_ref, 0), flat(own_ref, 0)
        values[low], values[high] = flat(other_ref, 1), flat(own_ref, 1)
        later[...] = flat(q_ref, 0)

    @pl.when(side_ref[0] != 0)
    def _():
        keys[low], keys[high] = flat(own_ref, 0), flat(other_ref, 0)
        values[low], values[high] = flat(own_ref, 1), flat(other_ref, 1)
        later[...] = flat(next_q_ref, 0)

    blocks = []
    for block in range(4):
        spot = block * HALF
        at = slice(max(0, spot - SPAN), spot + HALF)
        wide = at.stop - at.start
        key = lax.broadcasted_iota(jnp.int32, (wide, HALF), 0) + at.start
        here = lax.broadcasted_iota(jnp.int32, (wide, HALF), 1) + spot
        keep = (key >= first_ref[0, :, spot : spot + HALF]) & (key <= here)
        blocks.append((spot, at, jnp.where(keep, 0.0, -1e30)))
    for spot, at, bias in blocks:
        for h in range(features // HEAD):
            lanes = slice(h * HEAD, (h + 1) * HEAD)
            if spot < SPAN:
                piece = q_ref.shape[3]
                some = slice(spot // piece, (spot + HALF) // piece)
                q = q_ref[some, 0, 0, :, lanes].reshape(HALF, HEAD)
            else:
                q = later[spot - SPAN : spot - SPAN + HALF, lanes]
            scores = dot(keys[at, lanes], q, NT) + bias
            top = jnp.max(scores, axis=0, keepdims=True)
            raised = jnp.exp2((scores - top) * factor)
            total = jnp.sum(raised, axis=0, keepdims=True)
            weights = (raised * (1.0 / total)).astype(jnp.bfloat16)
            contexts[spot : spot + HALF, lanes] = dot(weights, values[at, lanes], TN).astype(jnp.bfloat16)
    source = lax.broadcasted_iota(jnp.int32, (2 * SPAN, SPAN), 0)
    for index, ref in ((here_ref[0], out_ref), (ahead_ref[0], sent_ref)):
        chosen = jnp.where(source == index, 1.0, 0.0).astype(jnp.bfloat16)
        ref[0] = dot(chosen, contexts[...], TN).astype(jnp.bfloat16)


def attend(side, first, here, ahead, q, next_q, own, other, low, low_q, after, weight):
    pieces, rows, _, piece, features = own.shape

    def line(array):
        return pl.BlockSpec((1, 1, array.shape[2]), lambda r: (r + low, 0, 0))

    def states(array, at):
        return pl.BlockSpec((pieces, 1, array.shape[2], piece, features), lambda r: (0, r + at, 0, 0, 0))

    block = pl.BlockSpec((1, SPAN, features), lambda r: (r, 0, 0))
    return pl.pallas_call(
        attend_kernel,
        grid=(rows,),
        in_specs=[
            pl.BlockSpec(memory_space=pltpu.SMEM),
            line(first),
            line(here),
            line(ahead),
            states(q, low_q),
            states(next_q, low_q),
            states(own, 0),
            states(other, 0),
            *[first_tile(array) for array in after],
        ],
        out_specs=[block, block],
        out_shape=[jax.ShapeDtypeStruct((rows, SPAN, features), jnp.bfloat16)] * 2,
        scratch_shapes=[
            pltpu.VMEM((2 * SPAN, features), jnp.bfloat16),
            pltpu.VMEM((2 * SPAN, features), jnp.bfloat16),
            pltpu.VMEM((SPAN, features), jnp.bfloat16),
            pltpu.VMEM((2 * SPAN, features), jnp.bfloat16),
        ],
        compiler_params=pltpu.CompilerParams(vmem_limit_bytes=28 * 2**20),
        cost_estimate=cost(rows * weight, 1),
        name="attend",
    )(side, first, here, ahead, q, next_q, own, other, *after)


def join_kernel(side_ref, mine_ref, other_ref, weight_ref, second_ref, *refs):
    out_ref = refs[-1]
    rows, tokens, depth = mine_ref.shape
    pieces, _, piece, wide = out_ref.shape
    weight = weight_ref[...].reshape(depth, wide)
    second = second_ref[...].reshape(depth, wide)
    for r in range(rows):
        total = dot(mine_ref[r], weight) + dot(other_ref[r], second)
        out_ref[:, r] = total.astype(jnp.bfloat16).reshape(pieces, piece, wide)


def join(side, mine, other, weight, pieces, after=()):
    rows, tokens, depth = mine.shape
    heads, _, head, units = weight.shape
    wide = units // 2
    whole = pl.BlockSpec((rows, tokens, depth), lambda n, side: (0, 0, 0))
    return pl.pallas_call(
        join_kernel,
        grid_spec=pltpu.PrefetchScalarGridSpec(
            num_scalar_prefetch=1,
            grid=(units // wide,),
            in_specs=[
                whole,
                whole,
                pl.BlockSpec((heads, 1, head, wide), lambda n, side: (0, side[0], 0, n)),
                pl.BlockSpec((heads, 1, head, wide), lambda n, side: (0, 1 - side[0], 0, n)),
                *[first_tile(array) for array in after],
            ],
            out_specs=pl.BlockSpec((pieces, rows, tokens // pieces, wide), lambda n, side: (0, 0, 0, n)),
        ),
        out_shape=jax.ShapeDtypeStruct((pieces, rows, tokens // pieces, units), jnp.bfloat16),
        compiler_params=PARAMS,
        cost_estimate=cost(1, 1),
        name="join",
    )(side, mine, other, weight, weight, *after)


def body(queries, key_states, value_vectors, hypothesis_lengths, join_weight):
    _, rows, piece, width = queries.shape
    pieces = SPAN // piece
    share = width // pieces
    side = lax.axis_index("dir")
    ring = lax.axis_index("y") * 8 + lax.axis_index("z")

    def exchange(parts):
        return lax.all_to_all(parts, "x", split_axis=0, concat_axis=0, tiled=True)

    to_left = [(RINGS + c + 1, RINGS + c) for c in range(RINGS - 1)]
    to_right = [(RINGS + c, RINGS + c + 1) for c in range(RINGS - 1)]
    outward = [(c, c + 1) for c in range(RINGS - 1)] + to_left

    def passed(array, pairs):
        return lax.ppermute(array, ("dir", "y", "z"), pairs)

    turned = lax.ppermute(
        join_weight.reshape(piece, -1), ("y", "x"), [(y * 4 + x, x * 4 + y) for y in range(4) for x in range(4)]
    )
    weight = lax.all_gather(turned, ("z", "y"), tiled=True)
    units = weight.shape[1]
    weight_rows = weight.reshape(share // HEAD, 2, HEAD, units)
    base = (ring - 1 + side) * SPAN
    lines = tables(jnp.stack([base, side]).astype(jnp.int32), hypothesis_lengths)

    both = (key_states, value_vectors)
    own, other = [None] * 3, [None] * 3
    own[0] = exchange(pack(both, CHUNKS[0], pieces))
    other[0] = passed(own[0], outward)
    q_most = exchange(pack((queries,), (0, 3), pieces, (own[0], turned)))
    next_most = passed(q_most, to_left)
    own[1] = exchange(pack(both, CHUNKS[1], pieces, (q_most, other[0])))
    other[1] = passed(own[1], outward)
    own[2] = exchange(pack(both, CHUNKS[2], pieces, (own[1], next_most)))
    other[2] = passed(own[2], outward)

    def contexts(i, q, next_q, low_q, after=(), weight=LONG):
        low = CHUNKS[i][0]
        return attend(side[None], *lines, q, next_q, own[i], other[i], low, low_q, after, weight)

    def swapped(mine, ahead):
        mine = mine + passed(ahead, to_right)
        return mine, lax.ppermute(mine, "dir", [(0, 1), (1, 0)])

    def joined_part(mine, partner, after=()):
        return join(side[None], mine, partner, weight_rows, pieces, after)

    def gated(arrived):
        total = jnp.sum(arrived.astype(jnp.float32), axis=0)
        return (jax.nn.silu(total[..., : units // 2]) * total[..., units // 2 :]).astype(jnp.bfloat16)

    first_part = contexts(0, q_most, next_most, CHUNKS[0][0])
    q_last = exchange(pack((queries,), (3, 4), pieces, (own[2], first_part[1])))
    next_last = passed(q_last, to_left)
    first_part = swapped(*first_part)
    second_part = contexts(1, q_most, next_most, CHUNKS[1][0], (q_last, first_part[0]))
    third_part = contexts(2, q_last, next_last, 0, (second_part[1], first_part[1]))
    arrived = [exchange(joined_part(*first_part))]
    partial_value = joined_part(*swapped(*second_part), ())
    arrived.append(exchange(partial_value))
    arrived.append(exchange(joined_part(*swapped(*third_part), (arrived[0], partial_value))))
    joined = [gated(one) for one in arrived]
    return jnp.concatenate(joined)


def solution(mesh):
    fine = Mesh(mesh.devices.reshape(2, 4, 8, 4), ("dir", "y", "z", "x"))
    states = P("dir", None, ("y", "z", "x"), None)
    return jax.shard_map(
        body,
        mesh=fine,
        in_specs=(states, states, states, P(), P(("y", "z", "x"), None, "dir")),
        out_specs=P(None, ("y", "z", "x"), "dir"),
        check_vma=False,
    )
```

time: 248 us -> 420 us (1.69)
  Pallas kernels: 41.9 us -> 236 us
  local copies, waits for them, and re-layouts: 28.3 us -> 11 us
  blocking collectives: 0 us -> 11.5 us
  waiting for transfers between devices: 89.8 us -> 78.8 us
    pallas_call x10 -> x8, Pallas kernels: 30.8 us -> 225 us  [the longest x5 199 us: pack(): pl.pallas_call(lambda *refs: pack_kernel(count, low, *refs), grid=(1,), i...]
    unnamed x65 -> x25, local copies, waits for them, and re-layouts: 28.3 us -> 11 us
    ppermute x9 -> x8, waiting for transfers between devices: 34.8 us -> 17.6 us  [passed(): return lax.ppermute(array, ('dir', 'y', 'z'), pairs)]
    ppermute x1, waiting for transfers between devices: 0.01 us -> 11.8 us  [body(): lax.ppermute(join_weight.reshape(piece, -1), ('y', 'x'), [(y * 4 + x, x *...]
    all_to_all x0 -> x1, blocking collectives: none -> 11.5 us  [exchange(): return lax.all_to_all(parts, 'x', split_axis=0, concat_axis=0, tiled=True)]
    all_to_all x7, waiting for transfers between devices: 54.7 us -> 49.4 us  [exchange(): return lax.all_to_all(parts, 'x', split_axis=0, concat_axis=0, tiled=True)]
    ppermute x3, starting transfers between devices: 20.1 us -> 15.4 us  [swapped(): return (mine, lax.ppermute(mine, 'dir', [(0, 1), (1, 0)]))]
    ppermute x9 -> x8, starting transfers between devices: 11.7 us -> 12.6 us  [passed(): return lax.ppermute(array, ('dir', 'y', 'z'), pairs)]
  transfers between devices with their start and end apart: 21 -> 20, of which waited for: 7 -> 7; matrix products, arithmetic and copies ran while one was open for 1% -> 1% of each run, Pallas kernels for 17% -> 36%
where the time goes in v3:
time: 420 us; the launch traced here: 419 us
  Pallas kernels  236 us (56%)
  waiting for transfers between devices  78.8 us (19%)
  starting transfers between devices  64.4 us (15%)
  between operations  13.8 us (3%)
  blocking collectives  11.5 us (3%)
  local copies, waits for them, and re-layouts  11 us (3%)
    pallas_call x5, Pallas kernels, pack(): pl.pallas_call(lambda *refs: pack_kernel(count, low, *refs), grid=(1,), i...  199 us
    all_to_all x7, waiting for transfers between devices, exchange(): return lax.all_to_all(parts, 'x', split_axis=0, concat_axis=0, tiled=True)  49.4 us
    all_to_all x7, starting transfers between devices, exchange(): return lax.all_to_all(parts, 'x', split_axis=0, concat_axis=0, tiled=True)  31.7 us
    pallas_call x3, Pallas kernels, attend(): pl.pallas_call(attend_kernel, grid=(rows,), in_specs=[pl.BlockSpec(memory...  26 us
    ppermute x8, waiting for transfers between devices, passed(): return lax.ppermute(array, ('dir', 'y', 'z'), pairs)  17.6 us
    ppermute x3, starting transfers between devices, swapped(): return (mine, lax.ppermute(mine, 'dir', [(0, 1), (1, 0)]))  15.4 us
    ppermute x8, starting transfers between devices, passed(): return lax.ppermute(array, ('dir', 'y', 'z'), pairs)  12.6 us
    ppermute x1, waiting for transfers between devices, body(): lax.ppermute(join_weight.reshape(piece, -1), ('y', 'x'), [(y * 4 + x, x *...  11.8 us
  transfers between devices with their start and end apart: 20, of which 7 were waited for; matrix products, arithmetic and copies ran while one was open for 1% of the time, Pallas kernels for 36%

profile of v3, /device:TPU:8, one launch (start us, length us, event | category | flops | bytes accessed | tf_op | source)
XLA Modules:
  0.0 418.9 jit_solution(623543874849913177)
XLA Ops:
  6.5 32.9 %pack.5 = bf16[4,1,2,64,1024]{4,3,2,1,0:T(8,128)(2,1)} custom-call(bf16[1,4,64,4096]{3,2,1,0:T(8,128)(2,1)} %refs_0_.8, bf16[1,4,64,4096]{3,2,1,0:T(8,128)(2,1)} %refs_1_.5), custom_call_target="tpu_custom_call" | custom-call | flops 1 | bytes 1 | tf_op jit(solution)/shard_map/pack/pallas_call | solution.py:90
  39.5 0.0 copy-start.11
  39.5 4.4 %all-to-all-start = ((bf16[4,1,2,64,1024]{4,3,2,1,0:T(8,128)(2,1)}), bf16[4,1,2,64,1024]{4,3,2,1,0:T(8,128)(2,1)S(1)}, u32[]{:S(2)}, u32[]{:S(2)}) async-start(bf16[4,1,2,64,1024]{4,3,2,1,0:T(8,128)(2,1)} %pack.5), calls=%async_computation | async-start | bytes 2097152 | tf_op jit(solution)/shard_map/all_to_all | solution.py:239
  43.9 4.7 %collective-permute-start = (bf16[64,1024]{1,0:T(8,128)(2,1)S(1)}, bf16[64,1024]{1,0:T(8,128)(2,1)S(1)}, u32[]{:S(2)}, u32[]{:S(2)}) collective-permute-start(bf16[64,1024]{1,0:T(8,128)(2,1)S(1)} %bitcast.16), channel_id=1, source_target_pairs={{0,0},{1,32},{2,64},{3,96},{32,1},{33,33},{34,65},{35,97},{64,2},{... | collective-permute-start | bytes 393224 | tf_op jit(solution)/shard_map/ppermute | solution.py:248
  48.7 11.8 %collective-permute-done.refs_2_ = bf16[64,1024]{1,0:T(8,128)(2,1)S(1)} collective-permute-done((bf16[64,1024]{1,0:T(8,128)(2,1)S(1)}, bf16[64,1024]{1,0:T(8,128)(2,1)S(1)}, u32[]{:S(2)}, u32[]{:S(2)}) %collective-permute-start) | collective-permute-done | bytes 131104 | tf_op jit(solution)/shard_map/ppermute | solution.py:248
  60.5 0.0 all-to-all-done.refs_1_.own_ref
  60.5 48.9 %pack.6 = bf16[4,3,1,64,1024]{4,3,2,1,0:T(8,128)(2,1)} custom-call(bf16[1,4,64,4096]{3,2,1,0:T(8,128)(2,1)} %refs_0_.9, bf16[4,1,2,64,1024]{4,3,2,1,0:T(8,128)(2,1)S(1)} %all-to-all-done.refs_1_.own_ref, bf16[64,1024]{1,0:T(8,128)(2,1)S(1)} %collective-permute-done.refs_2_), custom_call_target="tpu_custom_call" | custom-call | flops 1 | bytes 1 | tf_op jit(solution)/shard_map/pack/pallas_call | solution.py:90
  109.4 7.0 %all-to-all-start.1 = ((bf16[4,3,1,64,1024]{4,3,2,1,0:T(8,128)(2,1)}), bf16[4,3,1,64,1024]{4,3,2,1,0:T(8,128)(2,1)S(1)}, u32[]{:S(2)}, u32[]{:S(2)}) async-start(bf16[4,3,1,64,1024]{4,3,2,1,0:T(8,128)(2,1)} %pack.6), calls=%async_computation.1 | async-start | bytes 3145728 | tf_op jit(solution)/shard_map/all_to_all | solution.py:239
  116.4 3.8 collective-permute-start.2
  120.2 0.0 all-gather.2.cloned.1.call-update
  120.2 17.6 %collective-permute-done.2.other_ref.refs_3_ = bf16[4,1,2,64,1024]{4,3,2,1,0:T(8,128)(2,1)} collective-permute-done((bf16[4,1,2,64,1024]{4,3,2,1,0:T(8,128)(2,1)S(1)}, bf16[4,1,2,64,1024]{4,3,2,1,0:T(8,128)(2,1)}, u32[]{:S(2)}, u32[]{:S(2)}) %collective-permute-start.2) | collective-permute-done | bytes 1048608 | tf_op jit(solution)/shard_map/ppermute | solution.py:246
  137.8 0.0 all-to-all-done.1.q_ref.refs_2_
  137.8 65.5 %pack.7 = bf16[4,2,2,64,1024]{4,3,2,1,0:T(8,128)(2,1)} custom-call(bf16[1,4,64,4096]{3,2,1,0:T(8,128)(2,1)} %refs_0_.8, bf16[1,4,64,4096]{3,2,1,0:T(8,128)(2,1)} %refs_1_.5, bf16[4,3,1,64,1024]{4,3,2,1,0:T(8,128)(2,1)S(1)} %all-to-all-done.1.q_ref.refs_2_, bf16[4,1,2,64,1024]{4,3,2,1,0:T(8,128)(2,1)} %collective-permute-done.2.other_ref.refs_3_), custom_call_target="tpu_custom_call" | custom-call | flops 1 | bytes 1 | tf_op jit(solution)/shard_map/pack/pallas_call | solution.py:90
  203.3 0.0 copy-start.9
  203.3 4.8 %all-to-all-start.3 = ((bf16[4,2,2,64,1024]{4,3,2,1,0:T(8,128)(2,1)}), bf16[4,2,2,64,1024]{4,3,2,1,0:T(8,128)(2,1)S(1)}, u32[]{:S(2)}, u32[]{:S(2)}) async-start(bf16[4,2,2,64,1024]{4,3,2,1,0:T(8,128)(2,1)} %pack.7), calls=%async_computation.3 | async-start | bytes 4194304 | tf_op jit(solution)/shard_map/all_to_all | solution.py:239
  208.2 1.9 collective-permute-start.1
  210.0 21.5 %all-to-all-done.3.refs_2_.own_ref = bf16[4,2,2,64,1024]{4,3,2,1,0:T(8,128)(2,1)S(1)} async-done(((bf16[4,2,2,64,1024]{4,3,2,1,0:T(8,128)(2,1)}), bf16[4,2,2,64,1024]{4,3,2,1,0:T(8,128)(2,1)S(1)}, u32[]{:S(2)}, u32[]{:S(2)}) %all-to-all-start.3) | async-done | bytes 2097184 | tf_op jit(solution)/shard_map/all_to_all | solution.py:239
  231.5 1.9 collective-permute-start.5
  233.5 0.1 pad_add_fusion.place_ref
  233.5 1.8 tables.1
  235.3 0.0 collective-permute-done.1.next_q_ref.refs_3_
  235.3 33.6 %pack.8 = bf16[4,1,2,64,1024]{4,3,2,1,0:T(8,128)(2,1)} custom-call(bf16[1,4,64,4096]{3,2,1,0:T(8,128)(2,1)} %refs_0_.8, bf16[1,4,64,4096]{3,2,1,0:T(8,128)(2,1)} %refs_1_.5, bf16[4,2,2,64,1024]{4,3,2,1,0:T(8,128)(2,1)S(1)} %all-to-all-done.3.refs_2_.own_ref, bf16[4,3,1,64,1024]{4,3,2,1,0:T(8,128)(2,1)} %collective-permute-done.1.next_q_ref.refs_3_), custom_call_target="tpu_custom_call" | custom-call | flops 1 | bytes 1 | tf_op jit(solution)/shard_map/pack/pallas_call | solution.py:90
  268.9 4.3 %all-to-all-start.4 = ((bf16[4,1,2,64,1024]{4,3,2,1,0:T(8,128)(2,1)}), bf16[4,1,2,64,1024]{4,3,2,1,0:T(8,128)(2,1)}, u32[]{:S(2)}, u32[]{:S(2)}) async-start(bf16[4,1,2,64,1024]{4,3,2,1,0:T(8,128)(2,1)} %pack.8), calls=%async_computation.4 | async-start | bytes 2097152 | tf_op jit(solution)/shard_map/all_to_all | solution.py:239
  273.2 1.4 copy-done.4
  274.6 7.4 %attend.3 = (bf16[1,256,1024]{2,1,0:T(8,128)(2,1)S(1)}, bf16[1,256,1024]{2,1,0:T(8,128)(2,1)}) custom-call(s32[1]{0:T(128)} %bitcast.side_ref, s32[4,1,512]{2,1,0:T(1,128)S(1)} %get-tuple-element.14.first_ref, s32[4,1,256]{2,1,0:T(1,128)S(1)} %get-tuple-element.15.here_ref, s32[4,1,256]{2,1,0:T(1,128)S(1)} %get-tuple-element.16.ahead_ref, ...), custom_call_target="tpu_custom_call" | custom-call | flops 10000000000 | bytes 1 | tf_op jit(solution)/shard_map/attend/pallas_call | solution.py:166
  282.0 0.8 copy-done.6
  282.8 0.8 collective-permute-start.3
  283.6 5.7 %all-to-all-done.4.refs_1_.own_ref = bf16[4,1,2,64,1024]{4,3,2,1,0:T(8,128)(2,1)} async-done(((bf16[4,1,2,64,1024]{4,3,2,1,0:T(8,128)(2,1)}), bf16[4,1,2,64,1024]{4,3,2,1,0:T(8,128)(2,1)}, u32[]{:S(2)}, u32[]{:S(2)}) %all-to-all-start.4) | async-done | bytes 1048608 | tf_op jit(solution)/shard_map/all_to_all | solution.py:239
  289.3 17.7 %pack.9 = bf16[4,1,1,64,1024]{4,3,2,1,0:T(8,128)(2,1)} custom-call(bf16[1,4,64,4096]{3,2,1,0:T(8,128)(2,1)} %refs_0_.9, bf16[4,1,2,64,1024]{4,3,2,1,0:T(8,128)(2,1)} %all-to-all-done.4.refs_1_.own_ref, bf16[1,256,1024]{2,1,0:T(8,128)(2,1)} %get-tuple-element.18.refs_2_), custom_call_target="tpu_custom_call" | custom-call | flops 1 | bytes 1 | tf_op jit(solution)/shard_map/pack/pallas_call | solution.py:90
  307.1 4.2 all-to-all-start.5
  311.2 0.8 copy-done.10
  312.0 1.2 add.29.mine_ref.refs_1_
  313.3 0.3 collective-permute-start.4
  313.6 1.9 collective-permute-start.9
  315.5 5.9 %all-to-all-done.5.refs_0_.q_ref = bf16[4,1,1,64,1024]{4,3,2,1,0:T(8,128)(2,1)} async-done(((bf16[4,1,1,64,1024]{4,3,2,1,0:T(8,128)(2,1)}), bf16[4,1,1,64,1024]{4,3,2,1,0:T(8,128)(2,1)}, u32[]{:S(2)}, u32[]{:S(2)}) %all-to-all-start.5) | async-done | bytes 524320 | tf_op jit(solution)/shard_map/all_to_all | solution.py:239
  321.4 0.7 collective-permute-start.8
  322.2 1.4 copy-done.5
  323.6 11.8 %attend.4 = (bf16[2,256,1024]{2,1,0:T(8,128)(2,1)S(1)}, bf16[2,256,1024]{2,1,0:T(8,128)(2,1)S(1)}) custom-call(s32[1]{0:T(128)} %bitcast.side_ref, s32[4,1,512]{2,1,0:T(1,128)S(1)} %get-tuple-element.14.first_ref, s32[4,1,256]{2,1,0:T(1,128)S(1)} %get-tuple-element.15.here_ref, s32[4,1,256]{2,1,0:T(1,128)S(1)} %get-tuple-element.16.ahead_ref, ...), custom_call_target="tpu_custom_call" | custom-call | flops 20000000000 | bytes 1 | tf_op jit(solution)/shard_map/attend/pallas_call | solution.py:166
  335.4 0.9 collective-permute-start.6
  336.3 0.0 collective-permute-done.4.other_ref.refs_1_
  336.3 0.0 collective-permute-done.8.next_q_ref
  336.3 6.8 %attend.5 = (bf16[1,256,1024]{2,1,0:T(8,128)(2,1)S(1)}, bf16[1,256,1024]{2,1,0:T(8,128)(2,1)S(1)}) custom-call(s32[1]{0:T(128)} %bitcast.side_ref, s32[4,1,512]{2,1,0:T(1,128)S(1)} %get-tuple-element.14.first_ref, s32[4,1,256]{2,1,0:T(1,128)S(1)} %get-tuple-element.15.here_ref, s32[4,1,256]{2,1,0:T(1,128)S(1)} %get-tuple-element.16.ahead_ref, ...), custom_call_target="tpu_custom_call" | custom-call | flops 10000000000 | bytes 1 | tf_op jit(solution)/shard_map/attend/pallas_call | solution.py:166
  343.1 0.7 collective-permute-start.10
  343.9 0.4 add.31.mine_ref
  344.3 9.9 %collective-permute-start.7 = (bf16[2,256,1024]{2,1,0:T(8,128)(2,1)S(1)}, bf16[2,256,1024]{2,1,0:T(8,128)(2,1)}, u32[]{:S(2)}, u32[]{:S(2)}) collective-permute-start(bf16[2,256,1024]{2,1,0:T(8,128)(2,1)S(1)} %add.31.mine_ref), channel_id=1, source_target_pairs={{0,128},{128,0},{1,129},{129,1},{2,130},{130,2},{3,131},{131,3},{4... | collective-permute-start | bytes 3145736 | tf_op jit(solution)/shard_map/ppermute | solution.py:274
  354.1 0.0 collective-permute-done.10
  354.2 0.2 add.33.mine_ref
  354.4 5.2 %collective-permute-start.11 = (bf16[1,256,1024]{2,1,0:T(8,128)(2,1)S(1)}, bf16[1,256,1024]{2,1,0:T(8,128)(2,1)}, u32[]{:S(2)}, u32[]{:S(2)}) collective-permute-start(bf16[1,256,1024]{2,1,0:T(8,128)(2,1)S(1)} %add.33.mine_ref), channel_id=1, source_target_pairs={{0,128},{128,0},{1,129},{129,1},{2,130},{130,2},{3,131},{131,3},{4... | collective-permute-start | bytes 1572872 | tf_op jit(solution)/shard_map/ppermute | solution.py:274
  359.6 2.2 copy-done
  361.8 2.5 join.3
  364.2 3.5 all-to-all-start.2
  367.7 2.2 copy-done.1
  369.9 4.7 %join.4.refs_1_ = bf16[4,2,64,1024]{3,2,1,0:T(8,128)(2,1)} custom-call(s32[1]{0:T(128)} %bitcast.side_ref, bf16[2,256,1024]{2,1,0:T(8,128)(2,1)S(1)} %add.31.mine_ref, bf16[2,256,1024]{2,1,0:T(8,128)(2,1)} %collective-permute-done.7.other_ref, bf16[8,2,128,1024]{3,2,1,0:T(8,128)(2,1)S(1)} %bitcast.9, bf16[8,2,128,1024]{3,2,1,0:T(8,128)(2,1)S(1)} %bitcast.10), custom_call_target="tpu_custom_call" | custom-call | flops 1 | bytes 1 | tf_op jit(solution)/shard_map/join/pallas_call | solution.py:210
  374.6 3.0 all-to-all-done.2.refs_0_
  377.6 2.2 copy-done.2
  379.8 2.7 join.5
  382.5 11.5 %all_to_all.40 = bf16[4,1,64,1024]{3,2,1,0:T(8,128)(2,1)S(1)} all-to-all(bf16[4,1,64,1024]{3,2,1,0:T(8,128)(2,1)S(1)} %join.5), channel_id=1, replica_groups=mesh['dir'=2,'y'=4,'z'=8,'x'=4] {'x'}, dimensions={0} | all-to-all | bytes 1048576 | tf_op jit(solution)/shard_map/all_to_all | solution.py:239
  394.0 3.5 all-to-all-start.6
  397.5 0.1 convert_reduce_fusion.2
  397.7 0.1 convert_reduce_fusion.1
  397.8 13.2 %all-to-all-done.6 = bf16[4,2,64,1024]{3,2,1,0:T(8,128)(2,1)S(1)} async-done(((bf16[4,2,64,1024]{3,2,1,0:T(8,128)(2,1)}), bf16[4,2,64,1024]{3,2,1,0:T(8,128)(2,1)S(1)}, u32[]{:S(2)}, u32[]{:S(2)}) %all-to-all-start.6) | async-done | bytes 1048608 | tf_op jit(solution)/shard_map/all_to_all | solution.py:239
  411.0 0.2 convert_reduce_fusion
  411.2 0.1 fusion
  411.3 0.7 pad_maximum_fusion
  (26 shorter events, 0.2 us)
Async XLA Ops:
  39.5 4.5 %copy-start.11 = (bf16[64,2,512]{2,1,0:T(2,128)(2,1)S(1)}, bf16[64,2,512]{2,1,0:T(2,128)(2,1)}, u32[]{:S(2)}) copy-start(bf16[64,2,512]{2,1,0:T(2,128)(2,1)} %param.9) | copy-start | bytes 393220
  39.5 21.0 %all-to-all-start = ((bf16[4,1,2,64,1024]{4,3,2,1,0:T(8,128)(2,1)}), bf16[4,1,2,64,1024]{4,3,2,1,0:T(8,128)(2,1)S(1)}, u32[]{:S(2)}, u32[]{:S(2)}) async-start(bf16[4,1,2,64,1024]{4,3,2,1,0:T(8,128)(2,1)} %pack.5), calls=%async_computation | async-start | bytes 2097152 | tf_op jit(solution)/shard_map/all_to_all | solution.py:239
  43.9 16.6 %collective-permute-start = (bf16[64,1024]{1,0:T(8,128)(2,1)S(1)}, bf16[64,1024]{1,0:T(8,128)(2,1)S(1)}, u32[]{:S(2)}, u32[]{:S(2)}) collective-permute-start(bf16[64,1024]{1,0:T(8,128)(2,1)S(1)} %bitcast.16), channel_id=1, source_target_pairs={{0,0},{1,32},{2,64},{3,96},{32,1},{33,33},{34,65},{35,97},{64,2},{... | collective-permute-start | bytes 393224 | tf_op jit(solution)/shard_map/ppermute | solution.py:248
  60.5 48.9 %copy-start.8 = (bf16[64,1024]{1,0:T(8,128)(2,1)}, bf16[64,1024]{1,0:T(8,128)(2,1)S(1)}, u32[]{:S(2)}) copy-start(bf16[64,1024]{1,0:T(8,128)(2,1)S(1)} %collective-permute-done.refs_2_) | copy-start | bytes 393220
  109.4 28.4 %all-to-all-start.1 = ((bf16[4,3,1,64,1024]{4,3,2,1,0:T(8,128)(2,1)}), bf16[4,3,1,64,1024]{4,3,2,1,0:T(8,128)(2,1)S(1)}, u32[]{:S(2)}, u32[]{:S(2)}) async-start(bf16[4,3,1,64,1024]{4,3,2,1,0:T(8,128)(2,1)} %pack.6), calls=%async_computation.1 | async-start | bytes 3145728 | tf_op jit(solution)/shard_map/all_to_all | solution.py:239
  116.4 243.2 %all-gather.2.cloned.1.call-start = ((), (), s32[]{:S(2)}) async-start(), calls=%async_computation.8 | async-start | bytes 4325376 | tf_op jit(solution)/shard_map/all_gather | solution.py:251
  116.4 21.5 %collective-permute-start.2 = (bf16[4,1,2,64,1024]{4,3,2,1,0:T(8,128)(2,1)S(1)}, bf16[4,1,2,64,1024]{4,3,2,1,0:T(8,128)(2,1)}, u32[]{:S(2)}, u32[]{:S(2)}) collective-permute-start(bf16[4,1,2,64,1024]{4,3,2,1,0:T(8,128)(2,1)S(1)} %all-to-all-done.refs_1_.own_ref), channel_id=1, source_target_pairs={{0,4},{4,8},{8,12},{12,16},{16,20},{20,24},{24,28},{28,32},{32,36}... | collective-permute-start | bytes 3145736 | tf_op jit(solution)/shard_map/ppermute | solution.py:246
  137.8 65.5 %copy-start.3 = (bf16[4,3,1,64,1024]{4,3,2,1,0:T(8,128)(2,1)}, bf16[4,3,1,64,1024]{4,3,2,1,0:T(8,128)(2,1)S(1)}, u32[]{:S(2)}) copy-start(bf16[4,3,1,64,1024]{4,3,2,1,0:T(8,128)(2,1)S(1)} %all-to-all-done.1.q_ref.refs_2_) | copy-start | bytes 4718596
  203.3 30.2 %copy-start.9 = (s32[4,512]{1,0:T(4,128)S(1)}, s32[4,512]{1,0:T(4,128)}, u32[]{:S(2)}) copy-start(s32[4,512]{1,0:T(4,128)} %lengths_ref.1) | copy-start | bytes 24580
  203.3 28.2 %all-to-all-start.3 = ((bf16[4,2,2,64,1024]{4,3,2,1,0:T(8,128)(2,1)}), bf16[4,2,2,64,1024]{4,3,2,1,0:T(8,128)(2,1)S(1)}, u32[]{:S(2)}, u32[]{:S(2)}) async-start(bf16[4,2,2,64,1024]{4,3,2,1,0:T(8,128)(2,1)} %pack.7), calls=%async_computation.3 | async-start | bytes 4194304 | tf_op jit(solution)/shard_map/all_to_all | solution.py:239
  208.2 27.1 %collective-permute-start.1 = (bf16[4,3,1,64,1024]{4,3,2,1,0:T(8,128)(2,1)}, bf16[4,3,1,64,1024]{4,3,2,1,0:T(8,128)(2,1)}, u32[]{:S(2)}, u32[]{:S(2)}) collective-permute-start(bf16[4,3,1,64,1024]{4,3,2,1,0:T(8,128)(2,1)} %copy-done.3), channel_id=1, source_target_pairs={{132,128},{136,132},{140,136},{144,140},{148,144},{152,148},{156,1... | collective-permute-start | bytes 4718600 | tf_op jit(solution)/shard_map/ppermute | solution.py:246
  231.5 90.6 %collective-permute-start.5 = (bf16[4,2,2,64,1024]{4,3,2,1,0:T(8,128)(2,1)S(1)}, bf16[4,2,2,64,1024]{4,3,2,1,0:T(8,128)(2,1)}, u32[]{:S(2)}, u32[]{:S(2)}) collective-permute-start(bf16[4,2,2,64,1024]{4,3,2,1,0:T(8,128)(2,1)S(1)} %all-to-all-done.3.refs_2_.own_ref), channel_id=1, source_target_pairs={{0,4},{4,8},{8,12},{12,16},{16,20},{20,24},{24,28},{28,32},{32,36}... | collective-permute-start | bytes 6291464 | tf_op jit(solution)/shard_map/ppermute | solution.py:246
  268.9 20.4 %all-to-all-start.4 = ((bf16[4,1,2,64,1024]{4,3,2,1,0:T(8,128)(2,1)}), bf16[4,1,2,64,1024]{4,3,2,1,0:T(8,128)(2,1)}, u32[]{:S(2)}, u32[]{:S(2)}) async-start(bf16[4,1,2,64,1024]{4,3,2,1,0:T(8,128)(2,1)} %pack.8), calls=%async_computation.4 | async-start | bytes 2097152 | tf_op jit(solution)/shard_map/all_to_all | solution.py:239
  273.2 1.4 copy-start.4
  282.0 0.8 copy-start.6
  282.8 29.2 %copy-start.7 = (bf16[1,256,1024]{2,1,0:T(8,128)(2,1)S(1)}, bf16[1,256,1024]{2,1,0:T(8,128)(2,1)}, u32[]{:S(2)}) copy-start(bf16[1,256,1024]{2,1,0:T(8,128)(2,1)} %copy-done.6) | copy-start | bytes 1572868
  282.8 28.4 %collective-permute-start.3 = (bf16[1,256,1024]{2,1,0:T(8,128)(2,1)}, bf16[1,256,1024]{2,1,0:T(8,128)(2,1)S(1)}, u32[]{:S(2)}, u32[]{:S(2)}) collective-permute-start(bf16[1,256,1024]{2,1,0:T(8,128)(2,1)} %get-tuple-element.18.refs_2_), channel_id=1, source_target_pairs={{128,132},{132,136},{136,140},{140,144},{144,148},{148,152},{152,1... | collective-permute-start | bytes 1572872 | tf_op jit(solution)/shard_map/ppermute | solution.py:246
  307.1 14.4 %all-to-all-start.5 = ((bf16[4,1,1,64,1024]{4,3,2,1,0:T(8,128)(2,1)}), bf16[4,1,1,64,1024]{4,3,2,1,0:T(8,128)(2,1)}, u32[]{:S(2)}, u32[]{:S(2)}) async-start(bf16[4,1,1,64,1024]{4,3,2,1,0:T(8,128)(2,1)} %pack.9), calls=%async_computation.5 | async-start | bytes 1048576 | tf_op jit(solution)/shard_map/all_to_all | solution.py:239
  311.2 0.8 copy-start.10
  313.3 23.0 %collective-permute-start.4 = (bf16[1,256,1024]{2,1,0:T(8,128)(2,1)S(1)}, bf16[1,256,1024]{2,1,0:T(8,128)(2,1)S(1)}, u32[]{:S(2)}, u32[]{:S(2)}) collective-permute-start(bf16[1,256,1024]{2,1,0:T(8,128)(2,1)S(1)} %add.29.mine_ref.refs_1_), channel_id=1, source_target_pairs={{0,128},{128,0},{1,129},{129,1},{2,130},{130,2},{3,131},{131,3},{4... | collective-permute-start | bytes 1572872 | tf_op jit(solution)/shard_map/ppermute | solution.py:274
  313.6 22.7 %collective-permute-start.9 = (bf16[4,1,2,64,1024]{4,3,2,1,0:T(8,128)(2,1)}, bf16[4,1,2,64,1024]{4,3,2,1,0:T(8,128)(2,1)}, u32[]{:S(2)}, u32[]{:S(2)}) collective-permute-start(bf16[4,1,2,64,1024]{4,3,2,1,0:T(8,128)(2,1)} %all-to-all-done.4.refs_1_.own_ref), channel_id=1, source_target_pairs={{0,4},{4,8},{8,12},{12,16},{16,20},{20,24},{24,28},{28,32},{32,36}... | collective-permute-start | bytes 3145736 | tf_op jit(solution)/shard_map/ppermute | solution.py:246
  321.4 14.8 %collective-permute-start.8 = (bf16[4,1,1,64,1024]{4,3,2,1,0:T(8,128)(2,1)}, bf16[4,1,1,64,1024]{4,3,2,1,0:T(8,128)(2,1)S(1)}, u32[]{:S(2)}, u32[]{:S(2)}) collective-permute-start(bf16[4,1,1,64,1024]{4,3,2,1,0:T(8,128)(2,1)} %all-to-all-done.5.refs_0_.q_ref), channel_id=1, source_target_pairs={{132,128},{136,132},{140,136},{144,140},{148,144},{152,148},{156,1... | collective-permute-start | bytes 1572872 | tf_op jit(solution)/shard_map/ppermute | solution.py:246
  322.1 1.4 copy-start.5
  335.4 8.5 %collective-permute-start.6 = (bf16[2,256,1024]{2,1,0:T(8,128)(2,1)S(1)}, bf16[2,256,1024]{2,1,0:T(8,128)(2,1)S(1)}, u32[]{:S(2)}, u32[]{:S(2)}) collective-permute-start(bf16[2,256,1024]{2,1,0:T(8,128)(2,1)S(1)} %get-tuple-element.20.refs_0_), channel_id=1, source_target_pairs={{128,132},{132,136},{136,140},{140,144},{144,148},{148,152},{152,1... | collective-permute-start | bytes 3145736 | tf_op jit(solution)/shard_map/ppermute | solution.py:246
  343.1 11.0 %collective-permute-start.10 = (bf16[1,256,1024]{2,1,0:T(8,128)(2,1)S(1)}, bf16[1,256,1024]{2,1,0:T(8,128)(2,1)S(1)}, u32[]{:S(2)}, u32[]{:S(2)}) collective-permute-start(bf16[1,256,1024]{2,1,0:T(8,128)(2,1)S(1)} %get-tuple-element.22), channel_id=1, source_target_pairs={{128,132},{132,136},{136,140},{140,144},{144,148},{148,152},{152,1... | collective-permute-start | bytes 1572872 | tf_op jit(solution)/shard_map/ppermute | solution.py:246
  344.3 23.4 %collective-permute-start.7 = (bf16[2,256,1024]{2,1,0:T(8,128)(2,1)S(1)}, bf16[2,256,1024]{2,1,0:T(8,128)(2,1)}, u32[]{:S(2)}, u32[]{:S(2)}) collective-permute-start(bf16[2,256,1024]{2,1,0:T(8,128)(2,1)S(1)} %add.31.mine_ref), channel_id=1, source_target_pairs={{0,128},{128,0},{1,129},{129,1},{2,130},{130,2},{3,131},{131,3},{4... | collective-permute-start | bytes 3145736 | tf_op jit(solution)/shard_map/ppermute | solution.py:274
  354.4 20.3 %collective-permute-start.11 = (bf16[1,256,1024]{2,1,0:T(8,128)(2,1)S(1)}, bf16[1,256,1024]{2,1,0:T(8,128)(2,1)}, u32[]{:S(2)}, u32[]{:S(2)}) collective-permute-start(bf16[1,256,1024]{2,1,0:T(8,128)(2,1)S(1)} %add.33.mine_ref), channel_id=1, source_target_pairs={{0,128},{128,0},{1,129},{129,1},{2,130},{130,2},{3,131},{131,3},{4... | collective-permute-start | bytes 1572872 | tf_op jit(solution)/shard_map/ppermute | solution.py:274
  359.6 2.2 copy-start
  364.2 13.4 %all-to-all-start.2 = ((bf16[4,1,64,1024]{3,2,1,0:T(8,128)(2,1)}), bf16[4,1,64,1024]{3,2,1,0:T(8,128)(2,1)S(1)}, u32[]{:S(2)}, u32[]{:S(2)}) async-start(bf16[4,1,64,1024]{3,2,1,0:T(8,128)(2,1)} %join.3), calls=%async_computation.2 | async-start | bytes 1048576 | tf_op jit(solution)/shard_map/all_to_all | solution.py:239
  367.7 2.2 copy-start.1
  377.6 2.2 copy-start.2
  394.0 17.0 %all-to-all-start.6 = ((bf16[4,2,64,1024]{3,2,1,0:T(8,128)(2,1)}), bf16[4,2,64,1024]{3,2,1,0:T(8,128)(2,1)S(1)}, u32[]{:S(2)}, u32[]{:S(2)}) async-start(bf16[4,2,64,1024]{3,2,1,0:T(8,128)(2,1)} %join.4.refs_1_), calls=%async_computation.6 | async-start | bytes 2097152 | tf_op jit(solution)/shard_map/all_to_all | solution.py:239
Sparse Core Ops, SparseCore 0:
  120.3 83.2 all-gather.1

commit v4 on v3

v4 whole, which is shorter than its diff:
```python
import math

import jax
import jax.numpy as jnp
from jax import lax
from jax.experimental import pallas as pl
from jax.experimental.pallas import tpu as pltpu
from jax.sharding import Mesh
from jax.sharding import PartitionSpec as P

HEAD = 128
SPAN = 256
HALF = SPAN // 2
RINGS = 32
LONG = 10**10
CHUNKS = ((0, 2), (2, 4))
NT = (((1,), (1,)), ((), ()))
NN = (((1,), (0,)), ((), ()))
TN = (((0,), (0,)), ((), ()))
PARAMS = pltpu.CompilerParams(vmem_limit_bytes=16 * 2**20)


def dot(a, b, dims=NN):
    return lax.dot_general(a, b, dims, preferred_element_type=jnp.float32)


def cost(flops, nbytes):
    return pl.CostEstimate(flops=flops, bytes_accessed=nbytes, transcendentals=0)


def table_kernel(place_ref, lengths_ref, first_ref, here_ref, ahead_ref):
    rows, count = lengths_ref.shape
    base = place_ref[0]
    lengths = lengths_ref[...].astype(jnp.float32)
    upto = lax.broadcasted_iota(jnp.int32, (count, count), 1) <= lax.broadcasted_iota(jnp.int32, (count, count), 0)
    before = lax.broadcasted_iota(jnp.int32, (count, count), 1) < lax.broadcasted_iota(jnp.int32, (count, count), 0)
    lengths = lengths.astype(jnp.bfloat16)
    ends = dot(jnp.where(upto, 1.0, 0.0).astype(jnp.bfloat16), lengths, NT)
    starts = dot(jnp.where(before, 1.0, 0.0).astype(jnp.bfloat16), lengths, NT)
    place = lax.broadcasted_iota(jnp.int32, (1, 2 * SPAN), 1)
    at = (place + base).astype(jnp.float32)
    for r in range(rows):
        start, stop = starts[:, r : r + 1], ends[:, r : r + 1]
        first = jnp.max(jnp.where(start <= at, start, 0.0), axis=0, keepdims=True).astype(jnp.int32) - base
        end = jnp.min(jnp.where(stop > at, stop, 1e6), axis=0, keepdims=True).astype(jnp.int32) - base
        mirror = jnp.where((first >= 0) & (first < SPAN), first + end - 1 - place, -1)
        first_ref[r] = first
        here_ref[r] = mirror[:, :SPAN]
        ahead_ref[r] = mirror[:, SPAN:]


def tables(place, lengths):
    rows = lengths.shape[0]
    return pl.pallas_call(
        table_kernel,
        in_specs=[pl.BlockSpec(memory_space=pltpu.SMEM), pl.BlockSpec(memory_space=pltpu.VMEM)],
        out_shape=[jax.ShapeDtypeStruct((rows, 1, n), jnp.int32) for n in (2 * SPAN, SPAN, SPAN)],
        compiler_params=PARAMS,
        cost_estimate=cost(1, 1),
        name="tables",
    )(place, lengths)


def pack_kernel(count, *refs):
    out_ref = refs[-1]
    pieces, share = out_ref.shape[0], out_ref.shape[-1]
    for t in range(count):
        for f in range(pieces):
            out_ref[f, 0, t] = refs[t][0, 0, :, f * share : (f + 1) * share]


def first_tile(array):
    lead = len(array.shape) - 2
    return pl.BlockSpec((1,) * lead + (16, 128), lambda *_: (0,) * (lead + 2))


def pack(states, chunk, pieces, after=()):
    low, high = chunk
    _, _, piece, width = states[0].shape
    share = width // pieces
    count = len(states)
    shape = (pieces, high - low, count, piece, share)
    return pl.pallas_call(
        lambda *refs: pack_kernel(count, *refs),
        grid=(high - low,),
        in_specs=[
            *[pl.BlockSpec((1, 1, piece, width), lambda r: (0, r + low, 0, 0))] * count,
            *[first_tile(array) for array in after],
        ],
        out_specs=pl.BlockSpec((pieces, 1, count, piece, share), lambda r: (0, r, 0, 0, 0)),
        out_shape=pltpu.HBM(shape, jnp.bfloat16),
        compiler_params=PARAMS,
        cost_estimate=cost(1, 1),
        name="pack",
    )(*[pltpu.with_memory_space_constraint(state, pltpu.HBM) for state in states], *after)


def attend_kernel(side_ref, first_ref, here_ref, ahead_ref, q_ref, next_q_ref, own_ref, other_ref, *refs):
    out_ref, sent_ref, contexts = refs[-3:]
    factor = math.log2(math.e) / math.sqrt(HEAD)
    pieces, _, _, piece, features = q_ref.shape
    block = SPAN // 2

    def rows(ref, index, start, stop, lanes):
        parts = []
        for ring in range(2):
            low, high = max(start - ring * SPAN, 0), min(stop - ring * SPAN, SPAN)
            if low < high:
                some = ref[ring][low // piece : high // piece, 0, index, :, lanes]
                parts.append(some.reshape(high - low, HEAD))
        return parts[0] if len(parts) == 1 else jnp.concatenate(parts, 0)

    def attend_rings(states, queries, spots, keep_at):
        for spot in spots:
            start, stop = max(0, spot - SPAN), spot + block
            key = lax.broadcasted_iota(jnp.int32, (stop - start, block), 0) + start
            here = lax.broadcasted_iota(jnp.int32, (stop - start, block), 1) + spot
            keep = (key >= first_ref[0, :, spot:stop]) & (key <= here)
            bias = jnp.where(keep, 0.0, -1e30)
            for h in range(features // HEAD):
                lanes = slice(h * HEAD, (h + 1) * HEAD)
                scores = dot(rows(states, 0, start, stop, lanes), rows(queries, 0, spot, stop, lanes), NT) + bias
                top = jnp.max(scores, axis=0, keepdims=True)
                raised = jnp.exp2((scores - top) * factor)
                total = jnp.sum(raised, axis=0, keepdims=True)
                weights = (raised * (1.0 / total)).astype(jnp.bfloat16)
                context = dot(weights, rows(states, 1, start, stop, lanes), TN)
                keep_at(slice(spot, stop), lanes, context.astype(jnp.bfloat16))

    @pl.when(side_ref[0] == 0)
    def _():
        def store(at, lanes, context):
            out_ref[0, at.start - SPAN : at.stop - SPAN, lanes] = context

        attend_rings((other_ref, own_ref), (None, q_ref), (SPAN, SPAN + block), store)
        sent_ref[...] = jnp.zeros_like(sent_ref)

    @pl.when(side_ref[0] != 0)
    def _():
        def store(at, lanes, context):
            contexts[at, lanes] = context

        attend_rings((own_ref, other_ref), (q_ref, next_q_ref), (0, block, SPAN, SPAN + block), store)
        source = lax.broadcasted_iota(jnp.int32, (2 * SPAN, SPAN), 0)
        for index, ref in ((here_ref[0], out_ref), (ahead_ref[0], sent_ref)):
            chosen = jnp.where(source == index, 1.0, 0.0).astype(jnp.bfloat16)
            ref[0] = dot(chosen, contexts[...], TN).astype(jnp.bfloat16)


def attend(side, first, here, ahead, q, next_q, own, other, chunk, base, after, weight):
    pieces, _, _, piece, features = own.shape
    low, high = chunk
    rows = high - low

    def line(array):
        return pl.BlockSpec((1, 1, array.shape[2]), lambda r: (r + low, 0, 0))

    def states(array, at):
        return pl.BlockSpec((pieces, 1, array.shape[2], piece, features), lambda r: (0, r + at, 0, 0, 0))

    block = pl.BlockSpec((1, SPAN, features), lambda r: (r, 0, 0))
    return pl.pallas_call(
        attend_kernel,
        grid=(rows,),
        in_specs=[
            pl.BlockSpec(memory_space=pltpu.SMEM),
            line(first),
            line(here),
            line(ahead),
            states(q, low),
            states(next_q, low),
            states(own, low - base),
            states(other, low - base),
            *[first_tile(array) for array in after],
        ],
        out_specs=[block, block],
        out_shape=[jax.ShapeDtypeStruct((rows, SPAN, features), jnp.bfloat16)] * 2,
        scratch_shapes=[pltpu.VMEM((2 * SPAN, features), jnp.bfloat16)],
        compiler_params=pltpu.CompilerParams(vmem_limit_bytes=28 * 2**20),
        cost_estimate=cost(rows * weight, 1),
        name="attend",
    )(side, first, here, ahead, q, next_q, own, other, *after)


def join_kernel(side_ref, mine_ref, other_ref, weight_ref, second_ref, *refs):
    out_ref = refs[-1]
    rows, tokens, depth = mine_ref.shape
    pieces, _, piece, wide = out_ref.shape
    weight = weight_ref[...].reshape(depth, wide)
    second = second_ref[...].reshape(depth, wide)
    for r in range(rows):
        total = dot(mine_ref[r], weight) + dot(other_ref[r], second)
        out_ref[:, r] = total.astype(jnp.bfloat16).reshape(pieces, piece, wide)


def join(side, mine, other, weight, pieces, after=()):
    rows, tokens, depth = mine.shape
    heads, _, head, units = weight.shape
    wide = units // 2
    whole = pl.BlockSpec((rows, tokens, depth), lambda n, side: (0, 0, 0))
    return pl.pallas_call(
        join_kernel,
        grid_spec=pltpu.PrefetchScalarGridSpec(
            num_scalar_prefetch=1,
            grid=(units // wide,),
            in_specs=[
                whole,
                whole,
                pl.BlockSpec((heads, 1, head, wide), lambda n, side: (0, side[0], 0, n)),
                pl.BlockSpec((heads, 1, head, wide), lambda n, side: (0, 1 - side[0], 0, n)),
                *[first_tile(array) for array in after],
            ],
            out_specs=pl.BlockSpec((pieces, rows, tokens // pieces, wide), lambda n, side: (0, 0, 0, n)),
        ),
        out_shape=jax.ShapeDtypeStruct((pieces, rows, tokens // pieces, units), jnp.bfloat16),
        compiler_params=PARAMS,
        cost_estimate=cost(1, 1),
        name="join",
    )(side, mine, other, weight, weight, *after)


def body(queries, key_states, value_vectors, hypothesis_lengths, join_weight):
    _, rows, piece, width = queries.shape
    pieces = SPAN // piece
    share = width // pieces
    side = lax.axis_index("dir")
    ring = lax.axis_index("y") * 8 + lax.axis_index("z")

    def exchange(parts):
        return lax.all_to_all(parts, "x", split_axis=0, concat_axis=0, tiled=True)

    to_left = [(RINGS + c + 1, RINGS + c) for c in range(RINGS - 1)]
    to_right = [(RINGS + c, RINGS + c + 1) for c in range(RINGS - 1)]
    outward = [(c, c + 1) for c in range(RINGS - 1)] + to_left

    def passed(array, pairs):
        return lax.ppermute(array, ("dir", "y", "z"), pairs)

    turned = lax.ppermute(
        join_weight.reshape(piece, -1), ("y", "x"), [(y * 4 + x, x * 4 + y) for y in range(4) for x in range(4)]
    )
    weight = lax.all_gather(turned, ("z", "y"), tiled=True)
    units = weight.shape[1]
    weight_rows = pltpu.with_memory_space_constraint(weight.reshape(share // HEAD, 2, HEAD, units), pltpu.HBM)
    base = (ring - 1 + side) * SPAN
    lines = tables(base[None], hypothesis_lengths)

    both = (key_states, value_vectors)
    own_early = exchange(pack(both, CHUNKS[0], pieces))
    other_early = passed(own_early, outward)
    q = exchange(pack((queries,), (0, rows), pieces, (own_early, turned)))
    next_q = passed(q, to_left)
    own_late = exchange(pack(both, CHUNKS[1], pieces, (q, other_early)))
    other_late = passed(own_late, outward)

    def contexts(own, other, chunk, low, after=(), weight=LONG):
        return attend(side[None], *lines, q, next_q, own, other, chunk, low, after, weight)

    def swapped(mine, ahead):
        mine = mine + passed(ahead, to_right)
        return mine, lax.ppermute(mine, "dir", [(0, 1), (1, 0)])

    def joined_part(mine, partner, after=()):
        return join(side[None], mine, partner, weight_rows, pieces, after)

    def gated(arrived):
        total = jnp.sum(arrived.astype(jnp.float32), axis=0)
        return (jax.nn.silu(total[..., : units // 2]) * total[..., units // 2 :]).astype(jnp.bfloat16)

    early = contexts(own_early, other_early, (0, 2), 0, (own_late,))
    late = contexts(own_late, other_late, (2, 4), 2, (early[1],))
    partial_value = joined_part(*swapped(*early), ())
    arrived = [exchange(partial_value), exchange(joined_part(*swapped(*late), (partial_value,)))]
    joined = [gated(one) for one in arrived]
    return jnp.concatenate(joined)


def solution(mesh):
    fine = Mesh(mesh.devices.reshape(2, 4, 8, 4), ("dir", "y", "z", "x"))
    states = P("dir", None, ("y", "z", "x"), None)
    return jax.shard_map(
        body,
        mesh=fine,
        in_specs=(states, states, states, P(), P(("y", "z", "x"), None, "dir")),
        out_specs=P(None, ("y", "z", "x"), "dir"),
        check_vma=False,
    )
```

time: 420 us -> 252 us (0.60)
  Pallas kernels: 236 us -> 30.8 us
  blocking collectives: 11.5 us -> 59.8 us
  starting transfers between devices: 64.4 us -> 34.5 us
  waiting for transfers between devices: 78.8 us -> 104 us
  local copies, waits for them, and re-layouts: 11 us -> 2.22 us
    pallas_call x5 -> x3, Pallas kernels: 199 us -> 9.12 us  [pack(): pl.pallas_call(lambda *refs: pack_kernel(count, *refs), grid=(high - low,...]
    all_to_all x1 -> x2, blocking collectives: 11.5 us -> 59.8 us  [exchange(): return lax.all_to_all(parts, 'x', split_axis=0, concat_axis=0, tiled=True)]
    ppermute x8 -> x5, waiting for transfers between devices: 17.6 us -> 50.1 us  [passed(): return lax.ppermute(array, ('dir', 'y', 'z'), pairs)]
    all_to_all x7 -> x3, starting transfers between devices: 31.7 us -> 12.2 us  [exchange(): return lax.all_to_all(parts, 'x', split_axis=0, concat_axis=0, tiled=True)]
    pallas_call x3 -> x2, Pallas kernels: 26 us -> 10.5 us  [attend(): pl.pallas_call(attend_kernel, grid=(rows,), in_specs=[pl.BlockSpec(memory...]
    unnamed x25 -> x11, local copies, waits for them, and re-layouts: 11 us -> 2.22 us
    ppermute x3 -> x2, starting transfers between devices: 15.4 us -> 9.09 us  [swapped(): return (mine, lax.ppermute(mine, 'dir', [(0, 1), (1, 0)]))]
    ppermute x1, waiting for transfers between devices: 11.8 us -> 6.59 us  [body(): lax.ppermute(join_weight.reshape(piece, -1), ('y', 'x'), [(y * 4 + x, x *...]
  transfers between devices with their start and end apart: 20 -> 12, of which waited for: 7 -> 5; matrix products, arithmetic and copies ran while one was open for 1% -> 1% of each run, Pallas kernels for 36% -> 11%
where the time goes in v4:
time: 252 us; the launch traced here: 249 us
  waiting for transfers between devices  104 us (41%)
  blocking collectives  59.8 us (24%)
  starting transfers between devices  34.5 us (14%)
  Pallas kernels  30.8 us (12%)
  between operations  13.6 us (5%)
  other arithmetic  3.34 us (1%)
    all_to_all x2, blocking collectives, exchange(): return lax.all_to_all(parts, 'x', split_axis=0, concat_axis=0, tiled=True)  59.8 us
    ppermute x5, waiting for transfers between devices, passed(): return lax.ppermute(array, ('dir', 'y', 'z'), pairs)  50.1 us
    all_to_all x3, waiting for transfers between devices, exchange(): return lax.all_to_all(parts, 'x', split_axis=0, concat_axis=0, tiled=True)  47.1 us
    all_to_all x3, starting transfers between devices, exchange(): return lax.all_to_all(parts, 'x', split_axis=0, concat_axis=0, tiled=True)  12.2 us
    pallas_call x2, Pallas kernels, attend(): pl.pallas_call(attend_kernel, grid=(rows,), in_specs=[pl.BlockSpec(memory...  10.5 us
    pallas_call x2, Pallas kernels, join(): pl.pallas_call(join_kernel, grid_spec=pltpu.PrefetchScalarGridSpec(num_sc...  9.94 us
    ppermute x5, starting transfers between devices, passed(): return lax.ppermute(array, ('dir', 'y', 'z'), pairs)  9.41 us
    pallas_call x3, Pallas kernels, pack(): pl.pallas_call(lambda *refs: pack_kernel(count, *refs), grid=(high - low,...  9.12 us
  transfers between devices with their start and end apart: 12, of which 5 were waited for; matrix products, arithmetic and copies ran while one was open for 1% of the time, Pallas kernels for 11%

profile of v4, /device:TPU:8, one launch (start us, length us, event | category | flops | bytes accessed | tf_op | source)
XLA Modules:
  0.0 248.7 jit_solution(10086477765496998171)
XLA Ops:
  6.5 2.6 %pack.3 = bf16[4,2,2,64,1024]{4,3,2,1,0:T(8,128)(2,1)} custom-call(bf16[1,4,64,4096]{3,2,1,0:T(8,128)(2,1)} %refs_0_.5, bf16[1,4,64,4096]{3,2,1,0:T(8,128)(2,1)} %refs_1_.3), custom_call_target="tpu_custom_call" | custom-call | flops 1 | bytes 1 | tf_op jit(solution)/shard_map/pack/pallas_call | solution.py:83
  9.1 0.0 copy-start.4
  9.2 30.8 %all_to_all.25.refs_1_.own_ref = bf16[4,2,2,64,1024]{4,3,2,1,0:T(8,128)(2,1)S(1)} all-to-all(bf16[4,2,2,64,1024]{4,3,2,1,0:T(8,128)(2,1)} %pack.3), channel_id=1, replica_groups=mesh['dir'=2,'y'=4,'z'=8,'x'=4] {'x'}, dimensions={0} | all-to-all | bytes 4194304 | tf_op jit(solution)/shard_map/all_to_all | solution.py:230
  39.9 3.8 %collective-permute-start.2 = (bf16[4,2,2,64,1024]{4,3,2,1,0:T(8,128)(2,1)S(1)}, bf16[4,2,2,64,1024]{4,3,2,1,0:T(8,128)(2,1)}, u32[]{:S(2)}, u32[]{:S(2)}) collective-permute-start(bf16[4,2,2,64,1024]{4,3,2,1,0:T(8,128)(2,1)S(1)} %all_to_all.25.refs_1_.own_ref), channel_id=1, source_target_pairs={{0,4},{4,8},{8,12},{12,16},{16,20},{20,24},{24,28},{28,32},{32,36}... | collective-permute-start | bytes 6291464 | tf_op jit(solution)/shard_map/ppermute | solution.py:237
  43.7 0.0 copy-done.4
  43.8 3.7 %collective-permute-start = (bf16[64,1024]{1,0:T(8,128)(2,1)S(1)}, bf16[64,1024]{1,0:T(8,128)(2,1)S(1)}, u32[]{:S(2)}, u32[]{:S(2)}) collective-permute-start(bf16[64,1024]{1,0:T(8,128)(2,1)S(1)} %bitcast.10), channel_id=1, source_target_pairs={{0,0},{1,32},{2,64},{3,96},{32,1},{33,33},{34,65},{35,97},{64,2},{... | collective-permute-start | bytes 393224 | tf_op jit(solution)/shard_map/ppermute | solution.py:239
  47.5 6.6 %collective-permute-done.refs_2_ = bf16[64,1024]{1,0:T(8,128)(2,1)S(1)} collective-permute-done((bf16[64,1024]{1,0:T(8,128)(2,1)S(1)}, bf16[64,1024]{1,0:T(8,128)(2,1)S(1)}, u32[]{:S(2)}, u32[]{:S(2)}) %collective-permute-start) | collective-permute-done | bytes 131104 | tf_op jit(solution)/shard_map/ppermute | solution.py:239
  54.1 0.0 copy-start.2
  54.1 3.9 %pack.4 = bf16[4,4,1,64,1024]{4,3,2,1,0:T(8,128)(2,1)} custom-call(bf16[1,4,64,4096]{3,2,1,0:T(8,128)(2,1)} %refs_0_.4, bf16[4,2,2,64,1024]{4,3,2,1,0:T(8,128)(2,1)S(1)} %all_to_all.25.refs_1_.own_ref, bf16[64,1024]{1,0:T(8,128)(2,1)S(1)} %collective-permute-done.refs_2_), custom_call_target="tpu_custom_call" | custom-call | flops 1 | bytes 1 | tf_op jit(solution)/shard_map/pack/pallas_call | solution.py:83
  57.9 0.0 copy-done.2
  57.9 4.5 %all-to-all-start.1 = ((bf16[4,4,1,64,1024]{4,3,2,1,0:T(8,128)(2,1)}), bf16[4,4,1,64,1024]{4,3,2,1,0:T(8,128)(2,1)}, u32[]{:S(2)}, u32[]{:S(2)}) async-start(bf16[4,4,1,64,1024]{4,3,2,1,0:T(8,128)(2,1)} %pack.4), calls=%async_computation.1 | async-start | bytes 4194304 | tf_op jit(solution)/shard_map/all_to_all | solution.py:230
  62.4 0.0 all-gather.2.cloned.1.call-start
  62.4 0.7 all-gather.2.cloned.1.call-update
  63.1 23.4 %all-to-all-done.1.refs_2_.q_ref = bf16[4,4,1,64,1024]{4,3,2,1,0:T(8,128)(2,1)} async-done(((bf16[4,4,1,64,1024]{4,3,2,1,0:T(8,128)(2,1)}), bf16[4,4,1,64,1024]{4,3,2,1,0:T(8,128)(2,1)}, u32[]{:S(2)}, u32[]{:S(2)}) %all-to-all-start.1) | async-done | bytes 2097184 | tf_op jit(solution)/shard_map/all_to_all | solution.py:230
  86.5 2.0 collective-permute-start.1
  88.6 0.0 collective-permute-done.2.refs_3_.other_ref
  88.6 2.6 %pack.5 = bf16[4,2,2,64,1024]{4,3,2,1,0:T(8,128)(2,1)} custom-call(bf16[1,4,64,4096]{3,2,1,0:T(8,128)(2,1)} %refs_0_.5, bf16[1,4,64,4096]{3,2,1,0:T(8,128)(2,1)} %refs_1_.3, bf16[4,4,1,64,1024]{4,3,2,1,0:T(8,128)(2,1)} %all-to-all-done.1.refs_2_.q_ref, bf16[4,2,2,64,1024]{4,3,2,1,0:T(8,128)(2,1)} %collective-permute-done.2.refs_3_.other_ref), custom_call_target="tpu_custom_call" | custom-call | flops 1 | bytes 1 | tf_op jit(solution)/shard_map/pack/pallas_call | solution.py:83
  91.2 0.0 copy-start.3
  91.2 29.0 %all_to_all.26.refs_0_.own_ref = bf16[4,2,2,64,1024]{4,3,2,1,0:T(8,128)(2,1)} all-to-all(bf16[4,2,2,64,1024]{4,3,2,1,0:T(8,128)(2,1)} %pack.5), channel_id=1, replica_groups=mesh['dir'=2,'y'=4,'z'=8,'x'=4] {'x'}, dimensions={0} | all-to-all | bytes 4194304 | tf_op jit(solution)/shard_map/all_to_all | solution.py:230
  120.2 1.9 collective-permute-start.5
  122.2 0.0 copy-done.3
  122.2 1.2 tables.1
  123.4 0.0 collective-permute-done.1.next_q_ref
  123.4 5.1 %attend.2 = (bf16[2,256,1024]{2,1,0:T(8,128)(2,1)S(1)}, bf16[2,256,1024]{2,1,0:T(8,128)(2,1)S(1)}) custom-call(s32[1]{0:T(128)} %bitcast.side_ref, s32[4,1,512]{2,1,0:T(1,128)S(1)} %get-tuple-element.12.first_ref, s32[4,1,256]{2,1,0:T(1,128)S(1)} %get-tuple-element.13.here_ref, s32[4,1,256]{2,1,0:T(1,128)S(1)} %get-tuple-element.14.ahead_ref, ...), custom_call_target="tpu_custom_call" | custom-call | flops 20000000000 | bytes 1 | tf_op jit(solution)/shard_map/attend/pallas_call | solution.py:162
  128.5 0.9 collective-permute-start.3
  129.5 50.1 %collective-permute-done.5.other_ref = bf16[4,2,2,64,1024]{4,3,2,1,0:T(8,128)(2,1)} collective-permute-done((bf16[4,2,2,64,1024]{4,3,2,1,0:T(8,128)(2,1)}, bf16[4,2,2,64,1024]{4,3,2,1,0:T(8,128)(2,1)}, u32[]{:S(2)}, u32[]{:S(2)}) %collective-permute-start.5) | collective-permute-done | bytes 2097184 | tf_op jit(solution)/shard_map/ppermute | solution.py:237
  179.5 5.4 %attend.3 = (bf16[2,256,1024]{2,1,0:T(8,128)(2,1)S(1)}, bf16[2,256,1024]{2,1,0:T(8,128)(2,1)S(1)}) custom-call(s32[1]{0:T(128)} %bitcast.side_ref, s32[4,1,512]{2,1,0:T(1,128)S(1)} %get-tuple-element.12.first_ref, s32[4,1,256]{2,1,0:T(1,128)S(1)} %get-tuple-element.13.here_ref, s32[4,1,256]{2,1,0:T(1,128)S(1)} %get-tuple-element.14.ahead_ref, ...), custom_call_target="tpu_custom_call" | custom-call | flops 20000000000 | bytes 1 | tf_op jit(solution)/shard_map/attend/pallas_call | solution.py:162
  184.9 0.7 collective-permute-start.6
  185.7 0.0 collective-permute-done.3
  185.7 0.4 add.22.mine_ref
  186.1 0.1 collective-permute-start.4
  186.2 0.0 collective-permute-done.6
  186.2 0.4 add.24.mine_ref
  186.6 9.0 %collective-permute-start.7 = (bf16[2,256,1024]{2,1,0:T(8,128)(2,1)S(1)}, bf16[2,256,1024]{2,1,0:T(8,128)(2,1)S(1)}, u32[]{:S(2)}, u32[]{:S(2)}) collective-permute-start(bf16[2,256,1024]{2,1,0:T(8,128)(2,1)S(1)} %add.24.mine_ref), channel_id=1, source_target_pairs={{0,128},{128,0},{1,129},{129,1},{2,130},{130,2},{3,131},{131,3},{4... | collective-permute-start | bytes 3145736 | tf_op jit(solution)/shard_map/ppermute | solution.py:261
  195.6 0.0 collective-permute-done.4.other_ref
  195.6 0.0 copy-start
  195.6 1.0 copy-done
  196.6 0.0 all-gather.2.cloned.1.call-done
  196.6 0.0 copy-start.1
  196.6 1.2 copy-done.1
  197.8 5.0 %join.2.refs_0_ = bf16[4,2,64,1024]{3,2,1,0:T(8,128)(2,1)} custom-call(s32[1]{0:T(128)} %bitcast.side_ref, bf16[2,256,1024]{2,1,0:T(8,128)(2,1)S(1)} %add.22.mine_ref, bf16[2,256,1024]{2,1,0:T(8,128)(2,1)S(1)} %copy-done.1, bf16[8,2,128,1024]{3,2,1,0:T(8,128)(2,1)} %bitcast.5, bf16[8,2,128,1024]{3,2,1,0:T(8,128)(2,1)} %bitcast.6), custom_call_target="tpu_custom_call" | custom-call | flops 1 | bytes 1 | tf_op jit(solution)/shard_map/join/pallas_call | solution.py:201
  202.8 4.3 %all-to-all-start.3 = ((bf16[4,2,64,1024]{3,2,1,0:T(8,128)(2,1)}), bf16[4,2,64,1024]{3,2,1,0:T(8,128)(2,1)}, u32[]{:S(2)}, u32[]{:S(2)}) async-start(bf16[4,2,64,1024]{3,2,1,0:T(8,128)(2,1)} %join.2.refs_0_), calls=%async_computation.3 | async-start | bytes 2097152 | tf_op jit(solution)/shard_map/all_to_all | solution.py:230
  207.1 0.0 collective-permute-done.7.other_ref
  207.1 5.0 %join.3 = bf16[4,2,64,1024]{3,2,1,0:T(8,128)(2,1)} custom-call(s32[1]{0:T(128)} %bitcast.side_ref, bf16[2,256,1024]{2,1,0:T(8,128)(2,1)S(1)} %add.24.mine_ref, bf16[2,256,1024]{2,1,0:T(8,128)(2,1)S(1)} %collective-permute-done.7.other_ref, bf16[8,2,128,1024]{3,2,1,0:T(8,128)(2,1)} %bitcast.7, bf16[8,2,128,1024]{3,2,1,0:T(8,128)(2,1)} %bitcast.8, ...), custom_call_target="tpu_custom_call" | custom-call | flops 1 | bytes 1 | tf_op jit(solution)/shard_map/join/pallas_call | solution.py:201
  212.0 10.6 %all-to-all-done.3 = bf16[4,2,64,1024]{3,2,1,0:T(8,128)(2,1)} async-done(((bf16[4,2,64,1024]{3,2,1,0:T(8,128)(2,1)}), bf16[4,2,64,1024]{3,2,1,0:T(8,128)(2,1)}, u32[]{:S(2)}, u32[]{:S(2)}) %all-to-all-start.3) | async-done | bytes 1048608 | tf_op jit(solution)/shard_map/all_to_all | solution.py:230
  222.7 3.5 %all-to-all-start.4 = ((bf16[4,2,64,1024]{3,2,1,0:T(8,128)(2,1)}), bf16[4,2,64,1024]{3,2,1,0:T(8,128)(2,1)S(1)}, u32[]{:S(2)}, u32[]{:S(2)}) async-start(bf16[4,2,64,1024]{3,2,1,0:T(8,128)(2,1)} %join.3), calls=%async_computation.4 | async-start | bytes 2097152 | tf_op jit(solution)/shard_map/all_to_all | solution.py:230
  226.2 1.5 convert_reduce_fusion.1
  227.7 0.1 fusion.1
  227.8 13.1 %all-to-all-done.4 = bf16[4,2,64,1024]{3,2,1,0:T(8,128)(2,1)S(1)} async-done(((bf16[4,2,64,1024]{3,2,1,0:T(8,128)(2,1)}), bf16[4,2,64,1024]{3,2,1,0:T(8,128)(2,1)S(1)}, u32[]{:S(2)}, u32[]{:S(2)}) %all-to-all-start.4) | async-done | bytes 1048608 | tf_op jit(solution)/shard_map/all_to_all | solution.py:230
  240.9 0.2 convert_reduce_fusion
  241.1 0.1 fusion
  241.2 0.7 pad_maximum_fusion
  (1 shorter events, 0.0 us)
Async XLA Ops:
  9.1 34.6 %copy-start.4 = (bf16[64,2,512]{2,1,0:T(2,128)(2,1)S(1)}, bf16[64,2,512]{2,1,0:T(2,128)(2,1)}, u32[]{:S(2)}) copy-start(bf16[64,2,512]{2,1,0:T(2,128)(2,1)} %param.9) | copy-start | bytes 393220
  39.9 48.7 %collective-permute-start.2 = (bf16[4,2,2,64,1024]{4,3,2,1,0:T(8,128)(2,1)S(1)}, bf16[4,2,2,64,1024]{4,3,2,1,0:T(8,128)(2,1)}, u32[]{:S(2)}, u32[]{:S(2)}) collective-permute-start(bf16[4,2,2,64,1024]{4,3,2,1,0:T(8,128)(2,1)S(1)} %all_to_all.25.refs_1_.own_ref), channel_id=1, source_target_pairs={{0,4},{4,8},{8,12},{12,16},{16,20},{20,24},{24,28},{28,32},{32,36}... | collective-permute-start | bytes 6291464 | tf_op jit(solution)/shard_map/ppermute | solution.py:237
  43.8 10.3 %collective-permute-start = (bf16[64,1024]{1,0:T(8,128)(2,1)S(1)}, bf16[64,1024]{1,0:T(8,128)(2,1)S(1)}, u32[]{:S(2)}, u32[]{:S(2)}) collective-permute-start(bf16[64,1024]{1,0:T(8,128)(2,1)S(1)} %bitcast.10), channel_id=1, source_target_pairs={{0,0},{1,32},{2,64},{3,96},{32,1},{33,33},{34,65},{35,97},{64,2},{... | collective-permute-start | bytes 393224 | tf_op jit(solution)/shard_map/ppermute | solution.py:239
  54.1 3.9 %copy-start.2 = (bf16[64,1024]{1,0:T(8,128)(2,1)}, bf16[64,1024]{1,0:T(8,128)(2,1)S(1)}, u32[]{:S(2)}) copy-start(bf16[64,1024]{1,0:T(8,128)(2,1)S(1)} %collective-permute-done.refs_2_) | copy-start | bytes 393220
  57.9 28.6 %all-to-all-start.1 = ((bf16[4,4,1,64,1024]{4,3,2,1,0:T(8,128)(2,1)}), bf16[4,4,1,64,1024]{4,3,2,1,0:T(8,128)(2,1)}, u32[]{:S(2)}, u32[]{:S(2)}) async-start(bf16[4,4,1,64,1024]{4,3,2,1,0:T(8,128)(2,1)} %pack.4), calls=%async_computation.1 | async-start | bytes 4194304 | tf_op jit(solution)/shard_map/all_to_all | solution.py:230
  62.4 134.2 %all-gather.2.cloned.1.call-start = ((), (), s32[]{:S(2)}) async-start(), calls=%async_computation.5 | async-start | bytes 4325376 | tf_op jit(solution)/shard_map/all_gather | solution.py:242
  86.5 36.9 %collective-permute-start.1 = (bf16[4,4,1,64,1024]{4,3,2,1,0:T(8,128)(2,1)}, bf16[4,4,1,64,1024]{4,3,2,1,0:T(8,128)(2,1)}, u32[]{:S(2)}, u32[]{:S(2)}) collective-permute-start(bf16[4,4,1,64,1024]{4,3,2,1,0:T(8,128)(2,1)} %all-to-all-done.1.refs_2_.q_ref), channel_id=1, source_target_pairs={{132,128},{136,132},{140,136},{144,140},{148,144},{152,148},{156,1... | collective-permute-start | bytes 6291464 | tf_op jit(solution)/shard_map/ppermute | solution.py:237
  91.2 31.0 %copy-start.3 = (s32[4,512]{1,0:T(4,128)S(1)}, s32[4,512]{1,0:T(4,128)}, u32[]{:S(2)}) copy-start(s32[4,512]{1,0:T(4,128)} %lengths_ref.1) | copy-start | bytes 24580
  120.2 59.3 %collective-permute-start.5 = (bf16[4,2,2,64,1024]{4,3,2,1,0:T(8,128)(2,1)}, bf16[4,2,2,64,1024]{4,3,2,1,0:T(8,128)(2,1)}, u32[]{:S(2)}, u32[]{:S(2)}) collective-permute-start(bf16[4,2,2,64,1024]{4,3,2,1,0:T(8,128)(2,1)} %all_to_all.26.refs_0_.own_ref), channel_id=1, source_target_pairs={{0,4},{4,8},{8,12},{12,16},{16,20},{20,24},{24,28},{28,32},{32,36}... | collective-permute-start | bytes 6291464 | tf_op jit(solution)/shard_map/ppermute | solution.py:237
  128.5 57.1 %collective-permute-start.3 = (bf16[2,256,1024]{2,1,0:T(8,128)(2,1)S(1)}, bf16[2,256,1024]{2,1,0:T(8,128)(2,1)S(1)}, u32[]{:S(2)}, u32[]{:S(2)}) collective-permute-start(bf16[2,256,1024]{2,1,0:T(8,128)(2,1)S(1)} %get-tuple-element.16.refs_0_), channel_id=1, source_target_pairs={{128,132},{132,136},{136,140},{140,144},{144,148},{148,152},{152,1... | collective-permute-start | bytes 3145736 | tf_op jit(solution)/shard_map/ppermute | solution.py:237
  184.9 1.3 collective-permute-start.6
  186.1 9.5 %collective-permute-start.4 = (bf16[2,256,1024]{2,1,0:T(8,128)(2,1)S(1)}, bf16[2,256,1024]{2,1,0:T(8,128)(2,1)S(1)}, u32[]{:S(2)}, u32[]{:S(2)}) collective-permute-start(bf16[2,256,1024]{2,1,0:T(8,128)(2,1)S(1)} %add.22.mine_ref), channel_id=1, source_target_pairs={{0,128},{128,0},{1,129},{129,1},{2,130},{130,2},{3,131},{131,3},{4... | collective-permute-start | bytes 3145736 | tf_op jit(solution)/shard_map/ppermute | solution.py:261
  186.6 20.4 %collective-permute-start.7 = (bf16[2,256,1024]{2,1,0:T(8,128)(2,1)S(1)}, bf16[2,256,1024]{2,1,0:T(8,128)(2,1)S(1)}, u32[]{:S(2)}, u32[]{:S(2)}) collective-permute-start(bf16[2,256,1024]{2,1,0:T(8,128)(2,1)S(1)} %add.24.mine_ref), channel_id=1, source_target_pairs={{0,128},{128,0},{1,129},{129,1},{2,130},{130,2},{3,131},{131,3},{4... | collective-permute-start | bytes 3145736 | tf_op jit(solution)/shard_map/ppermute | solution.py:261
  195.6 1.0 copy-start
  196.6 1.2 copy-start.1
  202.8 19.9 %all-to-all-start.3 = ((bf16[4,2,64,1024]{3,2,1,0:T(8,128)(2,1)}), bf16[4,2,64,1024]{3,2,1,0:T(8,128)(2,1)}, u32[]{:S(2)}, u32[]{:S(2)}) async-start(bf16[4,2,64,1024]{3,2,1,0:T(8,128)(2,1)} %join.2.refs_0_), calls=%async_computation.3 | async-start | bytes 2097152 | tf_op jit(solution)/shard_map/all_to_all | solution.py:230
  222.7 18.2 %all-to-all-start.4 = ((bf16[4,2,64,1024]{3,2,1,0:T(8,128)(2,1)}), bf16[4,2,64,1024]{3,2,1,0:T(8,128)(2,1)S(1)}, u32[]{:S(2)}, u32[]{:S(2)}) async-start(bf16[4,2,64,1024]{3,2,1,0:T(8,128)(2,1)} %join.3), calls=%async_computation.4 | async-start | bytes 2097152 | tf_op jit(solution)/shard_map/all_to_all | solution.py:230
Sparse Core Ops, SparseCore 0:
  65.8 91.5 all-gather.1

commit v5 on v4

--- a/solution.py
+++ b/solution.py
@@ -90,7 +90,7 @@
         out_specs=pl.BlockSpec((pieces, 1, count, piece, share), lambda r: (0, r, 0, 0, 0)),
         out_shape=pltpu.HBM(shape, jnp.bfloat16),
         compiler_params=PARAMS,
-        cost_estimate=cost(1, 1),
+        cost_estimate=cost(2*10**9, 1),
         name="pack",
     )(*[pltpu.with_memory_space_constraint(state, pltpu.HBM) for state in states], *after)
 
@@ -226,6 +226,9 @@
     side = lax.axis_index("dir")
     ring = lax.axis_index("y") * 8 + lax.axis_index("z")
 
+    def behind(array, *others):
+        return lax.optimization_barrier((array, *others))[0]
+
     def exchange(parts):
         return lax.all_to_all(parts, "x", split_axis=0, concat_axis=0, tiled=True)
 
@@ -268,10 +271,14 @@
         return (jax.nn.silu(total[..., : units // 2]) * total[..., units // 2 :]).astype(jnp.bfloat16)
 
     early = contexts(own_early, other_early, (0, 2), 0, (own_late,))
-    late = contexts(own_late, other_late, (2, 4), 2, (early[1],))
-    partial_value = joined_part(*swapped(*early), ())
-    arrived = [exchange(partial_value), exchange(joined_part(*swapped(*late), (partial_value,)))]
-    joined = [gated(one) for one in arrived]
+    late = contexts(own_late, other_late, (2, 3), 2, (early[1],))
+    partial_early = joined_part(*swapped(*early))
+    last = contexts(own_late, other_late, (3, 4), 2, (late[1], partial_early))
+    early = exchange(partial_early)
+    partial_late = joined_part(*swapped(*late), ())
+    late = exchange(behind(partial_late, early))
+    last = exchange(joined_part(*swapped(*last), (partial_late,)))
+    joined = [gated(one) for one in (early, late, last)]
     return jnp.concatenate(joined)
 
 

time: 252 us -> 252 us (level)
  starting transfers between devices: 34.5 us -> 96.6 us
  waiting for transfers between devices: 104 us -> 59.4 us
  blocking collectives: 59.8 us -> 31.3 us
  local copies, waits for them, and re-layouts: 2.22 us -> 11.3 us
  Pallas kernels: 30.8 us -> 35 us
    ppermute x5 -> x6, waiting for transfers between devices: 50.1 us -> 0.02 us  [passed(): return lax.ppermute(array, ('dir', 'y', 'z'), pairs)]
    ppermute x2 -> x3, starting transfers between devices: 9.09 us -> 57.3 us  [swapped(): return (mine, lax.ppermute(mine, 'dir', [(0, 1), (1, 0)]))]
    all_to_all x2 -> x1, blocking collectives: 59.8 us -> 31.3 us  [exchange(): return lax.all_to_all(parts, 'x', split_axis=0, concat_axis=0, tiled=True)]
    ppermute x1, waiting for transfers between devices: 6.59 us -> 21.9 us  [body(): lax.ppermute(join_weight.reshape(piece, -1), ('y', 'x'), [(y * 4 + x, x *...]
    all_to_all x3 -> x5, waiting for transfers between devices: 47.1 us -> 37.5 us  [exchange(): return lax.all_to_all(parts, 'x', split_axis=0, concat_axis=0, tiled=True)]
    unnamed x11 -> x29, local copies, waits for them, and re-layouts: 2.22 us -> 11.3 us
    all_to_all x3 -> x5, starting transfers between devices: 12.2 us -> 20.9 us  [exchange(): return lax.all_to_all(parts, 'x', split_axis=0, concat_axis=0, tiled=True)]
    ppermute x5 -> x6, starting transfers between devices: 9.41 us -> 12.9 us  [passed(): return lax.ppermute(array, ('dir', 'y', 'z'), pairs)]
  transfers between devices with their start and end apart: 12 -> 16, of which waited for: 5 -> 4; matrix products, arithmetic and copies ran while one was open for 1% -> 1% of each run, Pallas kernels for 11% -> 13%
where the time goes in v5:
time: 252 us; the launch traced here: 250 us
  starting transfers between devices  96.6 us (38%)
  waiting for transfers between devices  59.4 us (24%)
  Pallas kernels  35 us (14%)
  blocking collectives  31.3 us (12%)
  between operations  13.7 us (5%)
  local copies, waits for them, and re-layouts  11.3 us (4%)
  other arithmetic  3.07 us (1%)
    ppermute x3, starting transfers between devices, swapped(): return (mine, lax.ppermute(mine, 'dir', [(0, 1), (1, 0)]))  57.3 us
    all_to_all x5, waiting for transfers between devices, exchange(): return lax.all_to_all(parts, 'x', split_axis=0, concat_axis=0, tiled=True)  37.5 us
    all_to_all x1, blocking collectives, exchange(): return lax.all_to_all(parts, 'x', split_axis=0, concat_axis=0, tiled=True)  31.3 us
    ppermute x1, waiting for transfers between devices, body(): lax.ppermute(join_weight.reshape(piece, -1), ('y', 'x'), [(y * 4 + x, x *...  21.9 us
    all_to_all x5, starting transfers between devices, exchange(): return lax.all_to_all(parts, 'x', split_axis=0, concat_axis=0, tiled=True)  20.9 us
    pallas_call x3, Pallas kernels, attend(): pl.pallas_call(attend_kernel, grid=(rows,), in_specs=[pl.BlockSpec(memory...  13 us
    ppermute x6, starting transfers between devices, passed(): return lax.ppermute(array, ('dir', 'y', 'z'), pairs)  12.9 us
    pallas_call x3, Pallas kernels, join(): pl.pallas_call(join_kernel, grid_spec=pltpu.PrefetchScalarGridSpec(num_sc...  11.7 us
  transfers between devices with their start and end apart: 16, of which 4 were waited for; matrix products, arithmetic and copies ran while one was open for 1% of the time, Pallas kernels for 13%

profile of v5, /device:TPU:8, one launch (start us, length us, event | category | flops | bytes accessed | tf_op | source)
XLA Modules:
  0.0 250.5 jit_solution(1236702169945460819)
XLA Ops:
  6.5 2.7 %pack.3 = bf16[4,2,2,64,1024]{4,3,2,1,0:T(8,128)(2,1)} custom-call(bf16[1,4,64,4096]{3,2,1,0:T(8,128)(2,1)} %refs_0_.5, bf16[1,4,64,4096]{3,2,1,0:T(8,128)(2,1)} %refs_1_.3), custom_call_target="tpu_custom_call" | custom-call | flops 2000000000 | bytes 1 | tf_op jit(solution)/shard_map/pack/pallas_call | solution.py:83
  9.2 4.6 %all-to-all-start = ((bf16[4,2,2,64,1024]{4,3,2,1,0:T(8,128)(2,1)}), bf16[4,2,2,64,1024]{4,3,2,1,0:T(8,128)(2,1)}, u32[]{:S(2)}, u32[]{:S(2)}) async-start(bf16[4,2,2,64,1024]{4,3,2,1,0:T(8,128)(2,1)} %pack.3), calls=%async_computation | async-start | bytes 4194304 | tf_op jit(solution)/shard_map/all_to_all | solution.py:233
  13.9 0.0 all-gather.2.cloned.1.call-start
  13.9 5.4 %collective-permute-start = (bf16[64,1024]{1,0:T(8,128)(2,1)S(1)}, bf16[64,1024]{1,0:T(8,128)(2,1)S(1)}, u32[]{:S(2)}, u32[]{:S(2)}) collective-permute-start(bf16[64,1024]{1,0:T(8,128)(2,1)S(1)} %bitcast.16), channel_id=1, source_target_pairs={{0,0},{1,32},{2,64},{3,96},{32,1},{33,33},{34,65},{35,97},{64,2},{... | collective-permute-start | bytes 393224 | tf_op jit(solution)/shard_map/ppermute | solution.py:242
  19.4 21.9 %collective-permute-done.refs_2_ = bf16[64,1024]{1,0:T(8,128)(2,1)S(1)} collective-permute-done((bf16[64,1024]{1,0:T(8,128)(2,1)S(1)}, bf16[64,1024]{1,0:T(8,128)(2,1)S(1)}, u32[]{:S(2)}, u32[]{:S(2)}) %collective-permute-start) | collective-permute-done | bytes 131104 | tf_op jit(solution)/shard_map/ppermute | solution.py:242
  41.3 0.7 copy-done.8
  42.0 0.0 all-gather.2.cloned.1.call-update
  42.0 0.0 all-to-all-done.refs_1_.own_ref
  42.0 5.3 %collective-permute-start.2 = (bf16[4,2,2,64,1024]{4,3,2,1,0:T(8,128)(2,1)}, bf16[4,2,2,64,1024]{4,3,2,1,0:T(8,128)(2,1)S(1)}, u32[]{:S(2)}, u32[]{:S(2)}) collective-permute-start(bf16[4,2,2,64,1024]{4,3,2,1,0:T(8,128)(2,1)} %all-to-all-done.refs_1_.own_ref), channel_id=1, source_target_pairs={{0,4},{4,8},{8,12},{12,16},{16,20},{20,24},{24,28},{28,32},{32,36}... | collective-permute-start | bytes 6291464 | tf_op jit(solution)/shard_map/ppermute | solution.py:240
  47.3 0.0 copy-start.9
  47.3 0.9 copy-done.9
  48.2 3.8 %pack.4 = bf16[4,4,1,64,1024]{4,3,2,1,0:T(8,128)(2,1)} custom-call(bf16[1,4,64,4096]{3,2,1,0:T(8,128)(2,1)} %refs_0_.4, bf16[4,2,2,64,1024]{4,3,2,1,0:T(8,128)(2,1)} %all-to-all-done.refs_1_.own_ref, bf16[64,1024]{1,0:T(8,128)(2,1)S(1)} %copy-done.9), custom_call_target="tpu_custom_call" | custom-call | flops 2000000000 | bytes 1 | tf_op jit(solution)/shard_map/pack/pallas_call | solution.py:83
  52.0 31.3 %all_to_all.30.refs_2_.q_ref = bf16[4,4,1,64,1024]{4,3,2,1,0:T(8,128)(2,1)S(1)} all-to-all(bf16[4,4,1,64,1024]{4,3,2,1,0:T(8,128)(2,1)} %pack.4), channel_id=1, replica_groups=mesh['dir'=2,'y'=4,'z'=8,'x'=4] {'x'}, dimensions={0} | all-to-all | bytes 4194304 | tf_op jit(solution)/shard_map/all_to_all | solution.py:233
  83.3 2.0 collective-permute-start.1
  85.4 0.0 collective-permute-done.2.refs_3_.other_ref
  85.4 2.6 %pack.5 = bf16[4,2,2,64,1024]{4,3,2,1,0:T(8,128)(2,1)} custom-call(bf16[1,4,64,4096]{3,2,1,0:T(8,128)(2,1)} %refs_0_.5, bf16[1,4,64,4096]{3,2,1,0:T(8,128)(2,1)} %refs_1_.3, bf16[4,4,1,64,1024]{4,3,2,1,0:T(8,128)(2,1)S(1)} %all_to_all.30.refs_2_.q_ref, bf16[4,2,2,64,1024]{4,3,2,1,0:T(8,128)(2,1)S(1)} %collective-permute-done.2.refs_3_.other_ref), custom_call_target="tpu_custom_call" | custom-call | flops 2000000000 | bytes 1 | tf_op jit(solution)/shard_map/pack/pallas_call | solution.py:83
  88.0 1.3 copy-done.2
  89.3 4.6 %all-to-all-start.2 = ((bf16[4,2,2,64,1024]{4,3,2,1,0:T(8,128)(2,1)}), bf16[4,2,2,64,1024]{4,3,2,1,0:T(8,128)(2,1)}, u32[]{:S(2)}, u32[]{:S(2)}) async-start(bf16[4,2,2,64,1024]{4,3,2,1,0:T(8,128)(2,1)} %pack.5), calls=%async_computation.2 | async-start | bytes 4194304 | tf_op jit(solution)/shard_map/all_to_all | solution.py:233
  93.9 0.0 copy-done.10
  93.9 1.2 tables.1
  95.2 23.2 %all-to-all-done.2.refs_0_.own_ref = bf16[4,2,2,64,1024]{4,3,2,1,0:T(8,128)(2,1)} async-done(((bf16[4,2,2,64,1024]{4,3,2,1,0:T(8,128)(2,1)}), bf16[4,2,2,64,1024]{4,3,2,1,0:T(8,128)(2,1)}, u32[]{:S(2)}, u32[]{:S(2)}) %all-to-all-start.2) | async-done | bytes 2097184 | tf_op jit(solution)/shard_map/all_to_all | solution.py:233
  118.4 2.6 %collective-permute-start.5 = (bf16[4,2,2,64,1024]{4,3,2,1,0:T(8,128)(2,1)}, bf16[4,2,2,64,1024]{4,3,2,1,0:T(8,128)(2,1)S(1)}, u32[]{:S(2)}, u32[]{:S(2)}) collective-permute-start(bf16[4,2,2,64,1024]{4,3,2,1,0:T(8,128)(2,1)} %all-to-all-done.2.refs_0_.own_ref), channel_id=1, source_target_pairs={{0,4},{4,8},{8,12},{12,16},{16,20},{20,24},{24,28},{28,32},{32,36}... | collective-permute-start | bytes 6291464 | tf_op jit(solution)/shard_map/ppermute | solution.py:240
  121.0 0.0 collective-permute-done.1.next_q_ref
  121.0 1.6 copy-done.3
  122.6 5.0 %attend.3 = (bf16[2,256,1024]{2,1,0:T(8,128)(2,1)S(1)}, bf16[2,256,1024]{2,1,0:T(8,128)(2,1)S(1)}) custom-call(s32[1]{0:T(128)} %bitcast.side_ref, s32[4,1,512]{2,1,0:T(1,128)S(1)} %get-tuple-element.15.first_ref, s32[4,1,256]{2,1,0:T(1,128)S(1)} %get-tuple-element.16.here_ref, s32[4,1,256]{2,1,0:T(1,128)S(1)} %get-tuple-element.17.ahead_ref, ...), custom_call_target="tpu_custom_call" | custom-call | flops 20000000000 | bytes 1 | tf_op jit(solution)/shard_map/attend/pallas_call | solution.py:162
  127.6 0.7 collective-permute-start.3
  128.3 0.0 collective-permute-done.3
  128.3 0.4 add.29.mine_ref
  128.7 40.6 %collective-permute-start.4 = (bf16[2,256,1024]{2,1,0:T(8,128)(2,1)S(1)}, bf16[2,256,1024]{2,1,0:T(8,128)(2,1)S(1)}, u32[]{:S(2)}, u32[]{:S(2)}) collective-permute-start(bf16[2,256,1024]{2,1,0:T(8,128)(2,1)S(1)} %add.29.mine_ref), channel_id=1, source_target_pairs={{0,128},{128,0},{1,129},{129,1},{2,130},{130,2},{3,131},{131,3},{4... | collective-permute-start | bytes 3145736 | tf_op jit(solution)/shard_map/ppermute | solution.py:264
  169.3 0.0 collective-permute-done.5.other_ref
  169.3 4.9 %attend.4 = (bf16[1,256,1024]{2,1,0:T(8,128)(2,1)S(1)}, bf16[1,256,1024]{2,1,0:T(8,128)(2,1)}) custom-call(s32[1]{0:T(128)} %bitcast.side_ref, s32[4,1,512]{2,1,0:T(1,128)S(1)} %get-tuple-element.15.first_ref, s32[4,1,256]{2,1,0:T(1,128)S(1)} %get-tuple-element.16.here_ref, s32[4,1,256]{2,1,0:T(1,128)S(1)} %get-tuple-element.17.ahead_ref, ...), custom_call_target="tpu_custom_call" | custom-call | flops 10000000000 | bytes 1 | tf_op jit(solution)/shard_map/attend/pallas_call | solution.py:162
  174.2 0.8 copy-done.6
  175.0 1.5 collective-permute-start.6
  176.5 0.0 collective-permute-done.4.other_ref
  176.5 1.0 copy-done.4
  177.5 1.2 copy-done.5
  178.8 4.2 %join.3.refs_1_ = bf16[4,2,64,1024]{3,2,1,0:T(8,128)(2,1)S(1)} custom-call(s32[1]{0:T(128)} %bitcast.side_ref, bf16[2,256,1024]{2,1,0:T(8,128)(2,1)S(1)} %add.29.mine_ref, bf16[2,256,1024]{2,1,0:T(8,128)(2,1)S(1)} %copy-done.5, bf16[8,2,128,1024]{3,2,1,0:T(8,128)(2,1)} %bitcast.7, bf16[8,2,128,1024]{3,2,1,0:T(8,128)(2,1)} %bitcast.8), custom_call_target="tpu_custom_call" | custom-call | flops 1 | bytes 1 | tf_op jit(solution)/shard_map/join/pallas_call | solution.py:201
  182.9 1.0 copy-done
  183.9 3.7 %all-to-all-start.3 = ((bf16[4,2,64,1024]{3,2,1,0:T(8,128)(2,1)}), bf16[4,2,64,1024]{3,2,1,0:T(8,128)(2,1)S(1)}, u32[]{:S(2)}, u32[]{:S(2)}) async-start(bf16[4,2,64,1024]{3,2,1,0:T(8,128)(2,1)} %copy-done), calls=%async_computation.3 | async-start | bytes 2097152 | tf_op jit(solution)/shard_map/all_to_all | solution.py:233
  187.6 1.3 copy-done.1
  188.9 1.6 copy-done.12
  190.5 3.2 %attend.5 = (bf16[1,256,1024]{2,1,0:T(8,128)(2,1)S(1)}, bf16[1,256,1024]{2,1,0:T(8,128)(2,1)S(1)}) custom-call(s32[1]{0:T(128)} %bitcast.side_ref, s32[4,1,512]{2,1,0:T(1,128)S(1)} %get-tuple-element.15.first_ref, s32[4,1,256]{2,1,0:T(1,128)S(1)} %get-tuple-element.16.here_ref, s32[4,1,256]{2,1,0:T(1,128)S(1)} %get-tuple-element.17.ahead_ref, ...), custom_call_target="tpu_custom_call" | custom-call | flops 10000000000 | bytes 1 | tf_op jit(solution)/shard_map/attend/pallas_call | solution.py:162
  193.7 0.7 collective-permute-start.8
  194.4 0.0 collective-permute-done.6
  194.4 0.0 copy-done.7
  194.4 1.2 add.31.mine_ref
  195.6 7.9 %collective-permute-start.7 = (bf16[1,256,1024]{2,1,0:T(8,128)(2,1)S(1)}, bf16[1,256,1024]{2,1,0:T(8,128)(2,1)S(1)}, u32[]{:S(2)}, u32[]{:S(2)}) collective-permute-start(bf16[1,256,1024]{2,1,0:T(8,128)(2,1)S(1)} %add.31.mine_ref), channel_id=1, source_target_pairs={{0,128},{128,0},{1,129},{129,1},{2,130},{130,2},{3,131},{131,3},{4... | collective-permute-start | bytes 1572872 | tf_op jit(solution)/shard_map/ppermute | solution.py:264
  203.5 0.0 collective-permute-done.8
  203.5 0.2 add.33.mine_ref
  203.7 8.8 %collective-permute-start.9 = (bf16[1,256,1024]{2,1,0:T(8,128)(2,1)S(1)}, bf16[1,256,1024]{2,1,0:T(8,128)(2,1)S(1)}, u32[]{:S(2)}, u32[]{:S(2)}) collective-permute-start(bf16[1,256,1024]{2,1,0:T(8,128)(2,1)S(1)} %add.33.mine_ref), channel_id=1, source_target_pairs={{0,128},{128,0},{1,129},{129,1},{2,130},{130,2},{3,131},{131,3},{4... | collective-permute-start | bytes 1572872 | tf_op jit(solution)/shard_map/ppermute | solution.py:264
  212.6 0.0 collective-permute-done.7.other_ref
  212.6 3.7 %join.4.refs_0_ = bf16[4,1,64,1024]{3,2,1,0:T(8,128)(2,1)} custom-call(s32[1]{0:T(128)} %bitcast.side_ref, bf16[1,256,1024]{2,1,0:T(8,128)(2,1)S(1)} %add.31.mine_ref, bf16[1,256,1024]{2,1,0:T(8,128)(2,1)S(1)} %collective-permute-done.7.other_ref, bf16[8,2,128,1024]{3,2,1,0:T(8,128)(2,1)} %bitcast.9, bf16[8,2,128,1024]{3,2,1,0:T(8,128)(2,1)} %bitcast.10), custom_call_target="tpu_custom_call" | custom-call | flops 1 | bytes 1 | tf_op jit(solution)/shard_map/join/pallas_call | solution.py:201
  216.3 0.0 all-to-all-done.3
  216.3 4.5 %all-to-all-start.4 = ((bf16[4,1,64,1024]{3,2,1,0:T(8,128)(2,1)}), bf16[4,1,64,1024]{3,2,1,0:T(8,128)(2,1)S(1)}, u32[]{:S(2)}, u32[]{:S(2)}) async-start(bf16[4,1,64,1024]{3,2,1,0:T(8,128)(2,1)} %join.4.refs_0_), calls=%async_computation.4 | async-start | bytes 1048576 | tf_op jit(solution)/shard_map/all_to_all | solution.py:233
  220.8 0.2 convert_reduce_fusion
  221.0 0.0 collective-permute-done.9.other_ref
  221.0 3.8 %join.5 = bf16[4,1,64,1024]{3,2,1,0:T(8,128)(2,1)} custom-call(s32[1]{0:T(128)} %bitcast.side_ref, bf16[1,256,1024]{2,1,0:T(8,128)(2,1)S(1)} %add.33.mine_ref, bf16[1,256,1024]{2,1,0:T(8,128)(2,1)S(1)} %collective-permute-done.9.other_ref, bf16[8,2,128,1024]{3,2,1,0:T(8,128)(2,1)} %bitcast.11, bf16[8,2,128,1024]{3,2,1,0:T(8,128)(2,1)} %bitcast.12, ...), custom_call_target="tpu_custom_call" | custom-call | flops 1 | bytes 1 | tf_op jit(solution)/shard_map/join/pallas_call | solution.py:201
  224.8 5.7 %all-to-all-done.4 = bf16[4,1,64,1024]{3,2,1,0:T(8,128)(2,1)S(1)} async-done(((bf16[4,1,64,1024]{3,2,1,0:T(8,128)(2,1)}), bf16[4,1,64,1024]{3,2,1,0:T(8,128)(2,1)S(1)}, u32[]{:S(2)}, u32[]{:S(2)}) %all-to-all-start.4) | async-done | bytes 524320 | tf_op jit(solution)/shard_map/all_to_all | solution.py:233
  230.5 3.5 %all-to-all-start.5 = ((bf16[4,1,64,1024]{3,2,1,0:T(8,128)(2,1)}), bf16[4,1,64,1024]{3,2,1,0:T(8,128)(2,1)S(1)}, u32[]{:S(2)}, u32[]{:S(2)}) async-start(bf16[4,1,64,1024]{3,2,1,0:T(8,128)(2,1)} %join.5), calls=%async_computation.5 | async-start | bytes 1048576 | tf_op jit(solution)/shard_map/all_to_all | solution.py:233
  234.0 0.1 fusion
  234.1 0.1 convert_reduce_fusion.2
  234.2 8.5 %all-to-all-done.5 = bf16[4,1,64,1024]{3,2,1,0:T(8,128)(2,1)S(1)} async-done(((bf16[4,1,64,1024]{3,2,1,0:T(8,128)(2,1)}), bf16[4,1,64,1024]{3,2,1,0:T(8,128)(2,1)S(1)}, u32[]{:S(2)}, u32[]{:S(2)}) %all-to-all-start.5) | async-done | bytes 524320 | tf_op jit(solution)/shard_map/all_to_all | solution.py:233
  242.7 0.1 convert_reduce_fusion.1
  242.9 0.7 pad_maximum_fusion
  (19 shorter events, 0.1 us)
Async XLA Ops:
  9.2 4.7 %copy-start.13 = (bf16[64,2,512]{2,1,0:T(2,128)(2,1)S(1)}, bf16[64,2,512]{2,1,0:T(2,128)(2,1)}, u32[]{:S(2)}) copy-start(bf16[64,2,512]{2,1,0:T(2,128)(2,1)} %param.9) | copy-start | bytes 393220
  9.2 32.8 %all-to-all-start = ((bf16[4,2,2,64,1024]{4,3,2,1,0:T(8,128)(2,1)}), bf16[4,2,2,64,1024]{4,3,2,1,0:T(8,128)(2,1)}, u32[]{:S(2)}, u32[]{:S(2)}) async-start(bf16[4,2,2,64,1024]{4,3,2,1,0:T(8,128)(2,1)} %pack.3), calls=%async_computation | async-start | bytes 4194304 | tf_op jit(solution)/shard_map/all_to_all | solution.py:233
  13.9 163.7 %all-gather.2.cloned.1.call-start = ((), (), s32[]{:S(2)}) async-start(), calls=%async_computation.6 | async-start | bytes 4325376 | tf_op jit(solution)/shard_map/all_gather | solution.py:245
  13.9 27.4 %collective-permute-start = (bf16[64,1024]{1,0:T(8,128)(2,1)S(1)}, bf16[64,1024]{1,0:T(8,128)(2,1)S(1)}, u32[]{:S(2)}, u32[]{:S(2)}) collective-permute-start(bf16[64,1024]{1,0:T(8,128)(2,1)S(1)} %bitcast.16), channel_id=1, source_target_pairs={{0,0},{1,32},{2,64},{3,96},{32,1},{33,33},{34,65},{35,97},{64,2},{... | collective-permute-start | bytes 393224 | tf_op jit(solution)/shard_map/ppermute | solution.py:242
  41.3 0.7 copy-start.8
  42.0 43.4 %collective-permute-start.2 = (bf16[4,2,2,64,1024]{4,3,2,1,0:T(8,128)(2,1)}, bf16[4,2,2,64,1024]{4,3,2,1,0:T(8,128)(2,1)S(1)}, u32[]{:S(2)}, u32[]{:S(2)}) collective-permute-start(bf16[4,2,2,64,1024]{4,3,2,1,0:T(8,128)(2,1)} %all-to-all-done.refs_1_.own_ref), channel_id=1, source_target_pairs={{0,4},{4,8},{8,12},{12,16},{16,20},{20,24},{24,28},{28,32},{32,36}... | collective-permute-start | bytes 6291464 | tf_op jit(solution)/shard_map/ppermute | solution.py:240
  47.3 0.9 copy-start.9
  83.3 37.7 %collective-permute-start.1 = (bf16[4,4,1,64,1024]{4,3,2,1,0:T(8,128)(2,1)S(1)}, bf16[4,4,1,64,1024]{4,3,2,1,0:T(8,128)(2,1)}, u32[]{:S(2)}, u32[]{:S(2)}) collective-permute-start(bf16[4,4,1,64,1024]{4,3,2,1,0:T(8,128)(2,1)S(1)} %all_to_all.30.refs_2_.q_ref), channel_id=1, source_target_pairs={{132,128},{136,132},{140,136},{144,140},{148,144},{152,148},{156,1... | collective-permute-start | bytes 6291464 | tf_op jit(solution)/shard_map/ppermute | solution.py:240
  88.0 1.3 copy-start.2
  89.3 4.6 %copy-start.10 = (s32[4,512]{1,0:T(4,128)S(1)}, s32[4,512]{1,0:T(4,128)}, u32[]{:S(2)}) copy-start(s32[4,512]{1,0:T(4,128)} %lengths_ref.1) | copy-start | bytes 24580
  89.3 29.1 %all-to-all-start.2 = ((bf16[4,2,2,64,1024]{4,3,2,1,0:T(8,128)(2,1)}), bf16[4,2,2,64,1024]{4,3,2,1,0:T(8,128)(2,1)}, u32[]{:S(2)}, u32[]{:S(2)}) async-start(bf16[4,2,2,64,1024]{4,3,2,1,0:T(8,128)(2,1)} %pack.5), calls=%async_computation.2 | async-start | bytes 4194304 | tf_op jit(solution)/shard_map/all_to_all | solution.py:233
  118.4 51.0 %collective-permute-start.5 = (bf16[4,2,2,64,1024]{4,3,2,1,0:T(8,128)(2,1)}, bf16[4,2,2,64,1024]{4,3,2,1,0:T(8,128)(2,1)S(1)}, u32[]{:S(2)}, u32[]{:S(2)}) collective-permute-start(bf16[4,2,2,64,1024]{4,3,2,1,0:T(8,128)(2,1)} %all-to-all-done.2.refs_0_.own_ref), channel_id=1, source_target_pairs={{0,4},{4,8},{8,12},{12,16},{16,20},{20,24},{24,28},{28,32},{32,36}... | collective-permute-start | bytes 6291464 | tf_op jit(solution)/shard_map/ppermute | solution.py:240
  121.0 1.6 copy-start.3
  127.6 0.7 collective-permute-start.3
  128.7 47.8 %collective-permute-start.4 = (bf16[2,256,1024]{2,1,0:T(8,128)(2,1)S(1)}, bf16[2,256,1024]{2,1,0:T(8,128)(2,1)S(1)}, u32[]{:S(2)}, u32[]{:S(2)}) collective-permute-start(bf16[2,256,1024]{2,1,0:T(8,128)(2,1)S(1)} %add.29.mine_ref), channel_id=1, source_target_pairs={{0,128},{128,0},{1,129},{129,1},{2,130},{130,2},{3,131},{131,3},{4... | collective-permute-start | bytes 3145736 | tf_op jit(solution)/shard_map/ppermute | solution.py:264
  169.3 4.9 %copy-start.11 = (bf16[4,2,2,64,1024]{4,3,2,1,0:T(8,128)(2,1)}, bf16[4,2,2,64,1024]{4,3,2,1,0:T(8,128)(2,1)S(1)}, u32[]{:S(2)}) copy-start(bf16[4,2,2,64,1024]{4,3,2,1,0:T(8,128)(2,1)S(1)} %collective-permute-done.5.other_ref) | copy-start | bytes 6291460
  174.2 0.8 copy-start.6
  175.0 19.3 %collective-permute-start.6 = (bf16[1,256,1024]{2,1,0:T(8,128)(2,1)}, bf16[1,256,1024]{2,1,0:T(8,128)(2,1)}, u32[]{:S(2)}, u32[]{:S(2)}) collective-permute-start(bf16[1,256,1024]{2,1,0:T(8,128)(2,1)} %get-tuple-element.21.refs_0_), channel_id=1, source_target_pairs={{128,132},{132,136},{136,140},{140,144},{144,148},{148,152},{152,1... | collective-permute-start | bytes 1572872 | tf_op jit(solution)/shard_map/ppermute | solution.py:240
  176.5 1.0 copy-start.4
  177.5 1.2 copy-start.5
  182.9 1.0 copy-start
  183.9 32.4 %all-to-all-start.3 = ((bf16[4,2,64,1024]{3,2,1,0:T(8,128)(2,1)}), bf16[4,2,64,1024]{3,2,1,0:T(8,128)(2,1)S(1)}, u32[]{:S(2)}, u32[]{:S(2)}) async-start(bf16[4,2,64,1024]{3,2,1,0:T(8,128)(2,1)} %copy-done), calls=%async_computation.3 | async-start | bytes 2097152 | tf_op jit(solution)/shard_map/all_to_all | solution.py:233
  187.6 1.3 copy-start.1
  188.9 1.6 copy-start.12
  190.5 3.9 %copy-start.7 = (bf16[1,256,1024]{2,1,0:T(8,128)(2,1)S(1)}, bf16[1,256,1024]{2,1,0:T(8,128)(2,1)}, u32[]{:S(2)}) copy-start(bf16[1,256,1024]{2,1,0:T(8,128)(2,1)} %copy-done.6) | copy-start | bytes 1572868
  193.7 9.9 %collective-permute-start.8 = (bf16[1,256,1024]{2,1,0:T(8,128)(2,1)S(1)}, bf16[1,256,1024]{2,1,0:T(8,128)(2,1)S(1)}, u32[]{:S(2)}, u32[]{:S(2)}) collective-permute-start(bf16[1,256,1024]{2,1,0:T(8,128)(2,1)S(1)} %get-tuple-element.24), channel_id=1, source_target_pairs={{128,132},{132,136},{136,140},{140,144},{144,148},{148,152},{152,1... | collective-permute-start | bytes 1572872 | tf_op jit(solution)/shard_map/ppermute | solution.py:240
  195.6 16.9 %collective-permute-start.7 = (bf16[1,256,1024]{2,1,0:T(8,128)(2,1)S(1)}, bf16[1,256,1024]{2,1,0:T(8,128)(2,1)S(1)}, u32[]{:S(2)}, u32[]{:S(2)}) collective-permute-start(bf16[1,256,1024]{2,1,0:T(8,128)(2,1)S(1)} %add.31.mine_ref), channel_id=1, source_target_pairs={{0,128},{128,0},{1,129},{129,1},{2,130},{130,2},{3,131},{131,3},{4... | collective-permute-start | bytes 1572872 | tf_op jit(solution)/shard_map/ppermute | solution.py:264
  203.7 17.3 %collective-permute-start.9 = (bf16[1,256,1024]{2,1,0:T(8,128)(2,1)S(1)}, bf16[1,256,1024]{2,1,0:T(8,128)(2,1)S(1)}, u32[]{:S(2)}, u32[]{:S(2)}) collective-permute-start(bf16[1,256,1024]{2,1,0:T(8,128)(2,1)S(1)} %add.33.mine_ref), channel_id=1, source_target_pairs={{0,128},{128,0},{1,129},{129,1},{2,130},{130,2},{3,131},{131,3},{4... | collective-permute-start | bytes 1572872 | tf_op jit(solution)/shard_map/ppermute | solution.py:264
  216.3 14.2 %all-to-all-start.4 = ((bf16[4,1,64,1024]{3,2,1,0:T(8,128)(2,1)}), bf16[4,1,64,1024]{3,2,1,0:T(8,128)(2,1)S(1)}, u32[]{:S(2)}, u32[]{:S(2)}) async-start(bf16[4,1,64,1024]{3,2,1,0:T(8,128)(2,1)} %join.4.refs_0_), calls=%async_computation.4 | async-start | bytes 1048576 | tf_op jit(solution)/shard_map/all_to_all | solution.py:233
  230.5 12.2 %all-to-all-start.5 = ((bf16[4,1,64,1024]{3,2,1,0:T(8,128)(2,1)}), bf16[4,1,64,1024]{3,2,1,0:T(8,128)(2,1)S(1)}, u32[]{:S(2)}, u32[]{:S(2)}) async-start(bf16[4,1,64,1024]{3,2,1,0:T(8,128)(2,1)} %join.5), calls=%async_computation.5 | async-start | bytes 1048576 | tf_op jit(solution)/shard_map/all_to_all | solution.py:233
Sparse Core Ops, SparseCore 0:
  42.1 98.3 all-gather.1

commit v6 on v5

--- a/solution.py
+++ b/solution.py
@@ -12,7 +12,7 @@
 SPAN = 256
 HALF = SPAN // 2
 RINGS = 32
-LONG = 10**10
+LONG = 1
 CHUNKS = ((0, 2), (2, 4))
 NT = (((1,), (1,)), ((), ()))
 NN = (((1,), (0,)), ((), ()))
@@ -251,10 +251,10 @@
     both = (key_states, value_vectors)
     own_early = exchange(pack(both, CHUNKS[0], pieces))
     other_early = passed(own_early, outward)
-    q = exchange(pack((queries,), (0, rows), pieces, (own_early, turned)))
+    own_late = exchange(pack(both, CHUNKS[1], pieces, (own_early, turned)))
+    other_late = passed(own_late, outward)
+    q = exchange(pack((queries,), (0, rows), pieces, (own_late, other_early)))
     next_q = passed(q, to_left)
-    own_late = exchange(pack(both, CHUNKS[1], pieces, (q, other_early)))
-    other_late = passed(own_late, outward)
 
     def contexts(own, other, chunk, low, after=(), weight=LONG):
         return attend(side[None], *lines, q, next_q, own, other, chunk, low, after, weight)
@@ -270,7 +270,7 @@
         total = jnp.sum(arrived.astype(jnp.float32), axis=0)
         return (jax.nn.silu(total[..., : units // 2]) * total[..., units // 2 :]).astype(jnp.bfloat16)
 
-    early = contexts(own_early, other_early, (0, 2), 0, (own_late,))
+    early = contexts(own_early, other_early, (0, 2), 0, (other_late,))
     late = contexts(own_late, other_late, (2, 3), 2, (early[1],))
     partial_early = joined_part(*swapped(*early))
     last = contexts(own_late, other_late, (3, 4), 2, (late[1], partial_early))

time: 252 us -> 272 us (1.079)
  waiting for transfers between devices: 59.4 us -> 78.3 us
  starting transfers between devices: 96.6 us -> 104 us
  local copies, waits for them, and re-layouts: 11.3 us -> 5.28 us
    ppermute x6, waiting for transfers between devices: 0.02 us -> 17.9 us  [passed(): return lax.ppermute(array, ('dir', 'y', 'z'), pairs)]
    ppermute x3, starting transfers between devices: 57.3 us -> 64.5 us  [swapped(): return (mine, lax.ppermute(mine, 'dir', [(0, 1), (1, 0)]))]
    unnamed x29 -> x17, local copies, waits for them, and re-layouts: 11.3 us -> 5.28 us
  transfers between devices with their start and end apart: 16 -> 16, of which waited for: 4 -> 5; matrix products, arithmetic and copies ran while one was open for 1% -> 1% of each run, Pallas kernels for 13% -> 12%
where the time goes in v6:
time: 272 us; the launch traced here: 271 us
  starting transfers between devices  104 us (38%)
  waiting for transfers between devices  78.3 us (29%)
  Pallas kernels  35.9 us (13%)
  blocking collectives  31.3 us (12%)
  between operations  13.6 us (5%)
  local copies, waits for them, and re-layouts  5.28 us (2%)
  other arithmetic  3.07 us (1%)
    ppermute x3, starting transfers between devices, swapped(): return (mine, lax.ppermute(mine, 'dir', [(0, 1), (1, 0)]))  64.5 us
    all_to_all x5, waiting for transfers between devices, exchange(): return lax.all_to_all(parts, 'x', split_axis=0, concat_axis=0, tiled=True)  38.4 us
    all_to_all x1, blocking collectives, exchange(): return lax.all_to_all(parts, 'x', split_axis=0, concat_axis=0, tiled=True)  31.3 us
    ppermute x1, waiting for transfers between devices, body(): lax.ppermute(join_weight.reshape(piece, -1), ('y', 'x'), [(y * 4 + x, x *...  22 us
    all_to_all x5, starting transfers between devices, exchange(): return lax.all_to_all(parts, 'x', split_axis=0, concat_axis=0, tiled=True)  21.4 us
    ppermute x6, waiting for transfers between devices, passed(): return lax.ppermute(array, ('dir', 'y', 'z'), pairs)  17.9 us
    pallas_call x3, Pallas kernels, join(): pl.pallas_call(join_kernel, grid_spec=pltpu.PrefetchScalarGridSpec(num_sc...  12.8 us
    pallas_call x3, Pallas kernels, attend(): pl.pallas_call(attend_kernel, grid=(rows,), in_specs=[pl.BlockSpec(memory...  12.8 us
  transfers between devices with their start and end apart: 16, of which 5 were waited for; matrix products, arithmetic and copies ran while one was open for 1% of the time, Pallas kernels for 12%

profile of v6, /device:TPU:8, one launch (start us, length us, event | category | flops | bytes accessed | tf_op | source)
XLA Modules:
  0.0 271.2 jit_solution(8214045696161410799)
XLA Ops:
  6.5 2.6 pack.3
  9.2 0.0 copy-start.7
  9.2 4.6 %all-to-all-start = ((bf16[4,2,2,64,1024]{4,3,2,1,0:T(8,128)(2,1)}), bf16[4,2,2,64,1024]{4,3,2,1,0:T(8,128)(2,1)}, u32[]{:S(2)}, u32[]{:S(2)}) async-start(bf16[4,2,2,64,1024]{4,3,2,1,0:T(8,128)(2,1)} %pack.3), calls=%async_computation | async-start | bytes 4194304 | tf_op jit(solution)/shard_map/all_to_all | solution.py:233
  13.8 0.0 all-gather.2.cloned.1.call-start
  13.8 0.0 copy-done.7
  13.9 5.4 %collective-permute-start = (bf16[64,1024]{1,0:T(8,128)(2,1)S(1)}, bf16[64,1024]{1,0:T(8,128)(2,1)S(1)}, u32[]{:S(2)}, u32[]{:S(2)}) collective-permute-start(bf16[64,1024]{1,0:T(8,128)(2,1)S(1)} %bitcast.16), channel_id=1, source_target_pairs={{0,0},{1,32},{2,64},{3,96},{32,1},{33,33},{34,65},{35,97},{64,2},{... | collective-permute-start | bytes 393224 | tf_op jit(solution)/shard_map/ppermute | solution.py:242
  19.3 22.0 %collective-permute-done.refs_3_ = bf16[64,1024]{1,0:T(8,128)(2,1)S(1)} collective-permute-done((bf16[64,1024]{1,0:T(8,128)(2,1)S(1)}, bf16[64,1024]{1,0:T(8,128)(2,1)S(1)}, u32[]{:S(2)}, u32[]{:S(2)}) %collective-permute-start) | collective-permute-done | bytes 131104 | tf_op jit(solution)/shard_map/ppermute | solution.py:242
  41.3 0.0 copy-start.2
  41.3 0.7 copy-done.2
  42.0 0.0 all-gather.2.cloned.1.call-update
  42.0 0.0 all-to-all-done.refs_2_.own_ref
  42.0 5.2 %collective-permute-start.1 = (bf16[4,2,2,64,1024]{4,3,2,1,0:T(8,128)(2,1)}, bf16[4,2,2,64,1024]{4,3,2,1,0:T(8,128)(2,1)S(1)}, u32[]{:S(2)}, u32[]{:S(2)}) collective-permute-start(bf16[4,2,2,64,1024]{4,3,2,1,0:T(8,128)(2,1)} %all-to-all-done.refs_2_.own_ref), channel_id=1, source_target_pairs={{0,4},{4,8},{8,12},{12,16},{16,20},{20,24},{24,28},{28,32},{32,36}... | collective-permute-start | bytes 6291464 | tf_op jit(solution)/shard_map/ppermute | solution.py:240
  47.2 0.0 copy-start.3
  47.3 0.9 copy-done.3
  48.1 2.6 pack.4
  50.8 31.3 %all_to_all.30.refs_1_.own_ref = bf16[4,2,2,64,1024]{4,3,2,1,0:T(8,128)(2,1)S(1)} all-to-all(bf16[4,2,2,64,1024]{4,3,2,1,0:T(8,128)(2,1)} %pack.4), channel_id=1, replica_groups=mesh['dir'=2,'y'=4,'z'=8,'x'=4] {'x'}, dimensions={0} | all-to-all | bytes 4194304 | tf_op jit(solution)/shard_map/all_to_all | solution.py:233
  82.1 0.0 collective-permute-done.1.refs_2_.other_ref
  82.1 3.8 %pack.5 = bf16[4,4,1,64,1024]{4,3,2,1,0:T(8,128)(2,1)} custom-call(bf16[1,4,64,4096]{3,2,1,0:T(8,128)(2,1)} %refs_0_.5, bf16[4,2,2,64,1024]{4,3,2,1,0:T(8,128)(2,1)S(1)} %all_to_all.30.refs_1_.own_ref, bf16[4,2,2,64,1024]{4,3,2,1,0:T(8,128)(2,1)S(1)} %collective-permute-done.1.refs_2_.other_ref), custom_call_target="tpu_custom_call" | custom-call | flops 2000000000 | bytes 1 | tf_op jit(solution)/shard_map/pack/pallas_call | solution.py:83
  85.9 0.0 copy-start
  85.9 1.3 copy-done
  87.2 0.0 copy-start.6
  87.2 4.6 %all-to-all-start.2 = ((bf16[4,4,1,64,1024]{4,3,2,1,0:T(8,128)(2,1)}), bf16[4,4,1,64,1024]{4,3,2,1,0:T(8,128)(2,1)}, u32[]{:S(2)}, u32[]{:S(2)}) async-start(bf16[4,4,1,64,1024]{4,3,2,1,0:T(8,128)(2,1)} %pack.5), calls=%async_computation.2 | async-start | bytes 4194304 | tf_op jit(solution)/shard_map/all_to_all | solution.py:233
  91.8 2.2 collective-permute-start.3
  94.0 24.2 %all-to-all-done.2.q_ref = bf16[4,4,1,64,1024]{4,3,2,1,0:T(8,128)(2,1)} async-done(((bf16[4,4,1,64,1024]{4,3,2,1,0:T(8,128)(2,1)}), bf16[4,4,1,64,1024]{4,3,2,1,0:T(8,128)(2,1)}, u32[]{:S(2)}, u32[]{:S(2)}) %all-to-all-start.2) | async-done | bytes 2097184 | tf_op jit(solution)/shard_map/all_to_all | solution.py:233
  118.2 2.0 collective-permute-start.2
  120.2 0.0 copy-done.6
  120.2 1.2 tables.1
  121.4 17.9 %collective-permute-done.3.refs_0_.other_ref = bf16[4,2,2,64,1024]{4,3,2,1,0:T(8,128)(2,1)} collective-permute-done((bf16[4,2,2,64,1024]{4,3,2,1,0:T(8,128)(2,1)S(1)}, bf16[4,2,2,64,1024]{4,3,2,1,0:T(8,128)(2,1)}, u32[]{:S(2)}, u32[]{:S(2)}) %collective-permute-start.3) | collective-permute-done | bytes 2097184 | tf_op jit(solution)/shard_map/ppermute | solution.py:240
  139.3 0.0 collective-permute-done.2.next_q_ref
  139.3 1.6 copy-done.1
  140.9 5.1 %attend.3 = (bf16[2,256,1024]{2,1,0:T(8,128)(2,1)S(1)}, bf16[2,256,1024]{2,1,0:T(8,128)(2,1)S(1)}) custom-call(s32[1]{0:T(128)} %bitcast.side_ref, s32[4,1,512]{2,1,0:T(1,128)S(1)} %get-tuple-element.15.first_ref, s32[4,1,256]{2,1,0:T(1,128)S(1)} %get-tuple-element.16.here_ref, s32[4,1,256]{2,1,0:T(1,128)S(1)} %get-tuple-element.17.ahead_ref, ...), custom_call_target="tpu_custom_call" | custom-call | flops 2 | bytes 1 | tf_op jit(solution)/shard_map/attend/pallas_call | solution.py:162
  146.0 0.7 collective-permute-start.4
  146.7 0.0 collective-permute-done.4
  146.7 0.4 add.29.mine_ref
  147.1 47.8 %collective-permute-start.5 = (bf16[2,256,1024]{2,1,0:T(8,128)(2,1)S(1)}, bf16[2,256,1024]{2,1,0:T(8,128)(2,1)}, u32[]{:S(2)}, u32[]{:S(2)}) collective-permute-start(bf16[2,256,1024]{2,1,0:T(8,128)(2,1)S(1)} %add.29.mine_ref), channel_id=1, source_target_pairs={{0,128},{128,0},{1,129},{129,1},{2,130},{130,2},{3,131},{131,3},{4... | collective-permute-start | bytes 3145736 | tf_op jit(solution)/shard_map/ppermute | solution.py:264
  195.0 4.3 %attend.4 = (bf16[1,256,1024]{2,1,0:T(8,128)(2,1)S(1)}, bf16[1,256,1024]{2,1,0:T(8,128)(2,1)}) custom-call(s32[1]{0:T(128)} %bitcast.side_ref, s32[4,1,512]{2,1,0:T(1,128)S(1)} %get-tuple-element.15.first_ref, s32[4,1,256]{2,1,0:T(1,128)S(1)} %get-tuple-element.16.here_ref, s32[4,1,256]{2,1,0:T(1,128)S(1)} %get-tuple-element.17.ahead_ref, ...), custom_call_target="tpu_custom_call" | custom-call | flops 1 | bytes 1 | tf_op jit(solution)/shard_map/attend/pallas_call | solution.py:162
  199.3 0.8 copy-done.4
  200.1 1.5 collective-permute-start.6
  201.6 0.0 collective-permute-done.5.other_ref
  201.6 5.3 %join.3.refs_1_ = bf16[4,2,64,1024]{3,2,1,0:T(8,128)(2,1)} custom-call(s32[1]{0:T(128)} %bitcast.side_ref, bf16[2,256,1024]{2,1,0:T(8,128)(2,1)S(1)} %add.29.mine_ref, bf16[2,256,1024]{2,1,0:T(8,128)(2,1)} %collective-permute-done.5.other_ref, bf16[8,2,128,1024]{3,2,1,0:T(8,128)(2,1)} %bitcast.7, bf16[8,2,128,1024]{3,2,1,0:T(8,128)(2,1)} %bitcast.8), custom_call_target="tpu_custom_call" | custom-call | flops 1 | bytes 1 | tf_op jit(solution)/shard_map/join/pallas_call | solution.py:201
  206.8 4.2 %all-to-all-start.3 = ((bf16[4,2,64,1024]{3,2,1,0:T(8,128)(2,1)}), bf16[4,2,64,1024]{3,2,1,0:T(8,128)(2,1)S(1)}, u32[]{:S(2)}, u32[]{:S(2)}) async-start(bf16[4,2,64,1024]{3,2,1,0:T(8,128)(2,1)} %join.3.refs_1_), calls=%async_computation.3 | async-start | bytes 2097152 | tf_op jit(solution)/shard_map/all_to_all | solution.py:233
  211.1 3.4 %attend.5 = (bf16[1,256,1024]{2,1,0:T(8,128)(2,1)S(1)}, bf16[1,256,1024]{2,1,0:T(8,128)(2,1)S(1)}) custom-call(s32[1]{0:T(128)} %bitcast.side_ref, s32[4,1,512]{2,1,0:T(1,128)S(1)} %get-tuple-element.15.first_ref, s32[4,1,256]{2,1,0:T(1,128)S(1)} %get-tuple-element.16.here_ref, s32[4,1,256]{2,1,0:T(1,128)S(1)} %get-tuple-element.17.ahead_ref, ...), custom_call_target="tpu_custom_call" | custom-call | flops 1 | bytes 1 | tf_op jit(solution)/shard_map/attend/pallas_call | solution.py:162
  214.5 0.7 collective-permute-start.8
  215.2 0.0 collective-permute-done.6
  215.2 0.0 copy-done.5
  215.2 1.2 add.31.mine_ref
  216.4 7.8 %collective-permute-start.7 = (bf16[1,256,1024]{2,1,0:T(8,128)(2,1)S(1)}, bf16[1,256,1024]{2,1,0:T(8,128)(2,1)S(1)}, u32[]{:S(2)}, u32[]{:S(2)}) collective-permute-start(bf16[1,256,1024]{2,1,0:T(8,128)(2,1)S(1)} %add.31.mine_ref), channel_id=1, source_target_pairs={{0,128},{128,0},{1,129},{129,1},{2,130},{130,2},{3,131},{131,3},{4... | collective-permute-start | bytes 1572872 | tf_op jit(solution)/shard_map/ppermute | solution.py:264
  224.2 0.0 collective-permute-done.8
  224.2 0.2 add.33.mine_ref
  224.4 8.8 %collective-permute-start.9 = (bf16[1,256,1024]{2,1,0:T(8,128)(2,1)S(1)}, bf16[1,256,1024]{2,1,0:T(8,128)(2,1)S(1)}, u32[]{:S(2)}, u32[]{:S(2)}) collective-permute-start(bf16[1,256,1024]{2,1,0:T(8,128)(2,1)S(1)} %add.33.mine_ref), channel_id=1, source_target_pairs={{0,128},{128,0},{1,129},{129,1},{2,130},{130,2},{3,131},{131,3},{4... | collective-permute-start | bytes 1572872 | tf_op jit(solution)/shard_map/ppermute | solution.py:264
  233.3 0.0 collective-permute-done.7.other_ref
  233.3 3.7 %join.4.refs_0_ = bf16[4,1,64,1024]{3,2,1,0:T(8,128)(2,1)} custom-call(s32[1]{0:T(128)} %bitcast.side_ref, bf16[1,256,1024]{2,1,0:T(8,128)(2,1)S(1)} %add.31.mine_ref, bf16[1,256,1024]{2,1,0:T(8,128)(2,1)S(1)} %collective-permute-done.7.other_ref, bf16[8,2,128,1024]{3,2,1,0:T(8,128)(2,1)} %bitcast.9, bf16[8,2,128,1024]{3,2,1,0:T(8,128)(2,1)} %bitcast.10), custom_call_target="tpu_custom_call" | custom-call | flops 1 | bytes 1 | tf_op jit(solution)/shard_map/join/pallas_call | solution.py:201
  237.0 0.0 all-to-all-done.3
  237.0 4.5 %all-to-all-start.4 = ((bf16[4,1,64,1024]{3,2,1,0:T(8,128)(2,1)}), bf16[4,1,64,1024]{3,2,1,0:T(8,128)(2,1)S(1)}, u32[]{:S(2)}, u32[]{:S(2)}) async-start(bf16[4,1,64,1024]{3,2,1,0:T(8,128)(2,1)} %join.4.refs_0_), calls=%async_computation.4 | async-start | bytes 1048576 | tf_op jit(solution)/shard_map/all_to_all | solution.py:233
  241.6 0.2 convert_reduce_fusion
  241.7 0.0 collective-permute-done.9.other_ref
  241.8 3.8 %join.5 = bf16[4,1,64,1024]{3,2,1,0:T(8,128)(2,1)} custom-call(s32[1]{0:T(128)} %bitcast.side_ref, bf16[1,256,1024]{2,1,0:T(8,128)(2,1)S(1)} %add.33.mine_ref, bf16[1,256,1024]{2,1,0:T(8,128)(2,1)S(1)} %collective-permute-done.9.other_ref, bf16[8,2,128,1024]{3,2,1,0:T(8,128)(2,1)} %bitcast.11, bf16[8,2,128,1024]{3,2,1,0:T(8,128)(2,1)} %bitcast.12, ...), custom_call_target="tpu_custom_call" | custom-call | flops 1 | bytes 1 | tf_op jit(solution)/shard_map/join/pallas_call | solution.py:201
  245.5 5.7 %all-to-all-done.4 = bf16[4,1,64,1024]{3,2,1,0:T(8,128)(2,1)S(1)} async-done(((bf16[4,1,64,1024]{3,2,1,0:T(8,128)(2,1)}), bf16[4,1,64,1024]{3,2,1,0:T(8,128)(2,1)S(1)}, u32[]{:S(2)}, u32[]{:S(2)}) %all-to-all-start.4) | async-done | bytes 524320 | tf_op jit(solution)/shard_map/all_to_all | solution.py:233
  251.2 3.5 %all-to-all-start.5 = ((bf16[4,1,64,1024]{3,2,1,0:T(8,128)(2,1)}), bf16[4,1,64,1024]{3,2,1,0:T(8,128)(2,1)S(1)}, u32[]{:S(2)}, u32[]{:S(2)}) async-start(bf16[4,1,64,1024]{3,2,1,0:T(8,128)(2,1)} %join.5), calls=%async_computation.5 | async-start | bytes 1048576 | tf_op jit(solution)/shard_map/all_to_all | solution.py:233
  254.7 0.1 fusion
  254.8 0.1 convert_reduce_fusion.2
  254.9 8.5 %all-to-all-done.5 = bf16[4,1,64,1024]{3,2,1,0:T(8,128)(2,1)S(1)} async-done(((bf16[4,1,64,1024]{3,2,1,0:T(8,128)(2,1)}), bf16[4,1,64,1024]{3,2,1,0:T(8,128)(2,1)S(1)}, u32[]{:S(2)}, u32[]{:S(2)}) %all-to-all-start.5) | async-done | bytes 524320 | tf_op jit(solution)/shard_map/all_to_all | solution.py:233
  263.5 0.1 convert_reduce_fusion.1
  263.6 0.7 pad_maximum_fusion
  (7 shorter events, 0.1 us)
Async XLA Ops:
  9.2 4.6 %copy-start.7 = (bf16[64,2,512]{2,1,0:T(2,128)(2,1)S(1)}, bf16[64,2,512]{2,1,0:T(2,128)(2,1)}, u32[]{:S(2)}) copy-start(bf16[64,2,512]{2,1,0:T(2,128)(2,1)} %param.9) | copy-start | bytes 393220
  9.2 32.8 %all-to-all-start = ((bf16[4,2,2,64,1024]{4,3,2,1,0:T(8,128)(2,1)}), bf16[4,2,2,64,1024]{4,3,2,1,0:T(8,128)(2,1)}, u32[]{:S(2)}, u32[]{:S(2)}) async-start(bf16[4,2,2,64,1024]{4,3,2,1,0:T(8,128)(2,1)} %pack.3), calls=%async_computation | async-start | bytes 4194304 | tf_op jit(solution)/shard_map/all_to_all | solution.py:233
  13.8 187.8 %all-gather.2.cloned.1.call-start = ((), (), s32[]{:S(2)}) async-start(), calls=%async_computation.6 | async-start | bytes 4325376 | tf_op jit(solution)/shard_map/all_gather | solution.py:245
  13.9 27.4 %collective-permute-start = (bf16[64,1024]{1,0:T(8,128)(2,1)S(1)}, bf16[64,1024]{1,0:T(8,128)(2,1)S(1)}, u32[]{:S(2)}, u32[]{:S(2)}) collective-permute-start(bf16[64,1024]{1,0:T(8,128)(2,1)S(1)} %bitcast.16), channel_id=1, source_target_pairs={{0,0},{1,32},{2,64},{3,96},{32,1},{33,33},{34,65},{35,97},{64,2},{... | collective-permute-start | bytes 393224 | tf_op jit(solution)/shard_map/ppermute | solution.py:242
  41.3 0.7 copy-start.2
  42.0 40.1 %collective-permute-start.1 = (bf16[4,2,2,64,1024]{4,3,2,1,0:T(8,128)(2,1)}, bf16[4,2,2,64,1024]{4,3,2,1,0:T(8,128)(2,1)S(1)}, u32[]{:S(2)}, u32[]{:S(2)}) collective-permute-start(bf16[4,2,2,64,1024]{4,3,2,1,0:T(8,128)(2,1)} %all-to-all-done.refs_2_.own_ref), channel_id=1, source_target_pairs={{0,4},{4,8},{8,12},{12,16},{16,20},{20,24},{24,28},{28,32},{32,36}... | collective-permute-start | bytes 6291464 | tf_op jit(solution)/shard_map/ppermute | solution.py:240
  47.2 0.9 copy-start.3
  85.9 1.3 copy-start
  87.2 33.0 %copy-start.6 = (s32[4,512]{1,0:T(4,128)S(1)}, s32[4,512]{1,0:T(4,128)}, u32[]{:S(2)}) copy-start(s32[4,512]{1,0:T(4,128)} %lengths_ref.1) | copy-start | bytes 24580
  87.2 31.0 %all-to-all-start.2 = ((bf16[4,4,1,64,1024]{4,3,2,1,0:T(8,128)(2,1)}), bf16[4,4,1,64,1024]{4,3,2,1,0:T(8,128)(2,1)}, u32[]{:S(2)}, u32[]{:S(2)}) async-start(bf16[4,4,1,64,1024]{4,3,2,1,0:T(8,128)(2,1)} %pack.5), calls=%async_computation.2 | async-start | bytes 4194304 | tf_op jit(solution)/shard_map/all_to_all | solution.py:233
  91.8 47.5 %collective-permute-start.3 = (bf16[4,2,2,64,1024]{4,3,2,1,0:T(8,128)(2,1)S(1)}, bf16[4,2,2,64,1024]{4,3,2,1,0:T(8,128)(2,1)}, u32[]{:S(2)}, u32[]{:S(2)}) collective-permute-start(bf16[4,2,2,64,1024]{4,3,2,1,0:T(8,128)(2,1)S(1)} %all_to_all.30.refs_1_.own_ref), channel_id=1, source_target_pairs={{0,4},{4,8},{8,12},{12,16},{16,20},{20,24},{24,28},{28,32},{32,36}... | collective-permute-start | bytes 6291464 | tf_op jit(solution)/shard_map/ppermute | solution.py:240
  118.2 21.1 %collective-permute-start.2 = (bf16[4,4,1,64,1024]{4,3,2,1,0:T(8,128)(2,1)}, bf16[4,4,1,64,1024]{4,3,2,1,0:T(8,128)(2,1)}, u32[]{:S(2)}, u32[]{:S(2)}) collective-permute-start(bf16[4,4,1,64,1024]{4,3,2,1,0:T(8,128)(2,1)} %all-to-all-done.2.q_ref), channel_id=1, source_target_pairs={{132,128},{136,132},{140,136},{144,140},{148,144},{152,148},{156,1... | collective-permute-start | bytes 6291464 | tf_op jit(solution)/shard_map/ppermute | solution.py:240
  139.3 1.6 copy-start.1
  146.0 0.7 collective-permute-start.4
  147.1 54.4 %collective-permute-start.5 = (bf16[2,256,1024]{2,1,0:T(8,128)(2,1)S(1)}, bf16[2,256,1024]{2,1,0:T(8,128)(2,1)}, u32[]{:S(2)}, u32[]{:S(2)}) collective-permute-start(bf16[2,256,1024]{2,1,0:T(8,128)(2,1)S(1)} %add.29.mine_ref), channel_id=1, source_target_pairs={{0,128},{128,0},{1,129},{129,1},{2,130},{130,2},{3,131},{131,3},{4... | collective-permute-start | bytes 3145736 | tf_op jit(solution)/shard_map/ppermute | solution.py:264
  199.3 0.8 copy-start.4
  200.1 15.1 %collective-permute-start.6 = (bf16[1,256,1024]{2,1,0:T(8,128)(2,1)}, bf16[1,256,1024]{2,1,0:T(8,128)(2,1)}, u32[]{:S(2)}, u32[]{:S(2)}) collective-permute-start(bf16[1,256,1024]{2,1,0:T(8,128)(2,1)} %get-tuple-element.21.refs_0_), channel_id=1, source_target_pairs={{128,132},{132,136},{136,140},{140,144},{144,148},{148,152},{152,1... | collective-permute-start | bytes 1572872 | tf_op jit(solution)/shard_map/ppermute | solution.py:240
  206.8 30.2 %all-to-all-start.3 = ((bf16[4,2,64,1024]{3,2,1,0:T(8,128)(2,1)}), bf16[4,2,64,1024]{3,2,1,0:T(8,128)(2,1)S(1)}, u32[]{:S(2)}, u32[]{:S(2)}) async-start(bf16[4,2,64,1024]{3,2,1,0:T(8,128)(2,1)} %join.3.refs_1_), calls=%async_computation.3 | async-start | bytes 2097152 | tf_op jit(solution)/shard_map/all_to_all | solution.py:233
  211.1 4.1 %copy-start.5 = (bf16[1,256,1024]{2,1,0:T(8,128)(2,1)S(1)}, bf16[1,256,1024]{2,1,0:T(8,128)(2,1)}, u32[]{:S(2)}) copy-start(bf16[1,256,1024]{2,1,0:T(8,128)(2,1)} %copy-done.4) | copy-start | bytes 1572868
  214.5 9.8 %collective-permute-start.8 = (bf16[1,256,1024]{2,1,0:T(8,128)(2,1)S(1)}, bf16[1,256,1024]{2,1,0:T(8,128)(2,1)S(1)}, u32[]{:S(2)}, u32[]{:S(2)}) collective-permute-start(bf16[1,256,1024]{2,1,0:T(8,128)(2,1)S(1)} %get-tuple-element.24), channel_id=1, source_target_pairs={{128,132},{132,136},{136,140},{140,144},{144,148},{148,152},{152,1... | collective-permute-start | bytes 1572872 | tf_op jit(solution)/shard_map/ppermute | solution.py:240
  216.4 16.9 %collective-permute-start.7 = (bf16[1,256,1024]{2,1,0:T(8,128)(2,1)S(1)}, bf16[1,256,1024]{2,1,0:T(8,128)(2,1)S(1)}, u32[]{:S(2)}, u32[]{:S(2)}) collective-permute-start(bf16[1,256,1024]{2,1,0:T(8,128)(2,1)S(1)} %add.31.mine_ref), channel_id=1, source_target_pairs={{0,128},{128,0},{1,129},{129,1},{2,130},{130,2},{3,131},{131,3},{4... | collective-permute-start | bytes 1572872 | tf_op jit(solution)/shard_map/ppermute | solution.py:264
  224.4 17.3 %collective-permute-start.9 = (bf16[1,256,1024]{2,1,0:T(8,128)(2,1)S(1)}, bf16[1,256,1024]{2,1,0:T(8,128)(2,1)S(1)}, u32[]{:S(2)}, u32[]{:S(2)}) collective-permute-start(bf16[1,256,1024]{2,1,0:T(8,128)(2,1)S(1)} %add.33.mine_ref), channel_id=1, source_target_pairs={{0,128},{128,0},{1,129},{129,1},{2,130},{130,2},{3,131},{131,3},{4... | collective-permute-start | bytes 1572872 | tf_op jit(solution)/shard_map/ppermute | solution.py:264
  237.0 14.2 %all-to-all-start.4 = ((bf16[4,1,64,1024]{3,2,1,0:T(8,128)(2,1)}), bf16[4,1,64,1024]{3,2,1,0:T(8,128)(2,1)S(1)}, u32[]{:S(2)}, u32[]{:S(2)}) async-start(bf16[4,1,64,1024]{3,2,1,0:T(8,128)(2,1)} %join.4.refs_0_), calls=%async_computation.4 | async-start | bytes 1048576 | tf_op jit(solution)/shard_map/all_to_all | solution.py:233
  251.2 12.2 %all-to-all-start.5 = ((bf16[4,1,64,1024]{3,2,1,0:T(8,128)(2,1)}), bf16[4,1,64,1024]{3,2,1,0:T(8,128)(2,1)S(1)}, u32[]{:S(2)}, u32[]{:S(2)}) async-start(bf16[4,1,64,1024]{3,2,1,0:T(8,128)(2,1)} %join.5), calls=%async_computation.5 | async-start | bytes 1048576 | tf_op jit(solution)/shard_map/all_to_all | solution.py:233
Sparse Core Ops, SparseCore 0:
  42.1 107.5 all-gather.1

commit v7 on v4

--- a/solution.py
+++ b/solution.py
@@ -268,10 +268,13 @@
         return (jax.nn.silu(total[..., : units // 2]) * total[..., units // 2 :]).astype(jnp.bfloat16)
 
     early = contexts(own_early, other_early, (0, 2), 0, (own_late,))
-    late = contexts(own_late, other_late, (2, 4), 2, (early[1],))
-    partial_value = joined_part(*swapped(*early), ())
-    arrived = [exchange(partial_value), exchange(joined_part(*swapped(*late), (partial_value,)))]
-    joined = [gated(one) for one in arrived]
+    late = contexts(own_late, other_late, (2, 3), 2, (early[1],))
+    last = contexts(own_late, other_late, (3, 4), 2, (late[1],))
+    early = exchange(joined_part(*swapped(*early), ()))
+    late = swapped(*late)
+    late = exchange(joined_part(*late, (last[1],)))
+    last = exchange(joined_part(*swapped(*last), (early,)))
+    joined = [gated(one) for one in (early, late, last)]
     return jnp.concatenate(joined)
 
 

time: 252 us -> 243 us (0.964)
  waiting for transfers between devices: 104 us -> 83 us
  Pallas kernels: 30.8 us -> 35.7 us
  local copies, waits for them, and re-layouts: 2.22 us -> 5.01 us
    ppermute x5 -> x6, waiting for transfers between devices: 50.1 us -> 41.3 us  [passed(): return lax.ppermute(array, ('dir', 'y', 'z'), pairs)]
    ppermute x1, waiting for transfers between devices: 6.59 us -> 0.01 us  [body(): lax.ppermute(join_weight.reshape(piece, -1), ('y', 'x'), [(y * 4 + x, x *...]
    all_to_all x3 -> x4, waiting for transfers between devices: 47.1 us -> 41.3 us  [exchange(): return lax.all_to_all(parts, 'x', split_axis=0, concat_axis=0, tiled=True)]
    ppermute x2 -> x3, starting transfers between devices: 9.09 us -> 3.54 us  [swapped(): return (mine, lax.ppermute(mine, 'dir', [(0, 1), (1, 0)]))]
    pallas_call x2 -> x3, Pallas kernels: 9.94 us -> 13.1 us  [join(): pl.pallas_call(join_kernel, grid_spec=pltpu.PrefetchScalarGridSpec(num_sc...]
    all_to_all x3 -> x4, starting transfers between devices: 12.2 us -> 15 us  [exchange(): return lax.all_to_all(parts, 'x', split_axis=0, concat_axis=0, tiled=True)]
    unnamed x11 -> x21, local copies, waits for them, and re-layouts: 2.22 us -> 5.01 us
    ppermute x5 -> x6, starting transfers between devices: 9.41 us -> 11.9 us  [passed(): return lax.ppermute(array, ('dir', 'y', 'z'), pairs)]
  transfers between devices with their start and end apart: 12 -> 15, of which waited for: 5 -> 6; matrix products, arithmetic and copies ran while one was open for 1% -> 2% of each run, Pallas kernels for 11% -> 12%
where the time goes in v7:
time: 243 us; the launch traced here: 241 us
  waiting for transfers between devices  83 us (34%)
  blocking collectives  62.1 us (26%)
  starting transfers between devices  36 us (15%)
  Pallas kernels  35.7 us (15%)
  between operations  13.7 us (6%)
  local copies, waits for them, and re-layouts  5.01 us (2%)
  other arithmetic  4.95 us (2%)
    all_to_all x2, blocking collectives, exchange(): return lax.all_to_all(parts, 'x', split_axis=0, concat_axis=0, tiled=True)  62.1 us
    ppermute x6, waiting for transfers between devices, passed(): return lax.ppermute(array, ('dir', 'y', 'z'), pairs)  41.3 us
    all_to_all x4, waiting for transfers between devices, exchange(): return lax.all_to_all(parts, 'x', split_axis=0, concat_axis=0, tiled=True)  41.3 us
    all_to_all x4, starting transfers between devices, exchange(): return lax.all_to_all(parts, 'x', split_axis=0, concat_axis=0, tiled=True)  15 us
    pallas_call x3, Pallas kernels, join(): pl.pallas_call(join_kernel, grid_spec=pltpu.PrefetchScalarGridSpec(num_sc...  13.1 us
    pallas_call x3, Pallas kernels, attend(): pl.pallas_call(attend_kernel, grid=(rows,), in_specs=[pl.BlockSpec(memory...  12.4 us
    ppermute x6, starting transfers between devices, passed(): return lax.ppermute(array, ('dir', 'y', 'z'), pairs)  11.9 us
    pallas_call x3, Pallas kernels, pack(): pl.pallas_call(lambda *refs: pack_kernel(count, *refs), grid=(high - low,...  9.01 us
  transfers between devices with their start and end apart: 15, of which 6 were waited for; matrix products, arithmetic and copies ran while one was open for 2% of the time, Pallas kernels for 12%

profile of v7, /device:TPU:8, one launch (start us, length us, event | category | flops | bytes accessed | tf_op | source)
XLA Modules:
  0.0 240.5 jit_solution(8855185696974898815)
XLA Ops:
  6.5 2.6 %pack.3 = bf16[4,2,2,64,1024]{4,3,2,1,0:T(8,128)(2,1)} custom-call(bf16[1,4,64,4096]{3,2,1,0:T(8,128)(2,1)} %refs_0_.5, bf16[1,4,64,4096]{3,2,1,0:T(8,128)(2,1)} %refs_1_.3), custom_call_target="tpu_custom_call" | custom-call | flops 1 | bytes 1 | tf_op jit(solution)/shard_map/pack/pallas_call | solution.py:83
  9.1 4.6 %all-to-all-start = ((bf16[4,2,2,64,1024]{4,3,2,1,0:T(8,128)(2,1)}), bf16[4,2,2,64,1024]{4,3,2,1,0:T(8,128)(2,1)}, u32[]{:S(2)}, u32[]{:S(2)}) async-start(bf16[4,2,2,64,1024]{4,3,2,1,0:T(8,128)(2,1)} %pack.3), calls=%async_computation | async-start | bytes 4194304 | tf_op jit(solution)/shard_map/all_to_all | solution.py:230
  13.7 0.0 all-gather.2.cloned.1.call-start
  13.8 0.0 copy-done.9
  13.8 5.4 %collective-permute-start = (bf16[64,1024]{1,0:T(8,128)(2,1)S(1)}, bf16[64,1024]{1,0:T(8,128)(2,1)S(1)}, u32[]{:S(2)}, u32[]{:S(2)}) collective-permute-start(bf16[64,1024]{1,0:T(8,128)(2,1)S(1)} %bitcast.16), channel_id=1, source_target_pairs={{0,0},{1,32},{2,64},{3,96},{32,1},{33,33},{34,65},{35,97},{64,2},{... | collective-permute-start | bytes 393224 | tf_op jit(solution)/shard_map/ppermute | solution.py:239
  19.2 21.1 %all-to-all-done.refs_1_.own_ref = bf16[4,2,2,64,1024]{4,3,2,1,0:T(8,128)(2,1)} async-done(((bf16[4,2,2,64,1024]{4,3,2,1,0:T(8,128)(2,1)}), bf16[4,2,2,64,1024]{4,3,2,1,0:T(8,128)(2,1)}, u32[]{:S(2)}, u32[]{:S(2)}) %all-to-all-start) | async-done | bytes 2097184 | tf_op jit(solution)/shard_map/all_to_all | solution.py:230
  40.4 3.8 %collective-permute-start.2 = (bf16[4,2,2,64,1024]{4,3,2,1,0:T(8,128)(2,1)}, bf16[4,2,2,64,1024]{4,3,2,1,0:T(8,128)(2,1)}, u32[]{:S(2)}, u32[]{:S(2)}) collective-permute-start(bf16[4,2,2,64,1024]{4,3,2,1,0:T(8,128)(2,1)} %all-to-all-done.refs_1_.own_ref), channel_id=1, source_target_pairs={{0,4},{4,8},{8,12},{12,16},{16,20},{20,24},{24,28},{28,32},{32,36}... | collective-permute-start | bytes 6291464 | tf_op jit(solution)/shard_map/ppermute | solution.py:237
  44.2 0.0 collective-permute-done.refs_2_
  44.2 0.0 copy-start.2
  44.2 0.6 copy-done.2
  44.9 0.0 all-gather.2.cloned.1.call-update
  44.9 0.0 copy-start.3
  44.9 0.9 copy-done.3
  45.8 3.8 %pack.4 = bf16[4,4,1,64,1024]{4,3,2,1,0:T(8,128)(2,1)} custom-call(bf16[1,4,64,4096]{3,2,1,0:T(8,128)(2,1)} %refs_0_.4, bf16[4,2,2,64,1024]{4,3,2,1,0:T(8,128)(2,1)} %all-to-all-done.refs_1_.own_ref, bf16[64,1024]{1,0:T(8,128)(2,1)S(1)} %copy-done.3), custom_call_target="tpu_custom_call" | custom-call | flops 1 | bytes 1 | tf_op jit(solution)/shard_map/pack/pallas_call | solution.py:83
  49.6 31.7 %all_to_all.30.refs_2_.q_ref = bf16[4,4,1,64,1024]{4,3,2,1,0:T(8,128)(2,1)S(1)} all-to-all(bf16[4,4,1,64,1024]{4,3,2,1,0:T(8,128)(2,1)} %pack.4), channel_id=1, replica_groups=mesh['dir'=2,'y'=4,'z'=8,'x'=4] {'x'}, dimensions={0} | all-to-all | bytes 4194304 | tf_op jit(solution)/shard_map/all_to_all | solution.py:230
  81.3 2.1 collective-permute-start.1
  83.4 0.0 collective-permute-done.2.refs_3_.other_ref
  83.4 2.6 %pack.5 = bf16[4,2,2,64,1024]{4,3,2,1,0:T(8,128)(2,1)} custom-call(bf16[1,4,64,4096]{3,2,1,0:T(8,128)(2,1)} %refs_0_.5, bf16[1,4,64,4096]{3,2,1,0:T(8,128)(2,1)} %refs_1_.3, bf16[4,4,1,64,1024]{4,3,2,1,0:T(8,128)(2,1)S(1)} %all_to_all.30.refs_2_.q_ref, bf16[4,2,2,64,1024]{4,3,2,1,0:T(8,128)(2,1)} %collective-permute-done.2.refs_3_.other_ref), custom_call_target="tpu_custom_call" | custom-call | flops 1 | bytes 1 | tf_op jit(solution)/shard_map/pack/pallas_call | solution.py:83
  86.0 0.0 copy-start.7
  86.0 30.5 %all_to_all.31.refs_0_.own_ref = bf16[4,2,2,64,1024]{4,3,2,1,0:T(8,128)(2,1)} all-to-all(bf16[4,2,2,64,1024]{4,3,2,1,0:T(8,128)(2,1)} %pack.5), channel_id=1, replica_groups=mesh['dir'=2,'y'=4,'z'=8,'x'=4] {'x'}, dimensions={0} | all-to-all | bytes 4194304 | tf_op jit(solution)/shard_map/all_to_all | solution.py:230
  116.4 3.2 %collective-permute-start.5 = (bf16[4,2,2,64,1024]{4,3,2,1,0:T(8,128)(2,1)}, bf16[4,2,2,64,1024]{4,3,2,1,0:T(8,128)(2,1)}, u32[]{:S(2)}, u32[]{:S(2)}) collective-permute-start(bf16[4,2,2,64,1024]{4,3,2,1,0:T(8,128)(2,1)} %all_to_all.31.refs_0_.own_ref), channel_id=1, source_target_pairs={{0,4},{4,8},{8,12},{12,16},{16,20},{20,24},{24,28},{28,32},{32,36}... | collective-permute-start | bytes 6291464 | tf_op jit(solution)/shard_map/ppermute | solution.py:237
  119.6 0.0 copy-done.7
  119.6 1.2 tables.1
  120.9 0.0 collective-permute-done.1.next_q_ref
  120.9 5.3 %attend.3 = (bf16[2,256,1024]{2,1,0:T(8,128)(2,1)S(1)}, bf16[2,256,1024]{2,1,0:T(8,128)(2,1)S(1)}) custom-call(s32[1]{0:T(128)} %bitcast.side_ref, s32[4,1,512]{2,1,0:T(1,128)S(1)} %get-tuple-element.14.first_ref, s32[4,1,256]{2,1,0:T(1,128)S(1)} %get-tuple-element.15.here_ref, s32[4,1,256]{2,1,0:T(1,128)S(1)} %get-tuple-element.16.ahead_ref, ...), custom_call_target="tpu_custom_call" | custom-call | flops 20000000000 | bytes 1 | tf_op jit(solution)/shard_map/attend/pallas_call | solution.py:162
  126.2 0.7 collective-permute-start.3
  126.9 41.3 %collective-permute-done.5.other_ref = bf16[4,2,2,64,1024]{4,3,2,1,0:T(8,128)(2,1)} collective-permute-done((bf16[4,2,2,64,1024]{4,3,2,1,0:T(8,128)(2,1)}, bf16[4,2,2,64,1024]{4,3,2,1,0:T(8,128)(2,1)}, u32[]{:S(2)}, u32[]{:S(2)}) %collective-permute-start.5) | collective-permute-done | bytes 2097184 | tf_op jit(solution)/shard_map/ppermute | solution.py:237
  168.3 3.7 %attend.4 = (bf16[1,256,1024]{2,1,0:T(8,128)(2,1)S(1)}, bf16[1,256,1024]{2,1,0:T(8,128)(2,1)S(1)}) custom-call(s32[1]{0:T(128)} %bitcast.side_ref, s32[4,1,512]{2,1,0:T(1,128)S(1)} %get-tuple-element.14.first_ref, s32[4,1,256]{2,1,0:T(1,128)S(1)} %get-tuple-element.15.here_ref, s32[4,1,256]{2,1,0:T(1,128)S(1)} %get-tuple-element.16.ahead_ref, ...), custom_call_target="tpu_custom_call" | custom-call | flops 10000000000 | bytes 1 | tf_op jit(solution)/shard_map/attend/pallas_call | solution.py:162
  171.9 0.7 collective-permute-start.6
  172.6 0.0 collective-permute-done.3
  172.6 0.4 add.29.mine_ref
  173.0 0.1 collective-permute-start.4
  173.1 0.0 collective-permute-done.6
  173.2 1.0 add.31.mine_ref
  174.2 0.5 collective-permute-start.7
  174.6 3.5 %attend.5 = (bf16[1,256,1024]{2,1,0:T(8,128)(2,1)S(1)}, bf16[1,256,1024]{2,1,0:T(8,128)(2,1)S(1)}) custom-call(s32[1]{0:T(128)} %bitcast.side_ref, s32[4,1,512]{2,1,0:T(1,128)S(1)} %get-tuple-element.14.first_ref, s32[4,1,256]{2,1,0:T(1,128)S(1)} %get-tuple-element.15.here_ref, s32[4,1,256]{2,1,0:T(1,128)S(1)} %get-tuple-element.16.ahead_ref, ...), custom_call_target="tpu_custom_call" | custom-call | flops 10000000000 | bytes 1 | tf_op jit(solution)/shard_map/attend/pallas_call | solution.py:162
  178.1 0.0 copy-start
  178.1 0.8 copy-done
  178.9 0.8 copy-done.4
  179.7 0.0 collective-permute-done.7.other_ref
  179.7 1.0 copy-done.5
  180.8 4.1 %join.4 = bf16[4,1,64,1024]{3,2,1,0:T(8,128)(2,1)} custom-call(s32[1]{0:T(128)} %bitcast.side_ref, bf16[1,256,1024]{2,1,0:T(8,128)(2,1)} %add.31.mine_ref, bf16[1,256,1024]{2,1,0:T(8,128)(2,1)} %collective-permute-done.7.other_ref, bf16[8,2,128,1024]{3,2,1,0:T(8,128)(2,1)} %bitcast.7, bf16[8,2,128,1024]{3,2,1,0:T(8,128)(2,1)} %bitcast.8, ...), custom_call_target="tpu_custom_call" | custom-call | flops 1 | bytes 1 | tf_op jit(solution)/shard_map/join/pallas_call | solution.py:201
  184.8 3.5 %all-to-all-start.4 = ((bf16[4,1,64,1024]{3,2,1,0:T(8,128)(2,1)}), bf16[4,1,64,1024]{3,2,1,0:T(8,128)(2,1)S(1)}, u32[]{:S(2)}, u32[]{:S(2)}) async-start(bf16[4,1,64,1024]{3,2,1,0:T(8,128)(2,1)} %join.4), calls=%async_computation.4 | async-start | bytes 1048576 | tf_op jit(solution)/shard_map/all_to_all | solution.py:230
  188.3 0.0 copy-done.6
  188.3 1.5 collective-permute-start.8
  189.8 0.0 collective-permute-done.4.other_ref
  189.8 5.3 %join.3 = bf16[4,2,64,1024]{3,2,1,0:T(8,128)(2,1)} custom-call(s32[1]{0:T(128)} %bitcast.side_ref, bf16[2,256,1024]{2,1,0:T(8,128)(2,1)S(1)} %add.29.mine_ref, bf16[2,256,1024]{2,1,0:T(8,128)(2,1)} %collective-permute-done.4.other_ref, bf16[8,2,128,1024]{3,2,1,0:T(8,128)(2,1)} %bitcast.9, bf16[8,2,128,1024]{3,2,1,0:T(8,128)(2,1)} %bitcast.10), custom_call_target="tpu_custom_call" | custom-call | flops 1 | bytes 1 | tf_op jit(solution)/shard_map/join/pallas_call | solution.py:201
  195.1 1.8 all-to-all-done.4
  196.8 0.8 copy-done.8
  197.6 3.5 %all-to-all-start.3 = ((bf16[4,2,64,1024]{3,2,1,0:T(8,128)(2,1)}), bf16[4,2,64,1024]{3,2,1,0:T(8,128)(2,1)S(1)}, u32[]{:S(2)}, u32[]{:S(2)}) async-start(bf16[4,2,64,1024]{3,2,1,0:T(8,128)(2,1)} %join.3), calls=%async_computation.3 | async-start | bytes 2097152 | tf_op jit(solution)/shard_map/all_to_all | solution.py:230
  201.2 0.0 collective-permute-done.8
  201.2 0.0 copy-done.1
  201.2 1.2 add.33.mine_ref
  202.4 3.0 %collective-permute-start.9 = (bf16[1,256,1024]{2,1,0:T(8,128)(2,1)S(1)}, bf16[1,256,1024]{2,1,0:T(8,128)(2,1)S(1)}, u32[]{:S(2)}, u32[]{:S(2)}) collective-permute-start(bf16[1,256,1024]{2,1,0:T(8,128)(2,1)S(1)} %add.33.mine_ref), channel_id=1, source_target_pairs={{0,128},{128,0},{1,129},{129,1},{2,130},{130,2},{3,131},{131,3},{4... | collective-permute-start | bytes 1572872 | tf_op jit(solution)/shard_map/ppermute | solution.py:261
  205.4 1.1 convert_reduce_fusion.2
  206.6 0.3 collective-permute-done.9.other_ref
  206.9 8.7 %all-to-all-done.3.refs_0_ = bf16[4,2,64,1024]{3,2,1,0:T(8,128)(2,1)S(1)} async-done(((bf16[4,2,64,1024]{3,2,1,0:T(8,128)(2,1)}), bf16[4,2,64,1024]{3,2,1,0:T(8,128)(2,1)S(1)}, u32[]{:S(2)}, u32[]{:S(2)}) %all-to-all-start.3) | async-done | bytes 1048608 | tf_op jit(solution)/shard_map/all_to_all | solution.py:230
  215.6 3.7 %join.5 = bf16[4,1,64,1024]{3,2,1,0:T(8,128)(2,1)} custom-call(s32[1]{0:T(128)} %bitcast.side_ref, bf16[1,256,1024]{2,1,0:T(8,128)(2,1)S(1)} %add.33.mine_ref, bf16[1,256,1024]{2,1,0:T(8,128)(2,1)S(1)} %collective-permute-done.9.other_ref, bf16[8,2,128,1024]{3,2,1,0:T(8,128)(2,1)} %bitcast.11, bf16[8,2,128,1024]{3,2,1,0:T(8,128)(2,1)} %bitcast.12, ...), custom_call_target="tpu_custom_call" | custom-call | flops 1 | bytes 1 | tf_op jit(solution)/shard_map/join/pallas_call | solution.py:201
  219.3 3.5 %all-to-all-start.5 = ((bf16[4,1,64,1024]{3,2,1,0:T(8,128)(2,1)}), bf16[4,1,64,1024]{3,2,1,0:T(8,128)(2,1)S(1)}, u32[]{:S(2)}, u32[]{:S(2)}) async-start(bf16[4,1,64,1024]{3,2,1,0:T(8,128)(2,1)} %join.5), calls=%async_computation.5 | async-start | bytes 1048576 | tf_op jit(solution)/shard_map/all_to_all | solution.py:230
  222.8 0.2 convert_reduce_fusion
  223.0 0.1 fusion
  223.1 9.7 %all-to-all-done.5 = bf16[4,1,64,1024]{3,2,1,0:T(8,128)(2,1)S(1)} async-done(((bf16[4,1,64,1024]{3,2,1,0:T(8,128)(2,1)}), bf16[4,1,64,1024]{3,2,1,0:T(8,128)(2,1)S(1)}, u32[]{:S(2)}, u32[]{:S(2)}) %all-to-all-start.5) | async-done | bytes 524320 | tf_op jit(solution)/shard_map/all_to_all | solution.py:230
  232.8 0.1 convert_reduce_fusion.1
  233.0 0.7 pad_maximum_fusion
  (10 shorter events, 0.1 us)
Async XLA Ops:
  9.1 4.6 %copy-start.9 = (bf16[64,2,512]{2,1,0:T(2,128)(2,1)S(1)}, bf16[64,2,512]{2,1,0:T(2,128)(2,1)}, u32[]{:S(2)}) copy-start(bf16[64,2,512]{2,1,0:T(2,128)(2,1)} %param.9) | copy-start | bytes 393220
  9.1 31.3 %all-to-all-start = ((bf16[4,2,2,64,1024]{4,3,2,1,0:T(8,128)(2,1)}), bf16[4,2,2,64,1024]{4,3,2,1,0:T(8,128)(2,1)}, u32[]{:S(2)}, u32[]{:S(2)}) async-start(bf16[4,2,2,64,1024]{4,3,2,1,0:T(8,128)(2,1)} %pack.3), calls=%async_computation | async-start | bytes 4194304 | tf_op jit(solution)/shard_map/all_to_all | solution.py:230
  13.7 166.0 %all-gather.2.cloned.1.call-start = ((), (), s32[]{:S(2)}) async-start(), calls=%async_computation.6 | async-start | bytes 4325376 | tf_op jit(solution)/shard_map/all_gather | solution.py:242
  13.8 30.4 %collective-permute-start = (bf16[64,1024]{1,0:T(8,128)(2,1)S(1)}, bf16[64,1024]{1,0:T(8,128)(2,1)S(1)}, u32[]{:S(2)}, u32[]{:S(2)}) collective-permute-start(bf16[64,1024]{1,0:T(8,128)(2,1)S(1)} %bitcast.16), channel_id=1, source_target_pairs={{0,0},{1,32},{2,64},{3,96},{32,1},{33,33},{34,65},{35,97},{64,2},{... | collective-permute-start | bytes 393224 | tf_op jit(solution)/shard_map/ppermute | solution.py:239
  40.4 43.0 %collective-permute-start.2 = (bf16[4,2,2,64,1024]{4,3,2,1,0:T(8,128)(2,1)}, bf16[4,2,2,64,1024]{4,3,2,1,0:T(8,128)(2,1)}, u32[]{:S(2)}, u32[]{:S(2)}) collective-permute-start(bf16[4,2,2,64,1024]{4,3,2,1,0:T(8,128)(2,1)} %all-to-all-done.refs_1_.own_ref), channel_id=1, source_target_pairs={{0,4},{4,8},{8,12},{12,16},{16,20},{20,24},{24,28},{28,32},{32,36}... | collective-permute-start | bytes 6291464 | tf_op jit(solution)/shard_map/ppermute | solution.py:237
  44.2 0.7 copy-start.2
  44.9 0.9 copy-start.3
  81.3 39.6 %collective-permute-start.1 = (bf16[4,4,1,64,1024]{4,3,2,1,0:T(8,128)(2,1)S(1)}, bf16[4,4,1,64,1024]{4,3,2,1,0:T(8,128)(2,1)}, u32[]{:S(2)}, u32[]{:S(2)}) collective-permute-start(bf16[4,4,1,64,1024]{4,3,2,1,0:T(8,128)(2,1)S(1)} %all_to_all.30.refs_2_.q_ref), channel_id=1, source_target_pairs={{132,128},{136,132},{140,136},{144,140},{148,144},{152,148},{156,1... | collective-permute-start | bytes 6291464 | tf_op jit(solution)/shard_map/ppermute | solution.py:237
  86.0 33.7 %copy-start.7 = (s32[4,512]{1,0:T(4,128)S(1)}, s32[4,512]{1,0:T(4,128)}, u32[]{:S(2)}) copy-start(s32[4,512]{1,0:T(4,128)} %lengths_ref.1) | copy-start | bytes 24580
  116.4 51.8 %collective-permute-start.5 = (bf16[4,2,2,64,1024]{4,3,2,1,0:T(8,128)(2,1)}, bf16[4,2,2,64,1024]{4,3,2,1,0:T(8,128)(2,1)}, u32[]{:S(2)}, u32[]{:S(2)}) collective-permute-start(bf16[4,2,2,64,1024]{4,3,2,1,0:T(8,128)(2,1)} %all_to_all.31.refs_0_.own_ref), channel_id=1, source_target_pairs={{0,4},{4,8},{8,12},{12,16},{16,20},{20,24},{24,28},{28,32},{32,36}... | collective-permute-start | bytes 6291464 | tf_op jit(solution)/shard_map/ppermute | solution.py:237
  126.2 46.4 %collective-permute-start.3 = (bf16[2,256,1024]{2,1,0:T(8,128)(2,1)S(1)}, bf16[2,256,1024]{2,1,0:T(8,128)(2,1)S(1)}, u32[]{:S(2)}, u32[]{:S(2)}) collective-permute-start(bf16[2,256,1024]{2,1,0:T(8,128)(2,1)S(1)} %get-tuple-element.18.refs_0_), channel_id=1, source_target_pairs={{128,132},{132,136},{136,140},{140,144},{144,148},{148,152},{152,1... | collective-permute-start | bytes 3145736 | tf_op jit(solution)/shard_map/ppermute | solution.py:237
  171.9 1.2 collective-permute-start.6
  173.0 16.8 %collective-permute-start.4 = (bf16[2,256,1024]{2,1,0:T(8,128)(2,1)S(1)}, bf16[2,256,1024]{2,1,0:T(8,128)(2,1)}, u32[]{:S(2)}, u32[]{:S(2)}) collective-permute-start(bf16[2,256,1024]{2,1,0:T(8,128)(2,1)S(1)} %add.29.mine_ref), channel_id=1, source_target_pairs={{0,128},{128,0},{1,129},{129,1},{2,130},{130,2},{3,131},{131,3},{4... | collective-permute-start | bytes 3145736 | tf_op jit(solution)/shard_map/ppermute | solution.py:261
  174.2 5.6 %collective-permute-start.7 = (bf16[1,256,1024]{2,1,0:T(8,128)(2,1)}, bf16[1,256,1024]{2,1,0:T(8,128)(2,1)}, u32[]{:S(2)}, u32[]{:S(2)}) collective-permute-start(bf16[1,256,1024]{2,1,0:T(8,128)(2,1)} %add.31.mine_ref), channel_id=1, source_target_pairs={{0,128},{128,0},{1,129},{129,1},{2,130},{130,2},{3,131},{131,3},{4... | collective-permute-start | bytes 1572872 | tf_op jit(solution)/shard_map/ppermute | solution.py:261
  178.1 0.8 copy-start
  178.9 0.8 copy-start.4
  179.7 1.0 copy-start.5
  180.8 7.5 %copy-start.6 = (bf16[1,256,1024]{2,1,0:T(8,128)(2,1)S(1)}, bf16[1,256,1024]{2,1,0:T(8,128)(2,1)}, u32[]{:S(2)}) copy-start(bf16[1,256,1024]{2,1,0:T(8,128)(2,1)} %copy-done.4) | copy-start | bytes 1572868
  184.8 12.0 %all-to-all-start.4 = ((bf16[4,1,64,1024]{3,2,1,0:T(8,128)(2,1)}), bf16[4,1,64,1024]{3,2,1,0:T(8,128)(2,1)S(1)}, u32[]{:S(2)}, u32[]{:S(2)}) async-start(bf16[4,1,64,1024]{3,2,1,0:T(8,128)(2,1)} %join.4), calls=%async_computation.4 | async-start | bytes 1048576 | tf_op jit(solution)/shard_map/all_to_all | solution.py:230
  188.3 12.8 %collective-permute-start.8 = (bf16[1,256,1024]{2,1,0:T(8,128)(2,1)S(1)}, bf16[1,256,1024]{2,1,0:T(8,128)(2,1)}, u32[]{:S(2)}, u32[]{:S(2)}) collective-permute-start(bf16[1,256,1024]{2,1,0:T(8,128)(2,1)S(1)} %copy-done.6), channel_id=1, source_target_pairs={{128,132},{132,136},{136,140},{140,144},{144,148},{148,152},{152,1... | collective-permute-start | bytes 1572872 | tf_op jit(solution)/shard_map/ppermute | solution.py:237
  195.1 6.1 %copy-start.1 = (bf16[1,256,1024]{2,1,0:T(8,128)(2,1)S(1)}, bf16[1,256,1024]{2,1,0:T(8,128)(2,1)}, u32[]{:S(2)}) copy-start(bf16[1,256,1024]{2,1,0:T(8,128)(2,1)} %copy-done) | copy-start | bytes 1572868
  196.8 0.8 copy-start.8
  197.6 18.0 %all-to-all-start.3 = ((bf16[4,2,64,1024]{3,2,1,0:T(8,128)(2,1)}), bf16[4,2,64,1024]{3,2,1,0:T(8,128)(2,1)S(1)}, u32[]{:S(2)}, u32[]{:S(2)}) async-start(bf16[4,2,64,1024]{3,2,1,0:T(8,128)(2,1)} %join.3), calls=%async_computation.3 | async-start | bytes 2097152 | tf_op jit(solution)/shard_map/all_to_all | solution.py:230
  202.4 4.5 %collective-permute-start.9 = (bf16[1,256,1024]{2,1,0:T(8,128)(2,1)S(1)}, bf16[1,256,1024]{2,1,0:T(8,128)(2,1)S(1)}, u32[]{:S(2)}, u32[]{:S(2)}) collective-permute-start(bf16[1,256,1024]{2,1,0:T(8,128)(2,1)S(1)} %add.33.mine_ref), channel_id=1, source_target_pairs={{0,128},{128,0},{1,129},{129,1},{2,130},{130,2},{3,131},{131,3},{4... | collective-permute-start | bytes 1572872 | tf_op jit(solution)/shard_map/ppermute | solution.py:261
  219.3 13.5 %all-to-all-start.5 = ((bf16[4,1,64,1024]{3,2,1,0:T(8,128)(2,1)}), bf16[4,1,64,1024]{3,2,1,0:T(8,128)(2,1)S(1)}, u32[]{:S(2)}, u32[]{:S(2)}) async-start(bf16[4,1,64,1024]{3,2,1,0:T(8,128)(2,1)} %join.5), calls=%async_computation.5 | async-start | bytes 1048576 | tf_op jit(solution)/shard_map/all_to_all | solution.py:230
Sparse Core Ops, SparseCore 0:
  45.0 93.8 all-gather.1
